TPU v7x, 512 devices: a whole 4x4x16 slice. The times are simulated.
512 devices in a mesh: fsdp: 64 (over z_hi, y, x), sp: 8 (over z_lo, core).
Axes of the slice: x: 4, y: 4, z: 16 (z_hi: 4, z_lo: 4; z = z_hi * 4 + z_lo), core: 2. Of those that a mesh axis runs over, the one named last changes fastest.
Arguments:
- latents: bfloat16 [64, 192, 3072], P('fsdp', 'sp'), may hold values from -6 to 6
- step_noise: bfloat16 [64, 192, 3072], P('fsdp', 'sp'), may hold values from -6 to 6
- base_qkv: bfloat16 [3, 3072, 3072], P(None, 'fsdp', 'sp'), may hold values from -1 to 1
- down_qkv: bfloat16 [3, 3072, 64], P(None, 'fsdp'), may hold values from -0.109375 to 0.109375
- up_query_key_value: bfloat16 [3, 64, 3072], P(None, None, 'sp'), may hold values from -0.625 to 0.625
- base_out: bfloat16 [3072, 3072], P('sp', 'fsdp'), may hold values from -0.109375 to 0.109375
- down_out: bfloat16 [3072, 64], P('sp'), may hold values from -0.109375 to 0.109375
- up_out: bfloat16 [64, 3072], P(None, 'fsdp'), may hold values from -0.625 to 0.625
- modulation: float32 [16, 3, 3072], replicated, may hold values from -3 to 3
- timestep: int32 [64], P('fsdp'), may hold values from 0 to 14
Outputs:
- velocity: bfloat16 [64, 192, 3072], P('fsdp', 'sp')
- next_latents: bfloat16 [64, 192, 3072], P('fsdp', 'sp')
Inputs may be any that keep to these rules, and one draw needn't show every extreme that they name: timestep[n] + 1 is also a step of the plan.
All inputs are finite; a program needn't handle non-finite values.
Results may differ from a plain program's by a relative error of at most 0.02.
Values may be sent and summed in bfloat16 or wider, within the bound.
No kernel may reach another device: no remote copies, remote signals or barrier semaphores. Data moves between devices by JAX's collectives and lax.ppermute only.
A program may use at most 64 MiB of HBM per device.

v0:
```python
import jax
import jax.numpy as jnp
from jax import lax
from jax.sharding import PartitionSpec as P

HEAD_DIM = 128
NSTEP = 16


EPSILON = 1e-06
SHIFT_FACTOR = 5.0
NOISE_LEVEL = 0.7


def plan_sigma(position):
    ramp = 1.0 - position / NSTEP
    return SHIFT_FACTOR * ramp / (1.0 + (SHIFT_FACTOR - 1.0) * ramp)


def per_device(
    latents,
    step_noise,
    base_qkv,
    down_qkv,
    up_query_key_value,
    base_out,
    down_out,
    up_out,
    modulation,
    timestep,
):
    step_index = timestep[0]
    mod_rows = lax.dynamic_index_in_dim(modulation, step_index, 0, keepdims=False)
    latent_f = latents[0].astype(jnp.float32)
    mean_square = jnp.mean(latent_f * latent_f, axis=-1, keepdims=True)
    normalized_rows = (
        latent_f * lax.rsqrt(mean_square + EPSILON) * (1.0 + mod_rows[1]) + mod_rows[0]
    ).astype(jnp.bfloat16)
    head_cols = base_qkv.shape[2]
    seq_len = normalized_rows.shape[0] * lax.axis_size("sp")
    every_token = lax.all_gather(normalized_rows, "sp", axis=0, tiled=True)
    lowrank = jnp.einsum(
        "prk,pkc->prc", down_qkv, up_query_key_value, preferred_element_type=jnp.float32
    )
    merged_qkv = (base_qkv.astype(jnp.float32) + lowrank).astype(jnp.bfloat16)
    projected = jnp.einsum(
        "lr,prc->plc",
        every_token,
        lax.all_gather(merged_qkv, "fsdp", axis=1, tiled=True),
        preferred_element_type=jnp.float32,
    ).astype(jnp.bfloat16)
    heads_here = head_cols // HEAD_DIM
    split_heads = projected.reshape(3, seq_len, heads_here, HEAD_DIM).transpose(2, 0, 1, 3)

    def one_head(triple):
        scores = jnp.dot(triple[0], triple[1].T, preferred_element_type=jnp.float32) * (
            1.0 / HEAD_DIM**0.5
        )
        attention_weights = jax.nn.softmax(scores, axis=-1).astype(jnp.bfloat16)
        return jnp.dot(attention_weights, triple[2], preferred_element_type=jnp.float32).astype(
            jnp.bfloat16
        )

    per_head = lax.map(one_head, split_heads)
    attention_result = per_head.transpose(1, 0, 2).reshape(seq_len, head_cols)
    merged_out = (
        base_out.astype(jnp.float32) + jnp.dot(down_out, up_out, preferred_element_type=jnp.float32)
    ).astype(jnp.bfloat16)
    full_out = lax.all_gather(merged_out, "fsdp", axis=1, tiled=True)
    block_out = lax.psum_scatter(
        jnp.dot(attention_result, full_out, preferred_element_type=jnp.float32).astype(
            jnp.bfloat16
        ),
        "sp",
        scatter_dimension=0,
        tiled=True,
    ).astype(jnp.float32)
    velocity = ((1.0 + mod_rows[2]) * block_out).astype(jnp.bfloat16)
    position = step_index.astype(jnp.float32)
    step_size = plan_sigma(position + 1.0) - plan_sigma(position)
    next_rows = (
        latent_f
        + step_size * velocity.astype(jnp.float32)
        + NOISE_LEVEL * jnp.sqrt(-step_size) * step_noise[0].astype(jnp.float32)
    )
    return (velocity[None], next_rows.astype(jnp.bfloat16)[None])


def solution(mesh):
    in_specs = (
        P("fsdp", "sp", None),
        P("fsdp", "sp", None),
        P(None, "fsdp", "sp"),
        P(None, "fsdp", None),
        P(None, None, "sp"),
        P("sp", "fsdp"),
        P("sp", None),
        P(None, "fsdp"),
        P(),
        P("fsdp"),
    )
    out_specs = (P("fsdp", "sp", None), P("fsdp", "sp", None))
    return jax.shard_map(
        per_device, mesh=mesh, in_specs=in_specs, out_specs=out_specs, check_vma=False
    )
```

profile of v0, /device:TPU:2, one launch (start us, length us, event | category | flops | bytes accessed | tf_op | source)
XLA Modules:
  0.0 406.6 jit_solution(8936487235050677608)
XLA Ops:
  7.2 0.0 copy-start
  7.2 0.0 all-gather.6.cloned.1.call-start
  7.9 1.0 fusion.11
  9.0 1.0 dynamic-slice_add_fusion.1
  10.0 1.7 fusion.14
  11.7 0.0 all-gather.6.cloned.1.call-update
  11.7 0.0 all-gather.4.cloned.1.call-start
  11.8 0.0 copy-done
  11.8 1.7 fusion.9
  13.5 0.0 all-gather.4.cloned.1.call-update
  13.5 0.0 all-gather.8.cloned.1.call-start
  13.6 1.6 fusion.10
  15.1 0.0 all-gather.8.cloned.1.call-update
  15.2 0.0 reduce-scatter.2.cloned.1.call-start
  15.2 43.8 %all-gather.6.cloned.1.call-done = bf16[192,3072]{1,0:T(8,128)(2,1)} async-done(((bf16[24,3072]{1,0:T(8,128)(2,1)}), bf16[192,3072]{1,0:T(8,128)(2,1)}) %all-gather.6.cloned.1.call-update) | async-done | bytes 1179664 | tf_op jit(solution)/shard_map/all_gather | solution.py:41
  59.0 179.3 %all-gather.4.cloned.1.call-done = bf16[3,3072,384]{2,1,0:T(8,128)(2,1)} async-done(((bf16[3,48,384]{2,1,0:T(8,128)(2,1)}), bf16[3,3072,384]{2,1,0:T(8,128)(2,1)}) %all-gather.4.cloned.1.call-update) | async-done | bytes 7077904 | tf_op jit(solution)/shard_map/all_gather | solution.py:49
  238.3 5.1 %fusion.7 = bf16[3,192,384]{2,1,0:T(8,128)(2,1)S(1)} fusion(bf16[3,3072,384]{2,1,0:T(8,128)(2,1)} %all-gather.4.cloned.1.call-done, bf16[192,3072]{1,0:T(8,128)(2,1)} %all-gather.6.cloned.1.call-done), kind=kOutput, calls=%fused_computation.16 | convolution fusion | flops 1359175680 | bytes 8699904 | tf_op jit(solution)/shard_map/lr,prc->plc/dot_general | solution.py:46
  243.4 0.1 reshape.51
  243.5 0.1 copy.13
  243.6 1.6 while.10
  243.6 0.2 fusion.32
  243.9 0.1 fusion.33
  243.9 0.2 fusion.34
  244.2 0.2 fusion.32
  244.4 0.1 fusion.33
  244.5 0.2 fusion.34
  244.7 0.2 fusion.32
  244.9 0.1 fusion.33
  245.0 0.2 fusion.34
  245.3 110.8 %all-gather.8.cloned.1.call-done = bf16[384,3072]{0,1:T(8,128)(2,1)} async-done(((bf16[384,48]{0,1:T(8,128)(2,1)}), bf16[384,3072]{0,1:T(8,128)(2,1)}) %all-gather.8.cloned.1.call-update) | async-done | bytes 2359312 | tf_op jit(solution)/shard_map/all_gather | solution.py:69
  356.0 0.0 copy-start.1
  356.0 0.0 copy-start.2
  356.0 3.7 convolution_convert_fusion.1
  359.7 0.0 reduce-scatter.2.cloned.1.call-update
  359.9 38.4 %reduce-scatter.2.cloned.1.call-done = bf16[24,3072]{1,0:T(8,128)(2,1)} async-done(((bf16[192,3072]{1,0:T(8,128)(2,1)}), bf16[24,3072]{1,0:T(8,128)(2,1)}) %reduce-scatter.2.cloned.1.call-update) | async-done | bytes 147472 | tf_op jit(solution)/shard_map/reduce_scatter | solution.py:70
  398.3 0.0 copy-done.1
  398.3 0.0 copy-done.2
  398.3 1.7 fusion.17
  (2 shorter events, 0.0 us)
Async XLA Ops:
  7.2 4.6 %copy-start = (bf16[3,64,384]{2,1,0:T(8,128)(2,1)S(1)}, bf16[3,64,384]{2,1,0:T(8,128)(2,1)}, u32[]{:S(2)}) copy-start(bf16[3,64,384]{2,1,0:T(8,128)(2,1)} %param.16) | copy-start | bytes 442372
  7.2 51.9 %all-gather.6.cloned.1.call-start = ((), (), s32[]{:S(2)}) async-start(), calls=%async_computation.2 | async-start | bytes 1327104 | tf_op jit(solution)/shard_map/all_gather | solution.py:41
  11.7 226.6 %all-gather.4.cloned.1.call-start = ((), (), s32[]{:S(2)}) async-start(), calls=%async_computation.1 | async-start | bytes 7188480 | tf_op jit(solution)/shard_map/all_gather | solution.py:49
  13.5 342.5 %all-gather.8.cloned.1.call-start = ((), (), s32[]{:S(2)}) async-start(), calls=%async_computation.3 | async-start | bytes 2396160 | tf_op jit(solution)/shard_map/all_gather | solution.py:69
  15.2 383.1 %reduce-scatter.2.cloned.1.call-start = ((), (), s32[]{:S(2)}) async-start(), calls=%async_computation.4 | async-start | bytes 1327104 | tf_op jit(solution)/shard_map/reduce_scatter | solution.py:70
  356.0 42.3 %copy-start.1 = (bf16[1,24,3072]{2,1,0:T(8,128)(2,1)S(1)}, bf16[1,24,3072]{2,1,0:T(8,128)(2,1)}, u32[]{:S(2)}) copy-start(bf16[1,24,3072]{2,1,0:T(8,128)(2,1)} %param.12) | copy-start | bytes 442372
  356.0 42.3 %copy-start.2 = (bf16[1,24,3072]{2,1,0:T(8,128)(2,1)S(1)}, bf16[1,24,3072]{2,1,0:T(8,128)(2,1)}, u32[]{:S(2)}) copy-start(bf16[1,24,3072]{2,1,0:T(8,128)(2,1)} %param.13) | copy-start | bytes 442372
Sparse Core Ops, SparseCore 0:
  11.8 47.1 all-gather.5
  63.8 174.4 all-gather.3
  242.4 113.5 all-gather.7
  359.9 38.3 reduce-scatter.1
where the time goes:
time: 407 us
  waiting for transfers between devices  372 us (91%)
  between operations  14.6 us (4%)
  matrix products  13.5 us (3%)
  other arithmetic  5.68 us (1%)
    all_gather x1, waiting for transfers between devices, per_device(): lax.all_gather(merged_qkv, 'fsdp', axis=1, tiled=True)  179 us
    all_gather x1, waiting for transfers between devices, per_device(): full_out = lax.all_gather(merged_out, 'fsdp', axis=1, tiled=True)  111 us
    all_gather x1, waiting for transfers between devices, per_device(): every_token = lax.all_gather(normalized_rows, 'sp', axis=0, tiled=True)  43.8 us
    reduce_scatter x1, waiting for transfers between devices, per_device(): lax.psum_scatter(jnp.dot(attention_result, full_out, preferred_element_ty...  38.4 us
  transfers between devices with their start and end apart: 4, of which 4 were waited for; matrix products, arithmetic and copies ran while one was open for 2% of the time, Pallas kernels for 0%

commit v1 on v0

v1 whole, which is shorter than its diff:
```python
import jax
import jax.numpy as jnp
from jax import lax
from jax.sharding import PartitionSpec as P

HEAD_DIM = 128
NSTEP = 16
QUAD = 4


EPSILON = 1e-06
SHIFT_FACTOR = 5.0
NOISE_LEVEL = 0.7


def plan_sigma(position):
    ramp = 1.0 - position / NSTEP
    return SHIFT_FACTOR * ramp / (1.0 + (SHIFT_FACTOR - 1.0) * ramp)


def fsdp_index(z, y, x):
    return ((z % QUAD) * QUAD + y % QUAD) * QUAD + x % QUAD


Y_GROUPS = [[fsdp_index(z, y, x) for y in range(QUAD)] for z in range(QUAD) for x in range(QUAD)]


def shift_fsdp(value, dz=0, dx=0):
    pairs = [
        (fsdp_index(z, y, x), fsdp_index(z + dz, y, x + dx))
        for z in range(QUAD)
        for y in range(QUAD)
        for x in range(QUAD)
    ]
    return lax.ppermute(value, "fsdp", pairs)


def shift_run(value, dz):
    pairs = [
        (z * 2 + core, ((z + dz) % QUAD) * 2 + core) for z in range(QUAD) for core in range(2)
    ]
    return lax.ppermute(value, "sp", pairs)


def other_core(value):
    return lax.ppermute(value, "sp", [(i, i ^ 1) for i in range(2 * QUAD)])


def exchange_y(value):
    return lax.all_to_all(value, "fsdp", 0, 0, axis_index_groups=Y_GROUPS, tiled=True)


def per_device(
    latents,
    step_noise,
    base_qkv,
    down_qkv,
    up_query_key_value,
    base_out,
    down_out,
    up_out,
    modulation,
    timestep,
):
    z_hi = lax.axis_index("fsdp") // (QUAD * QUAD)
    x = lax.axis_index("fsdp") % QUAD
    rows, width = latents.shape[1:]
    part = base_qkv.shape[1]
    head_cols = base_qkv.shape[2]
    heads_here = head_cols // HEAD_DIM
    seq_len = rows * 2 * QUAD
    slab = width // QUAD

    lowrank = jnp.einsum(
        "prk,pkc->prc", down_qkv, up_query_key_value, preferred_element_type=jnp.float32
    )
    merged_qkv = (base_qkv.astype(jnp.float32) + lowrank).astype(jnp.bfloat16)
    lowrank_out = jnp.einsum("rk,kc->cr", down_out, up_out, preferred_element_type=jnp.float32)
    merged_out = (base_out.T.astype(jnp.float32) + lowrank_out).astype(jnp.bfloat16)
    merged = jnp.concatenate([merged_qkv, merged_out[None]], axis=0)

    def place(buffer, block, axis, index):
        start = [jnp.int32(0)] * buffer.ndim
        start[axis] = index.astype(jnp.int32)
        return lax.dynamic_update_slice(buffer, jnp.expand_dims(block, axis), start)

    held = jnp.zeros((4, QUAD, part, head_cols), jnp.bfloat16)
    for k in range(QUAD):
        block = merged if k == 0 else shift_fsdp(merged, dz=k)
        held = place(held, block, 1, (z_hi - k) % QUAD)
    weights = jnp.zeros((4, QUAD, QUAD, part, head_cols), jnp.bfloat16)
    for k in range(QUAD):
        block = held if k == 0 else shift_fsdp(held, dx=k)
        weights = place(weights, block, 2, (x - k) % QUAD)
    weights = weights.reshape(4, slab, head_cols)

    step_index = timestep[0]
    mod_rows = lax.dynamic_index_in_dim(modulation, step_index, 0, keepdims=False)
    latent_f = latents[0].astype(jnp.float32)
    mean_square = jnp.mean(latent_f * latent_f, axis=-1, keepdims=True)
    normalized_rows = (
        latent_f * lax.rsqrt(mean_square + EPSILON) * (1.0 + mod_rows[1]) + mod_rows[0]
    ).astype(jnp.bfloat16)
    slices = normalized_rows.reshape(rows, QUAD, QUAD, slab // QUAD).transpose(2, 0, 1, 3)
    mine = exchange_y(slices.reshape(QUAD, rows, slab))
    run = jnp.stack([mine] + [shift_run(mine, k) for k in range(1, QUAD)], axis=1)
    both = jnp.stack([run, other_core(run)], axis=2)
    tokens = both.reshape(QUAD * seq_len, slab)

    partial = jnp.stack(
        [
            jnp.dot(tokens, weights[p], preferred_element_type=jnp.float32)
            .astype(jnp.bfloat16)
            .reshape(QUAD, seq_len, head_cols)
            for p in range(3)
        ],
        axis=1,
    )
    projected = jnp.sum(exchange_y(partial).astype(jnp.float32), axis=0).astype(jnp.bfloat16)
    heads = projected.reshape(3, seq_len, heads_here, HEAD_DIM).transpose(0, 2, 1, 3)
    scores = jnp.einsum("hqe,hke->hqk", heads[0], heads[1], preferred_element_type=jnp.float32)
    attention_weights = jax.nn.softmax(scores * (1.0 / HEAD_DIM**0.5), axis=-1).astype(jnp.bfloat16)
    attended = jnp.einsum(
        "hqk,hke->qhe", attention_weights, heads[2], preferred_element_type=jnp.float32
    ).astype(jnp.bfloat16)
    attended = attended.reshape(seq_len, head_cols)

    gathered = lax.all_gather(attended, "fsdp", axis_index_groups=Y_GROUPS, axis=0, tiled=True)
    out_partial = lax.dot_general(
        gathered, weights[3], (((1,), (1,)), ((), ())), preferred_element_type=jnp.float32
    ).reshape(QUAD, QUAD, 2, rows, slab)
    pair = out_partial[:, :, 0] + other_core(out_partial[:, :, 1].astype(jnp.bfloat16)).astype(
        jnp.float32
    )
    total = pair[:, 0]
    for k in range(1, QUAD):
        total = total + shift_run(pair[:, k].astype(jnp.bfloat16), -k).astype(jnp.float32)
    columns = exchange_y(total.astype(jnp.bfloat16))
    block_out = (
        columns.reshape(QUAD, rows, QUAD, slab // QUAD)
        .transpose(1, 2, 0, 3)
        .reshape(rows, width)
        .astype(jnp.float32)
    )

    velocity = ((1.0 + mod_rows[2]) * block_out).astype(jnp.bfloat16)
    position = step_index.astype(jnp.float32)
    step_size = plan_sigma(position + 1.0) - plan_sigma(position)
    next_rows = (
        latent_f
        + step_size * velocity.astype(jnp.float32)
        + NOISE_LEVEL * jnp.sqrt(-step_size) * step_noise[0].astype(jnp.float32)
    )
    return (velocity[None], next_rows.astype(jnp.bfloat16)[None])


def solution(mesh):
    in_specs = (
        P("fsdp", "sp", None),
        P("fsdp", "sp", None),
        P(None, "fsdp", "sp"),
        P(None, "fsdp", None),
        P(None, None, "sp"),
        P("sp", "fsdp"),
        P("sp", None),
        P(None, "fsdp"),
        P(),
        P("fsdp"),
    )
    out_specs = (P("fsdp", "sp", None), P("fsdp", "sp", None))
    return jax.shard_map(
        per_device, mesh=mesh, in_specs=in_specs, out_specs=out_specs, check_vma=False
    )
```

time: 407 us -> 183 us (0.45)
  waiting for transfers between devices: 372 us -> 56.9 us
  starting transfers between devices: 0.16 us -> 67 us
  blocking collectives: 0 us -> 39.4 us
  between operations: 14.6 us -> 1.98 us
  matrix products: 13.5 us -> 6.18 us
  local copies, waits for them, and re-layouts: 0.21 us -> 5.5 us
    all_gather x3 -> x0, waiting for transfers between devices: 334 us -> none  [the longest x1 179 us: per_device(): lax.all_gather(merged_qkv, 'fsdp', axis=1, tiled=True)]
    ppermute x0 -> x14, starting transfers between devices: none -> 59.2 us  [the longest x6 36 us: shift_fsdp(): return lax.ppermute(value, 'fsdp', pairs)]
    ppermute x0 -> x14, waiting for transfers between devices: none -> 45 us  [the longest x6 34.3 us: shift_fsdp(): return lax.ppermute(value, 'fsdp', pairs)]
    reduce_scatter x1 -> x0, waiting for transfers between devices: 38.4 us -> none  [per_device(): lax.psum_scatter(jnp.dot(attention_result, full_out, preferred_element_ty...]
    all_to_all x0 -> x1, blocking collectives: none -> 25.7 us  [exchange_y(): lax.all_to_all(value, 'fsdp', 0, 0, axis_index_groups=Y_GROUPS, tiled=True)]
    all_gather x0 -> x1, blocking collectives: none -> 13.7 us  [per_device(): lax.all_gather(attended, 'fsdp', axis_index_groups=Y_GROUPS, axis=0, tile...]
    all_to_all x0 -> x2, waiting for transfers between devices: none -> 12 us  [exchange_y(): lax.all_to_all(value, 'fsdp', 0, 0, axis_index_groups=Y_GROUPS, tiled=True)]
    all_to_all x0 -> x2, starting transfers between devices: none -> 7.74 us  [exchange_y(): lax.all_to_all(value, 'fsdp', 0, 0, axis_index_groups=Y_GROUPS, tiled=True)]
  transfers between devices with their start and end apart: 4 -> 16, of which waited for: 4 -> 9; matrix products, arithmetic and copies ran while one was open for 2% -> 3% of each run, Pallas kernels for 0% -> 0%
where the time goes in v1:
time: 183 us; the launch traced here: 182 us
  starting transfers between devices  67 us (37%)
  waiting for transfers between devices  56.9 us (31%)
  blocking collectives  39.4 us (22%)
  matrix products  6.18 us (3%)
  local copies, waits for them, and re-layouts  5.5 us (3%)
  other arithmetic  4.96 us (3%)
  between operations  1.98 us (1%)
    ppermute x6, starting transfers between devices, shift_fsdp(): return lax.ppermute(value, 'fsdp', pairs)  36 us
    ppermute x6, waiting for transfers between devices, shift_fsdp(): return lax.ppermute(value, 'fsdp', pairs)  34.3 us
    all_to_all x1, blocking collectives, exchange_y(): lax.all_to_all(value, 'fsdp', 0, 0, axis_index_groups=Y_GROUPS, tiled=True)  25.7 us
    ppermute x6, starting transfers between devices, shift_run(): return lax.ppermute(value, 'sp', pairs)  19.4 us
    all_gather x1, blocking collectives, per_device(): lax.all_gather(attended, 'fsdp', axis_index_groups=Y_GROUPS, axis=0, tile...  13.7 us
    all_to_all x2, waiting for transfers between devices, exchange_y(): lax.all_to_all(value, 'fsdp', 0, 0, axis_index_groups=Y_GROUPS, tiled=True)  12 us
    ppermute x6, waiting for transfers between devices, shift_run(): return lax.ppermute(value, 'sp', pairs)  8.68 us
    all_to_all x2, starting transfers between devices, exchange_y(): lax.all_to_all(value, 'fsdp', 0, 0, axis_index_groups=Y_GROUPS, tiled=True)  7.74 us
  transfers between devices with their start and end apart: 16, of which 9 were waited for; matrix products, arithmetic and copies ran while one was open for 3% of the time, Pallas kernels for 0%

profile of v1, /device:TPU:2, one launch (start us, length us, event | category | flops | bytes accessed | tf_op | source)
XLA Modules:
  0.0 182.0 jit_solution(6932833686519657319)
XLA Ops:
  0.6 0.9 copy-done
  1.5 1.1 fusion.4
  2.6 0.9 fusion.7
  3.6 9.1 %collective-permute-start.4 = (bf16[4,48,384]{2,1,0:T(8,128)(2,1)S(1)}, bf16[4,48,384]{2,1,0:T(8,128)(2,1)S(1)}, u32[]{:S(2)}, u32[]{:S(2)}) collective-permute-start(bf16[4,48,384]{2,1,0:T(8,128)(2,1)S(1)} %pad_maximum_fusion.3), channel_id=1, source_target_pairs={{0,128},{8,136},{16,144},{24,152},{32,160},{40,168},{48,176},{56,1... | collective-permute-start | bytes 442376 | tf_op jit(solution)/shard_map/ppermute | solution.py:35
  12.7 10.9 %collective-permute-start.5 = (bf16[4,48,384]{2,1,0:T(8,128)(2,1)S(1)}, bf16[4,48,384]{2,1,0:T(8,128)(2,1)S(1)}, u32[]{:S(2)}, u32[]{:S(2)}) collective-permute-start(bf16[4,48,384]{2,1,0:T(8,128)(2,1)S(1)} %pad_maximum_fusion.3), channel_id=1, source_target_pairs={{0,256},{8,264},{16,272},{24,280},{32,288},{40,296},{48,304},{56,3... | collective-permute-start | bytes 442376 | tf_op jit(solution)/shard_map/ppermute | solution.py:35
  23.6 5.5 %collective-permute-start.6 = (bf16[4,48,384]{2,1,0:T(8,128)(2,1)S(1)}, bf16[4,48,384]{2,1,0:T(8,128)(2,1)S(1)}, u32[]{:S(2)}, u32[]{:S(2)}) collective-permute-start(bf16[4,48,384]{2,1,0:T(8,128)(2,1)S(1)} %pad_maximum_fusion.3), channel_id=1, source_target_pairs={{0,384},{8,392},{16,400},{24,408},{32,416},{40,424},{48,432},{56,4... | collective-permute-start | bytes 442376 | tf_op jit(solution)/shard_map/ppermute | solution.py:35
  29.8 1.0 multiply_reduce_fusion
  30.8 1.1 fusion.17
  32.0 1.2 reshape.160
  33.6 10.7 %collective-permute-done.5 = bf16[4,48,384]{2,1,0:T(8,128)(2,1)S(1)} collective-permute-done((bf16[4,48,384]{2,1,0:T(8,128)(2,1)S(1)}, bf16[4,48,384]{2,1,0:T(8,128)(2,1)S(1)}, u32[]{:S(2)}, u32[]{:S(2)}) %collective-permute-start.5) | collective-permute-done | bytes 147488 | tf_op jit(solution)/shard_map/ppermute | solution.py:35
  44.3 4.7 %collective-permute-done.6 = bf16[4,48,384]{2,1,0:T(8,128)(2,1)S(1)} collective-permute-done((bf16[4,48,384]{2,1,0:T(8,128)(2,1)S(1)}, bf16[4,48,384]{2,1,0:T(8,128)(2,1)S(1)}, u32[]{:S(2)}, u32[]{:S(2)}) %collective-permute-start.6) | collective-permute-done | bytes 147488 | tf_op jit(solution)/shard_map/ppermute | solution.py:35
  49.1 3.5 %collective-permute-start.7 = (bf16[4,4,48,384]{3,2,1,0:T(8,128)(2,1)S(1)}, bf16[4,4,48,384]{3,2,1,0:T(8,128)(2,1)S(1)}, u32[]{:S(2)}, u32[]{:S(2)}) collective-permute-start(bf16[4,4,48,384]{3,2,1,0:T(8,128)(2,1)S(1)} %bitcast_dynamic-update-slice_fusion.4), channel_id=1, source_target_pairs={{0,8},{8,16},{16,24},{24,0},{32,40},{40,48},{48,56},{56,32},{64,72... | collective-permute-start | bytes 1769480 | tf_op jit(solution)/shard_map/ppermute | solution.py:35
  52.7 0.9 reshape.156
  53.6 4.4 %all-to-all-start = ((bf16[4,24,768]{2,1,0:T(8,128)(2,1)}), bf16[4,24,768]{2,1,0:T(8,128)(2,1)S(1)}, u32[]{:S(2)}, u32[]{:S(2)}) async-start(bf16[4,24,768]{2,1,0:T(8,128)(2,1)} %reshape.156), calls=%async_computation | async-start | bytes 294912 | tf_op jit(solution)/shard_map/all_to_all | solution.py:50
  58.0 6.1 %all-to-all-done = bf16[4,24,768]{2,1,0:T(8,128)(2,1)S(1)} async-done(((bf16[4,24,768]{2,1,0:T(8,128)(2,1)}), bf16[4,24,768]{2,1,0:T(8,128)(2,1)S(1)}, u32[]{:S(2)}, u32[]{:S(2)}) %all-to-all-start) | async-done | bytes 147488 | tf_op jit(solution)/shard_map/all_to_all | solution.py:50
  64.0 1.9 %collective-permute-start = (bf16[4,24,768]{2,1,0:T(8,128)(2,1)S(1)}, bf16[4,24,768]{2,1,0:T(8,128)(2,1)S(1)}, u32[]{:S(2)}, u32[]{:S(2)}) collective-permute-start(bf16[4,24,768]{2,1,0:T(8,128)(2,1)S(1)} %all-to-all-done), channel_id=1, source_target_pairs={{0,2},{1,3},{2,4},{3,5},{4,6},{5,7},{6,0},{7,1},{8,10},{9,11},{10,... | collective-permute-start | bytes 442376 | tf_op jit(solution)/shard_map/ppermute | solution.py:42
  66.0 4.2 %collective-permute-start.1 = (bf16[4,24,768]{2,1,0:T(8,128)(2,1)S(1)}, bf16[4,24,768]{2,1,0:T(8,128)(2,1)S(1)}, u32[]{:S(2)}, u32[]{:S(2)}) collective-permute-start(bf16[4,24,768]{2,1,0:T(8,128)(2,1)S(1)} %all-to-all-done), channel_id=1, source_target_pairs={{0,4},{1,5},{2,6},{3,7},{4,0},{5,1},{6,2},{7,3},{8,12},{9,13},{10,... | collective-permute-start | bytes 442376 | tf_op jit(solution)/shard_map/ppermute | solution.py:42
  70.2 4.8 %collective-permute-start.2 = (bf16[4,24,768]{2,1,0:T(8,128)(2,1)S(1)}, bf16[4,24,768]{2,1,0:T(8,128)(2,1)S(1)}, u32[]{:S(2)}, u32[]{:S(2)}) collective-permute-start(bf16[4,24,768]{2,1,0:T(8,128)(2,1)S(1)} %all-to-all-done), channel_id=1, source_target_pairs={{0,6},{1,7},{2,0},{3,1},{4,2},{5,3},{6,4},{7,5},{8,14},{9,15},{10,... | collective-permute-start | bytes 442376 | tf_op jit(solution)/shard_map/ppermute | solution.py:42
  75.0 3.0 %collective-permute-start.8 = (bf16[4,4,48,384]{3,2,1,0:T(8,128)(2,1)S(1)}, bf16[4,4,48,384]{3,2,1,0:T(8,128)(2,1)S(1)}, u32[]{:S(2)}, u32[]{:S(2)}) collective-permute-start(bf16[4,4,48,384]{3,2,1,0:T(8,128)(2,1)S(1)} %bitcast_dynamic-update-slice_fusion.4), channel_id=1, source_target_pairs={{0,16},{8,24},{16,0},{24,8},{32,48},{40,56},{48,32},{56,40},{64,80... | collective-permute-start | bytes 1769480 | tf_op jit(solution)/shard_map/ppermute | solution.py:35
  78.1 0.3 broadcast_in_dim.40
  78.5 4.1 %collective-permute-start.9 = (bf16[4,4,48,384]{3,2,1,0:T(8,128)(2,1)S(1)}, bf16[4,4,48,384]{3,2,1,0:T(8,128)(2,1)S(1)}, u32[]{:S(2)}, u32[]{:S(2)}) collective-permute-start(bf16[4,4,48,384]{3,2,1,0:T(8,128)(2,1)S(1)} %bitcast_dynamic-update-slice_fusion.4), channel_id=1, source_target_pairs={{0,24},{8,0},{16,8},{24,16},{32,56},{40,32},{48,40},{56,48},{64,88... | collective-permute-start | bytes 1769480 | tf_op jit(solution)/shard_map/ppermute | solution.py:35
  82.7 1.9 %collective-permute-start.3 = (bf16[4,4,24,768]{3,2,0,1:T(8,128)(2,1)S(1)}, bf16[4,4,24,768]{3,2,0,1:T(8,128)(2,1)S(1)}, u32[]{:S(2)}, u32[]{:S(2)}) collective-permute-start(bf16[4,4,24,768]{3,2,0,1:T(8,128)(2,1)S(1)} %get-tuple-element.17), channel_id=1, source_target_pairs={{0,1},{1,0},{2,3},{3,2},{4,5},{5,4},{6,7},{7,6},{8,9},{9,8},{10,11... | collective-permute-start | bytes 1769480 | tf_op jit(solution)/shard_map/ppermute | solution.py:46
  84.8 9.9 %collective-permute-done.8 = bf16[4,4,48,384]{3,2,1,0:T(8,128)(2,1)S(1)} collective-permute-done((bf16[4,4,48,384]{3,2,1,0:T(8,128)(2,1)S(1)}, bf16[4,4,48,384]{3,2,1,0:T(8,128)(2,1)S(1)}, u32[]{:S(2)}, u32[]{:S(2)}) %collective-permute-start.8) | collective-permute-done | bytes 589856 | tf_op jit(solution)/shard_map/ppermute | solution.py:35
  94.8 8.9 %collective-permute-done.9 = bf16[4,4,48,384]{3,2,1,0:T(8,128)(2,1)S(1)} collective-permute-done((bf16[4,4,48,384]{3,2,1,0:T(8,128)(2,1)S(1)}, bf16[4,4,48,384]{3,2,1,0:T(8,128)(2,1)S(1)}, u32[]{:S(2)}, u32[]{:S(2)}) %collective-permute-start.9) | collective-permute-done | bytes 589856 | tf_op jit(solution)/shard_map/ppermute | solution.py:35
  103.9 0.2 fusion.26
  104.4 0.8 convolution_convert_fusion.2
  105.2 0.8 convolution_convert_fusion.1
  106.0 0.8 convolution_convert_fusion
  107.0 25.7 %all_to_all.15 = bf16[4,3,192,384]{3,2,1,0:T(8,128)(2,1)S(1)} all-to-all(bf16[4,3,192,384]{3,2,1,0:T(8,128)(2,1)S(1)} %pad_maximum_fusion), channel_id=1, replica_groups={{0,32,64,96},{8,40,72,104},{16,48,80,112},{24,56,88,120},{128,160,192,2..., dimensions={0} | all-to-all | bytes 3538944 | tf_op jit(solution)/shard_map/all_to_all | solution.py:50
  132.7 0.5 reduce_sum.31
  133.3 0.4 fusion.27
  133.7 0.6 fusion.5
  134.3 13.7 %all_gather.3 = bf16[768,384]{1,0:T(8,128)(2,1)S(1)} all-gather(bf16[192,384]{1,0:T(8,128)(2,1)S(1)} %bitcast.169), channel_id=1, replica_groups={{0,32,64,96},{8,40,72,104},{16,48,80,112},{24,56,88,120},{128,160,192,2..., dimensions={0}, use_global_device_ids=true | all-gather | bytes 737280 | tf_op jit(solution)/shard_map/all_gather | solution.py:128
  148.0 0.8 fusion.28
  148.9 1.9 %collective-permute-start.10 = (bf16[4,4,24,768]{3,2,1,0:T(8,128)(2,1)S(1)}, bf16[4,4,24,768]{3,2,1,0:T(8,128)(2,1)S(1)}, u32[]{:S(2)}, u32[]{:S(2)}) collective-permute-start(bf16[4,4,24,768]{3,2,1,0:T(8,128)(2,1)S(1)} %fusion.8), channel_id=1, source_target_pairs={{0,1},{1,0},{2,3},{3,2},{4,5},{5,4},{6,7},{7,6},{8,9},{9,8},{10,11... | collective-permute-start | bytes 1769480 | tf_op jit(solution)/shard_map/ppermute | solution.py:46
  150.8 2.0 %collective-permute-done.10 = bf16[4,4,24,768]{3,2,1,0:T(8,128)(2,1)S(1)} collective-permute-done((bf16[4,4,24,768]{3,2,1,0:T(8,128)(2,1)S(1)}, bf16[4,4,24,768]{3,2,1,0:T(8,128)(2,1)S(1)}, u32[]{:S(2)}, u32[]{:S(2)}) %collective-permute-start.10) | collective-permute-done | bytes 589856 | tf_op jit(solution)/shard_map/ppermute | solution.py:46
  153.0 2.3 %collective-permute-start.11 = (bf16[4,24,768]{2,1,0:T(8,128)(2,1)S(1)}, bf16[4,24,768]{2,1,0:T(8,128)(2,1)S(1)}, u32[]{:S(2)}, u32[]{:S(2)}) collective-permute-start(bf16[4,24,768]{2,1,0:T(8,128)(2,1)S(1)} %get-tuple-element.13), channel_id=1, source_target_pairs={{0,6},{1,7},{2,0},{3,1},{4,2},{5,3},{6,4},{7,5},{8,14},{9,15},{10,... | collective-permute-start | bytes 442376 | tf_op jit(solution)/shard_map/ppermute | solution.py:42
  155.3 2.5 %collective-permute-start.12 = (bf16[4,24,768]{2,1,0:T(8,128)(2,1)S(1)}, bf16[4,24,768]{2,1,0:T(8,128)(2,1)S(1)}, u32[]{:S(2)}, u32[]{:S(2)}) collective-permute-start(bf16[4,24,768]{2,1,0:T(8,128)(2,1)S(1)} %get-tuple-element.15), channel_id=1, source_target_pairs={{0,4},{1,5},{2,6},{3,7},{4,0},{5,1},{6,2},{7,3},{8,12},{9,13},{10,... | collective-permute-start | bytes 442376 | tf_op jit(solution)/shard_map/ppermute | solution.py:42
  157.8 3.6 %collective-permute-start.13 = (bf16[4,24,768]{2,1,0:T(8,128)(2,1)S(1)}, bf16[4,24,768]{2,1,0:T(8,128)(2,1)S(1)}, u32[]{:S(2)}, u32[]{:S(2)}) collective-permute-start(bf16[4,24,768]{2,1,0:T(8,128)(2,1)S(1)} %get-tuple-element.14), channel_id=1, source_target_pairs={{0,2},{1,3},{2,4},{3,5},{4,6},{5,7},{6,0},{7,1},{8,10},{9,11},{10,... | collective-permute-start | bytes 442376 | tf_op jit(solution)/shard_map/ppermute | solution.py:42
  161.4 0.7 collective-permute-done.11
  162.1 8.0 %collective-permute-done.12 = bf16[4,24,768]{2,1,0:T(8,128)(2,1)S(1)} collective-permute-done((bf16[4,24,768]{2,1,0:T(8,128)(2,1)S(1)}, bf16[4,24,768]{2,1,0:T(8,128)(2,1)S(1)}, u32[]{:S(2)}, u32[]{:S(2)}) %collective-permute-start.12) | collective-permute-done | bytes 147488 | tf_op jit(solution)/shard_map/ppermute | solution.py:42
  170.1 0.7 fusion.15
  170.9 3.3 %all-to-all-start.2 = ((bf16[4,24,768]{2,1,0:T(8,128)(2,1)}), bf16[4,24,768]{2,1,0:T(8,128)(2,1)S(1)}, u32[]{:S(2)}, u32[]{:S(2)}) async-start(bf16[4,24,768]{2,1,0:T(8,128)(2,1)} %fusion.15), calls=%async_computation.2 | async-start | bytes 294912 | tf_op jit(solution)/shard_map/all_to_all | solution.py:50
  174.3 5.9 %all-to-all-done.2 = bf16[4,24,768]{2,1,0:T(8,128)(2,1)S(1)} async-done(((bf16[4,24,768]{2,1,0:T(8,128)(2,1)}), bf16[4,24,768]{2,1,0:T(8,128)(2,1)S(1)}, u32[]{:S(2)}, u32[]{:S(2)}) %all-to-all-start.2) | async-done | bytes 147488 | tf_op jit(solution)/shard_map/all_to_all | solution.py:50
  180.2 0.3 reshape.162
  180.5 0.3 copy.60
  180.8 0.4 reshape.161
  181.2 0.8 add_convert_fusion
  (37 shorter events, 1.9 us)
Async XLA Ops:
  0.6 0.9 copy-start
  3.6 29.9 %collective-permute-start.4 = (bf16[4,48,384]{2,1,0:T(8,128)(2,1)S(1)}, bf16[4,48,384]{2,1,0:T(8,128)(2,1)S(1)}, u32[]{:S(2)}, u32[]{:S(2)}) collective-permute-start(bf16[4,48,384]{2,1,0:T(8,128)(2,1)S(1)} %pad_maximum_fusion.3), channel_id=1, source_target_pairs={{0,128},{8,136},{16,144},{24,152},{32,160},{40,168},{48,176},{56,1... | collective-permute-start | bytes 442376 | tf_op jit(solution)/shard_map/ppermute | solution.py:35
  12.7 31.6 %collective-permute-start.5 = (bf16[4,48,384]{2,1,0:T(8,128)(2,1)S(1)}, bf16[4,48,384]{2,1,0:T(8,128)(2,1)S(1)}, u32[]{:S(2)}, u32[]{:S(2)}) collective-permute-start(bf16[4,48,384]{2,1,0:T(8,128)(2,1)S(1)} %pad_maximum_fusion.3), channel_id=1, source_target_pairs={{0,256},{8,264},{16,272},{24,280},{32,288},{40,296},{48,304},{56,3... | collective-permute-start | bytes 442376 | tf_op jit(solution)/shard_map/ppermute | solution.py:35
  23.6 25.4 %collective-permute-start.6 = (bf16[4,48,384]{2,1,0:T(8,128)(2,1)S(1)}, bf16[4,48,384]{2,1,0:T(8,128)(2,1)S(1)}, u32[]{:S(2)}, u32[]{:S(2)}) collective-permute-start(bf16[4,48,384]{2,1,0:T(8,128)(2,1)S(1)} %pad_maximum_fusion.3), channel_id=1, source_target_pairs={{0,384},{8,392},{16,400},{24,408},{32,416},{40,424},{48,432},{56,4... | collective-permute-start | bytes 442376 | tf_op jit(solution)/shard_map/ppermute | solution.py:35
  49.1 35.6 %collective-permute-start.7 = (bf16[4,4,48,384]{3,2,1,0:T(8,128)(2,1)S(1)}, bf16[4,4,48,384]{3,2,1,0:T(8,128)(2,1)S(1)}, u32[]{:S(2)}, u32[]{:S(2)}) collective-permute-start(bf16[4,4,48,384]{3,2,1,0:T(8,128)(2,1)S(1)} %bitcast_dynamic-update-slice_fusion.4), channel_id=1, source_target_pairs={{0,8},{8,16},{16,24},{24,0},{32,40},{40,48},{48,56},{56,32},{64,72... | collective-permute-start | bytes 1769480 | tf_op jit(solution)/shard_map/ppermute | solution.py:35
  53.6 10.5 %all-to-all-start = ((bf16[4,24,768]{2,1,0:T(8,128)(2,1)}), bf16[4,24,768]{2,1,0:T(8,128)(2,1)S(1)}, u32[]{:S(2)}, u32[]{:S(2)}) async-start(bf16[4,24,768]{2,1,0:T(8,128)(2,1)} %reshape.156), calls=%async_computation | async-start | bytes 294912 | tf_op jit(solution)/shard_map/all_to_all | solution.py:50
  64.0 14.5 %collective-permute-start = (bf16[4,24,768]{2,1,0:T(8,128)(2,1)S(1)}, bf16[4,24,768]{2,1,0:T(8,128)(2,1)S(1)}, u32[]{:S(2)}, u32[]{:S(2)}) collective-permute-start(bf16[4,24,768]{2,1,0:T(8,128)(2,1)S(1)} %all-to-all-done), channel_id=1, source_target_pairs={{0,2},{1,3},{2,4},{3,5},{4,6},{5,7},{6,0},{7,1},{8,10},{9,11},{10,... | collective-permute-start | bytes 442376 | tf_op jit(solution)/shard_map/ppermute | solution.py:42
  66.0 16.6 %collective-permute-start.1 = (bf16[4,24,768]{2,1,0:T(8,128)(2,1)S(1)}, bf16[4,24,768]{2,1,0:T(8,128)(2,1)S(1)}, u32[]{:S(2)}, u32[]{:S(2)}) collective-permute-start(bf16[4,24,768]{2,1,0:T(8,128)(2,1)S(1)} %all-to-all-done), channel_id=1, source_target_pairs={{0,4},{1,5},{2,6},{3,7},{4,0},{5,1},{6,2},{7,3},{8,12},{9,13},{10,... | collective-permute-start | bytes 442376 | tf_op jit(solution)/shard_map/ppermute | solution.py:42
  70.2 12.4 %collective-permute-start.2 = (bf16[4,24,768]{2,1,0:T(8,128)(2,1)S(1)}, bf16[4,24,768]{2,1,0:T(8,128)(2,1)S(1)}, u32[]{:S(2)}, u32[]{:S(2)}) collective-permute-start(bf16[4,24,768]{2,1,0:T(8,128)(2,1)S(1)} %all-to-all-done), channel_id=1, source_target_pairs={{0,6},{1,7},{2,0},{3,1},{4,2},{5,3},{6,4},{7,5},{8,14},{9,15},{10,... | collective-permute-start | bytes 442376 | tf_op jit(solution)/shard_map/ppermute | solution.py:42
  75.0 19.7 %collective-permute-start.8 = (bf16[4,4,48,384]{3,2,1,0:T(8,128)(2,1)S(1)}, bf16[4,4,48,384]{3,2,1,0:T(8,128)(2,1)S(1)}, u32[]{:S(2)}, u32[]{:S(2)}) collective-permute-start(bf16[4,4,48,384]{3,2,1,0:T(8,128)(2,1)S(1)} %bitcast_dynamic-update-slice_fusion.4), channel_id=1, source_target_pairs={{0,16},{8,24},{16,0},{24,8},{32,48},{40,56},{48,32},{56,40},{64,80... | collective-permute-start | bytes 1769480 | tf_op jit(solution)/shard_map/ppermute | solution.py:35
  78.5 25.3 %collective-permute-start.9 = (bf16[4,4,48,384]{3,2,1,0:T(8,128)(2,1)S(1)}, bf16[4,4,48,384]{3,2,1,0:T(8,128)(2,1)S(1)}, u32[]{:S(2)}, u32[]{:S(2)}) collective-permute-start(bf16[4,4,48,384]{3,2,1,0:T(8,128)(2,1)S(1)} %bitcast_dynamic-update-slice_fusion.4), channel_id=1, source_target_pairs={{0,24},{8,0},{16,8},{24,16},{32,56},{40,32},{48,40},{56,48},{64,88... | collective-permute-start | bytes 1769480 | tf_op jit(solution)/shard_map/ppermute | solution.py:35
  82.7 21.4 %collective-permute-start.3 = (bf16[4,4,24,768]{3,2,0,1:T(8,128)(2,1)S(1)}, bf16[4,4,24,768]{3,2,0,1:T(8,128)(2,1)S(1)}, u32[]{:S(2)}, u32[]{:S(2)}) collective-permute-start(bf16[4,4,24,768]{3,2,0,1:T(8,128)(2,1)S(1)} %get-tuple-element.17), channel_id=1, source_target_pairs={{0,1},{1,0},{2,3},{3,2},{4,5},{5,4},{6,7},{7,6},{8,9},{9,8},{10,11... | collective-permute-start | bytes 1769480 | tf_op jit(solution)/shard_map/ppermute | solution.py:46
  148.9 3.9 %collective-permute-start.10 = (bf16[4,4,24,768]{3,2,1,0:T(8,128)(2,1)S(1)}, bf16[4,4,24,768]{3,2,1,0:T(8,128)(2,1)S(1)}, u32[]{:S(2)}, u32[]{:S(2)}) collective-permute-start(bf16[4,4,24,768]{3,2,1,0:T(8,128)(2,1)S(1)} %fusion.8), channel_id=1, source_target_pairs={{0,1},{1,0},{2,3},{3,2},{4,5},{5,4},{6,7},{7,6},{8,9},{9,8},{10,11... | collective-permute-start | bytes 1769480 | tf_op jit(solution)/shard_map/ppermute | solution.py:46
  153.0 28.2 %copy-start.1 = (bf16[1,24,3072]{2,1,0:T(8,128)(2,1)S(1)}, bf16[1,24,3072]{2,1,0:T(8,128)(2,1)}, u32[]{:S(2)}) copy-start(bf16[1,24,3072]{2,1,0:T(8,128)(2,1)} %param.10) | copy-start | bytes 442372
  153.0 28.2 %copy-start.2 = (bf16[1,24,3072]{2,1,0:T(8,128)(2,1)S(1)}, bf16[1,24,3072]{2,1,0:T(8,128)(2,1)}, u32[]{:S(2)}) copy-start(bf16[1,24,3072]{2,1,0:T(8,128)(2,1)} %param.11) | copy-start | bytes 442372
  153.0 9.1 %collective-permute-start.11 = (bf16[4,24,768]{2,1,0:T(8,128)(2,1)S(1)}, bf16[4,24,768]{2,1,0:T(8,128)(2,1)S(1)}, u32[]{:S(2)}, u32[]{:S(2)}) collective-permute-start(bf16[4,24,768]{2,1,0:T(8,128)(2,1)S(1)} %get-tuple-element.13), channel_id=1, source_target_pairs={{0,6},{1,7},{2,0},{3,1},{4,2},{5,3},{6,4},{7,5},{8,14},{9,15},{10,... | collective-permute-start | bytes 442376 | tf_op jit(solution)/shard_map/ppermute | solution.py:42
  155.3 14.8 %collective-permute-start.12 = (bf16[4,24,768]{2,1,0:T(8,128)(2,1)S(1)}, bf16[4,24,768]{2,1,0:T(8,128)(2,1)S(1)}, u32[]{:S(2)}, u32[]{:S(2)}) collective-permute-start(bf16[4,24,768]{2,1,0:T(8,128)(2,1)S(1)} %get-tuple-element.15), channel_id=1, source_target_pairs={{0,4},{1,5},{2,6},{3,7},{4,0},{5,1},{6,2},{7,3},{8,12},{9,13},{10,... | collective-permute-start | bytes 442376 | tf_op jit(solution)/shard_map/ppermute | solution.py:42
  157.8 12.3 %collective-permute-start.13 = (bf16[4,24,768]{2,1,0:T(8,128)(2,1)S(1)}, bf16[4,24,768]{2,1,0:T(8,128)(2,1)S(1)}, u32[]{:S(2)}, u32[]{:S(2)}) collective-permute-start(bf16[4,24,768]{2,1,0:T(8,128)(2,1)S(1)} %get-tuple-element.14), channel_id=1, source_target_pairs={{0,2},{1,3},{2,4},{3,5},{4,6},{5,7},{6,0},{7,1},{8,10},{9,11},{10,... | collective-permute-start | bytes 442376 | tf_op jit(solution)/shard_map/ppermute | solution.py:42
  170.9 9.4 %all-to-all-start.2 = ((bf16[4,24,768]{2,1,0:T(8,128)(2,1)}), bf16[4,24,768]{2,1,0:T(8,128)(2,1)S(1)}, u32[]{:S(2)}, u32[]{:S(2)}) async-start(bf16[4,24,768]{2,1,0:T(8,128)(2,1)} %fusion.15), calls=%async_computation.2 | async-start | bytes 294912 | tf_op jit(solution)/shard_map/all_to_all | solution.py:50

commit v2 on v1

--- a/solution.py
+++ b/solution.py
@@ -23,11 +23,13 @@
 
 
 Y_GROUPS = [[fsdp_index(z, y, x) for y in range(QUAD)] for z in range(QUAD) for x in range(QUAD)]
+Z_GROUPS = [[fsdp_index(z, y, x) for z in range(QUAD)] for y in range(QUAD) for x in range(QUAD)]
+X_GROUPS = [[fsdp_index(z, y, x) for x in range(QUAD)] for z in range(QUAD) for y in range(QUAD)]
 
 
-def shift_fsdp(value, dz=0, dx=0):
+def shift_fsdp(value, dy=0, dx=0):
     pairs = [
-        (fsdp_index(z, y, x), fsdp_index(z + dz, y, x + dx))
+        (fsdp_index(z, y, x), fsdp_index(z, y + dy, x + dx))
         for z in range(QUAD)
         for y in range(QUAD)
         for x in range(QUAD)
@@ -42,12 +44,26 @@
     return lax.ppermute(value, "sp", pairs)
 
 
+def place(buffer, block, axis, index):
+    start = [jnp.int32(0)] * buffer.ndim
+    start[axis] = index.astype(jnp.int32)
+    return lax.dynamic_update_slice(buffer, jnp.expand_dims(block, axis), start)
+
+
 def other_core(value):
     return lax.ppermute(value, "sp", [(i, i ^ 1) for i in range(2 * QUAD)])
 
 
-def exchange_y(value):
-    return lax.all_to_all(value, "fsdp", 0, 0, axis_index_groups=Y_GROUPS, tiled=True)
+def exchange(value, axis, groups):
+    return lax.all_to_all(value, axis, 0, 0, axis_index_groups=groups, tiled=True)
+
+
+def gather(value, axis, groups):
+    return exchange(jnp.broadcast_to(value[None], (QUAD,) + value.shape), axis, groups)
+
+
+def after(value, earlier):
+    return value + earlier.ravel()[0] * 0
 
 
 def per_device(
@@ -62,7 +78,7 @@
     modulation,
     timestep,
 ):
-    z_hi = lax.axis_index("fsdp") // (QUAD * QUAD)
+    y = lax.axis_index("fsdp") // QUAD % QUAD
     x = lax.axis_index("fsdp") % QUAD
     rows, width = latents.shape[1:]
     part = base_qkv.shape[1]
@@ -77,22 +93,22 @@
     merged_qkv = (base_qkv.astype(jnp.float32) + lowrank).astype(jnp.bfloat16)
     lowrank_out = jnp.einsum("rk,kc->cr", down_out, up_out, preferred_element_type=jnp.float32)
     merged_out = (base_out.T.astype(jnp.float32) + lowrank_out).astype(jnp.bfloat16)
+
     merged = jnp.concatenate([merged_qkv, merged_out[None]], axis=0)
+    held = lax.all_gather(merged, "fsdp", axis_index_groups=Z_GROUPS, axis=0)
 
-    def place(buffer, block, axis, index):
-        start = [jnp.int32(0)] * buffer.ndim
-        start[axis] = index.astype(jnp.int32)
-        return lax.dynamic_update_slice(buffer, jnp.expand_dims(block, axis), start)
+    weights = gather(held[:, :3], "fsdp", X_GROUPS).transpose(2, 1, 0, 3, 4)
+    weights = weights.reshape(3, slab, head_cols)
 
-    held = jnp.zeros((4, QUAD, part, head_cols), jnp.bfloat16)
+    row = jnp.zeros((QUAD, QUAD, part, head_cols), jnp.bfloat16)
     for k in range(QUAD):
-        block = merged if k == 0 else shift_fsdp(merged, dz=k)
-        held = place(held, block, 1, (z_hi - k) % QUAD)
-    weights = jnp.zeros((4, QUAD, QUAD, part, head_cols), jnp.bfloat16)
+        block = held[:, 3] if k == 0 else shift_fsdp(held[:, 3], dy=k)
+        row = place(row, block, 1, (y - k) % QUAD)
+    out_rows = jnp.zeros((QUAD, QUAD, QUAD, part, head_cols), jnp.bfloat16)
     for k in range(QUAD):
-        block = held if k == 0 else shift_fsdp(held, dx=k)
-        weights = place(weights, block, 2, (x - k) % QUAD)
-    weights = weights.reshape(4, slab, head_cols)
+        block = row if k == 0 else shift_fsdp(row, dx=k)
+        out_rows = place(out_rows, block, 2, (x - k) % QUAD)
+    out_rows = out_rows.reshape(width, head_cols)
 
     step_index = timestep[0]
     mod_rows = lax.dynamic_index_in_dim(modulation, step_index, 0, keepdims=False)
@@ -102,7 +118,8 @@
         latent_f * lax.rsqrt(mean_square + EPSILON) * (1.0 + mod_rows[1]) + mod_rows[0]
     ).astype(jnp.bfloat16)
     slices = normalized_rows.reshape(rows, QUAD, QUAD, slab // QUAD).transpose(2, 0, 1, 3)
-    mine = exchange_y(slices.reshape(QUAD, rows, slab))
+    mine = exchange(slices.reshape(QUAD, rows, slab), "fsdp", Y_GROUPS)
+    mine = after(mine, held)
     run = jnp.stack([mine] + [shift_run(mine, k) for k in range(1, QUAD)], axis=1)
     both = jnp.stack([run, other_core(run)], axis=2)
     tokens = both.reshape(QUAD * seq_len, slab)
@@ -116,7 +133,8 @@
         ],
         axis=1,
     )
-    projected = jnp.sum(exchange_y(partial).astype(jnp.float32), axis=0).astype(jnp.bfloat16)
+    projected = exchange(partial, "fsdp", Y_GROUPS).astype(jnp.float32)
+    projected = jnp.sum(projected, axis=0).astype(jnp.bfloat16)
     heads = projected.reshape(3, seq_len, heads_here, HEAD_DIM).transpose(0, 2, 1, 3)
     scores = jnp.einsum("hqe,hke->hqk", heads[0], heads[1], preferred_element_type=jnp.float32)
     attention_weights = jax.nn.softmax(scores * (1.0 / HEAD_DIM**0.5), axis=-1).astype(jnp.bfloat16)
@@ -125,23 +143,21 @@
     ).astype(jnp.bfloat16)
     attended = attended.reshape(seq_len, head_cols)
 
-    gathered = lax.all_gather(attended, "fsdp", axis_index_groups=Y_GROUPS, axis=0, tiled=True)
-    out_partial = lax.dot_general(
-        gathered, weights[3], (((1,), (1,)), ((), ())), preferred_element_type=jnp.float32
-    ).reshape(QUAD, QUAD, 2, rows, slab)
-    pair = out_partial[:, :, 0] + other_core(out_partial[:, :, 1].astype(jnp.bfloat16)).astype(
-        jnp.float32
-    )
-    total = pair[:, 0]
+    by_core = attended.reshape(QUAD, 2, rows, head_cols)
+
+    def project_out(flip):
+        return lax.dot_general(
+            by_core[:, flip].reshape(QUAD * rows, head_cols),
+            out_rows,
+            (((1,), (1,)), ((), ())),
+            preferred_element_type=jnp.float32,
+        )
+
+    theirs = other_core(project_out(1).astype(jnp.bfloat16)).astype(jnp.float32)
+    pair = (project_out(0) + theirs).reshape(QUAD, rows, width)
+    block_out = pair[0]
     for k in range(1, QUAD):
-        total = total + shift_run(pair[:, k].astype(jnp.bfloat16), -k).astype(jnp.float32)
-    columns = exchange_y(total.astype(jnp.bfloat16))
-    block_out = (
-        columns.reshape(QUAD, rows, QUAD, slab // QUAD)
-        .transpose(1, 2, 0, 3)
-        .reshape(rows, width)
-        .astype(jnp.float32)
-    )
+        block_out = block_out + shift_run(pair[k].astype(jnp.bfloat16), -k).astype(jnp.float32)
 
     velocity = ((1.0 + mod_rows[2]) * block_out).astype(jnp.bfloat16)
     position = step_index.astype(jnp.float32)

time: 183 us -> 159 us (0.87)
  the two profiles are of different devices: /device:TPU:2 before, /device:TPU:43 now
where the time goes in v2:
time: 159 us; the launch traced here: 158 us
  starting transfers between devices  64.8 us (41%)
  waiting for transfers between devices  35.2 us (22%)
  blocking collectives  28.9 us (18%)
  local copies, waits for them, and re-layouts  11.7 us (7%)
  other arithmetic  7.65 us (5%)
  matrix products  7.07 us (4%)
  between operations  2.68 us (2%)
    all_gather x1, blocking collectives, per_device(): held = lax.all_gather(merged, 'fsdp', axis_index_groups=Z_GROUPS, axis=0)  28.9 us
    ppermute x6, waiting for transfers between devices, shift_fsdp(): return lax.ppermute(value, 'fsdp', pairs)  21.9 us
    ppermute x6, starting transfers between devices, shift_fsdp(): return lax.ppermute(value, 'fsdp', pairs)  21 us
    ppermute x6, starting transfers between devices, shift_run(): return lax.ppermute(value, 'sp', pairs)  20 us
    all_to_all x3, starting transfers between devices, exchange(): lax.all_to_all(value, axis, 0, 0, axis_index_groups=groups, tiled=True)  14.3 us
    ppermute x6, waiting for transfers between devices, shift_run(): return lax.ppermute(value, 'sp', pairs)  11.7 us
    ppermute x2, starting transfers between devices, other_core(): return lax.ppermute(value, 'sp', [(i, i ^ 1) for i in range(2 * QUAD)])  9.45 us
  transfers between devices with their start and end apart: 17, of which 6 were waited for; matrix products, arithmetic and copies ran while one was open for 7% of the time, Pallas kernels for 0%

profile of v2, /device:TPU:43, one launch (start us, length us, event | category | flops | bytes accessed | tf_op | source)
XLA Modules:
  0.0 158.0 jit_solution(2886547902223957042)
XLA Ops:
  0.7 1.3 reshape.97
  2.0 1.0 fusion.15
  3.7 1.1 fusion.18
  5.2 0.9 reshape.92
  6.1 4.3 %all-to-all-start = ((bf16[4,24,768]{2,1,0:T(8,128)(2,1)}), bf16[4,24,768]{2,1,0:T(8,128)(2,1)S(1)}, u32[]{:S(2)}, u32[]{:S(2)}) async-start(bf16[4,24,768]{2,1,0:T(8,128)(2,1)} %reshape.92), calls=%async_computation | async-start | bytes 294912 | tf_op jit(solution)/shard_map/all_to_all | solution.py:58
  10.8 28.9 %all-gather = bf16[16,48,384]{2,1,0:T(8,128)(2,1)S(1)} all-gather(bf16[4,48,384]{2,1,0:T(8,128)(2,1)S(1)} %pad_maximum_fusion.3), channel_id=2, replica_groups={{0,128,256,384},{8,136,264,392},{16,144,272,400},{24,152,280,408},{32,1..., dimensions={0}, use_global_device_ids=true | all-gather | bytes 737280 | tf_op jit(solution)/shard_map/all_gather | solution.py:98
  39.8 3.3 %collective-permute-start.4 = (bf16[4,48,384]{2,1,0:T(8,128)(2,1)S(1)}, bf16[4,48,384]{2,1,0:T(8,128)(2,1)S(1)}, u32[]{:S(2)}, u32[]{:S(2)}) collective-permute-start(bf16[4,48,384]{2,1,0:T(8,128)(2,1)S(1)} %get-tuple-element.13), channel_id=1, source_target_pairs={{0,32},{8,40},{16,48},{24,56},{32,64},{40,72},{48,80},{56,88},{64,... | collective-permute-start | bytes 442376 | tf_op jit(solution)/shard_map/ppermute | solution.py:37
  43.1 4.2 %collective-permute-start.5 = (bf16[4,48,384]{2,1,0:T(8,128)(2,1)S(1)}, bf16[4,48,384]{2,1,0:T(8,128)(2,1)S(1)}, u32[]{:S(2)}, u32[]{:S(2)}) collective-permute-start(bf16[4,48,384]{2,1,0:T(8,128)(2,1)S(1)} %get-tuple-element.13), channel_id=1, source_target_pairs={{0,64},{8,72},{16,80},{24,88},{32,96},{40,104},{48,112},{56,120},{... | collective-permute-start | bytes 442376 | tf_op jit(solution)/shard_map/ppermute | solution.py:37
  47.3 0.3 reshape.93
  47.7 0.5 slice.88
  48.8 1.4 broadcast_in_dim.48
  50.3 4.4 %all-to-all-start.1 = ((bf16[4,4,3,48,384]{4,3,1,2,0:T(8,128)(2,1)}), bf16[4,4,3,48,384]{4,3,1,2,0:T(8,128)(2,1)S(1)}, u32[]{:S(2)}, u32[]{:S(2)}) async-start(bf16[4,4,3,48,384]{4,3,1,2,0:T(8,128)(2,1)} %broadcast_in_dim.48), calls=%async_computation.1 | async-start | bytes 3538944 | tf_op jit(solution)/shard_map/all_to_all | solution.py:58
  54.7 3.4 %collective-permute-start.2 = (bf16[4,24,768]{2,1,0:T(8,128)(2,1)S(1)}, bf16[4,24,768]{2,1,0:T(8,128)(2,1)S(1)}, u32[]{:S(2)}, u32[]{:S(2)}) collective-permute-start(bf16[4,24,768]{2,1,0:T(8,128)(2,1)S(1)} %broadcast_add_fusion), channel_id=1, source_target_pairs={{0,6},{1,7},{2,0},{3,1},{4,2},{5,3},{6,4},{7,5},{8,14},{9,15},{10,... | collective-permute-start | bytes 442376 | tf_op jit(solution)/shard_map/ppermute | solution.py:44
  58.1 2.8 %collective-permute-start.1 = (bf16[4,24,768]{2,1,0:T(8,128)(2,1)S(1)}, bf16[4,24,768]{2,1,0:T(8,128)(2,1)S(1)}, u32[]{:S(2)}, u32[]{:S(2)}) collective-permute-start(bf16[4,24,768]{2,1,0:T(8,128)(2,1)S(1)} %broadcast_add_fusion), channel_id=1, source_target_pairs={{0,4},{1,5},{2,6},{3,7},{4,0},{5,1},{6,2},{7,3},{8,12},{9,13},{10,... | collective-permute-start | bytes 442376 | tf_op jit(solution)/shard_map/ppermute | solution.py:44
  60.9 4.3 %collective-permute-start = (bf16[4,24,768]{2,1,0:T(8,128)(2,1)S(1)}, bf16[4,24,768]{2,1,0:T(8,128)(2,1)S(1)}, u32[]{:S(2)}, u32[]{:S(2)}) collective-permute-start(bf16[4,24,768]{2,1,0:T(8,128)(2,1)S(1)} %broadcast_add_fusion), channel_id=1, source_target_pairs={{0,2},{1,3},{2,4},{3,5},{4,6},{5,7},{6,0},{7,1},{8,10},{9,11},{10,... | collective-permute-start | bytes 442376 | tf_op jit(solution)/shard_map/ppermute | solution.py:44
  65.2 4.0 %collective-permute-start.6 = (bf16[4,48,384]{2,1,0:T(8,128)(2,1)S(1)}, bf16[4,48,384]{2,1,0:T(8,128)(2,1)S(1)}, u32[]{:S(2)}, u32[]{:S(2)}) collective-permute-start(bf16[4,48,384]{2,1,0:T(8,128)(2,1)S(1)} %get-tuple-element.13), channel_id=1, source_target_pairs={{0,96},{8,104},{16,112},{24,120},{32,0},{40,8},{48,16},{56,24},{64... | collective-permute-start | bytes 442376 | tf_op jit(solution)/shard_map/ppermute | solution.py:37
  69.2 1.9 %collective-permute-done = bf16[4,24,768]{2,1,0:T(8,128)(2,1)S(1)} collective-permute-done((bf16[4,24,768]{2,1,0:T(8,128)(2,1)S(1)}, bf16[4,24,768]{2,1,0:T(8,128)(2,1)S(1)}, u32[]{:S(2)}, u32[]{:S(2)}) %collective-permute-start) | collective-permute-done | bytes 147488 | tf_op jit(solution)/shard_map/ppermute | solution.py:44
  71.2 7.1 %collective-permute-start.3 = (bf16[4,4,24,768]{3,2,0,1:T(8,128)(2,1)S(1)}, bf16[4,4,24,768]{3,2,0,1:T(8,128)(2,1)S(1)}, u32[]{:S(2)}, u32[]{:S(2)}) collective-permute-start(bf16[4,4,24,768]{3,2,0,1:T(8,128)(2,1)S(1)} %get-tuple-element.16), channel_id=1, source_target_pairs={{0,1},{1,0},{2,3},{3,2},{4,5},{5,4},{6,7},{7,6},{8,9},{9,8},{10,11... | collective-permute-start | bytes 1769480 | tf_op jit(solution)/shard_map/ppermute | solution.py:54
  78.4 3.1 %collective-permute-start.7 = (bf16[4,4,48,384]{3,2,1,0:T(8,128)(2,1)S(1)}, bf16[4,4,48,384]{3,2,1,0:T(8,128)(2,1)}, u32[]{:S(2)}, u32[]{:S(2)}) collective-permute-start(bf16[4,4,48,384]{3,2,1,0:T(8,128)(2,1)S(1)} %bitcast_dynamic-update-slice_fusion.4), channel_id=1, source_target_pairs={{0,8},{8,16},{16,24},{24,0},{32,40},{40,48},{48,56},{56,32},{64,72... | collective-permute-start | bytes 1769480 | tf_op jit(solution)/shard_map/ppermute | solution.py:37
  81.6 1.1 copy.51
  83.2 1.1 copy-done.2
  84.2 0.8 convolution_convert_fusion.1
  85.0 0.8 convolution_convert_fusion.2
  85.8 0.8 convolution_convert_fusion.3
  86.6 1.4 pad_maximum_fusion
  88.0 5.5 %all-to-all-start.2 = ((bf16[4,3,192,384]{3,2,1,0:T(8,128)(2,1)}), bf16[4,3,192,384]{3,2,1,0:T(8,128)(2,1)}, u32[]{:S(2)}, u32[]{:S(2)}) async-start(bf16[4,3,192,384]{3,2,1,0:T(8,128)(2,1)} %pad_maximum_fusion), calls=%async_computation.2 | async-start | bytes 3538944 | tf_op jit(solution)/shard_map/all_to_all | solution.py:58
  93.6 2.5 %collective-permute-start.8 = (bf16[4,4,48,384]{3,2,1,0:T(8,128)(2,1)S(1)}, bf16[4,4,48,384]{3,2,1,0:T(8,128)(2,1)}, u32[]{:S(2)}, u32[]{:S(2)}) collective-permute-start(bf16[4,4,48,384]{3,2,1,0:T(8,128)(2,1)S(1)} %bitcast_dynamic-update-slice_fusion.4), channel_id=1, source_target_pairs={{0,16},{8,24},{16,0},{24,8},{32,48},{40,56},{48,32},{56,40},{64,80... | collective-permute-start | bytes 1769480 | tf_op jit(solution)/shard_map/ppermute | solution.py:37
  96.2 4.0 %collective-permute-start.9 = (bf16[4,4,48,384]{3,2,1,0:T(8,128)(2,1)S(1)}, bf16[4,4,48,384]{3,2,1,0:T(8,128)(2,1)S(1)}, u32[]{:S(2)}, u32[]{:S(2)}) collective-permute-start(bf16[4,4,48,384]{3,2,1,0:T(8,128)(2,1)S(1)} %bitcast_dynamic-update-slice_fusion.4), channel_id=1, source_target_pairs={{0,24},{8,0},{16,8},{24,16},{32,56},{40,32},{48,40},{56,48},{64,88... | collective-permute-start | bytes 1769480 | tf_op jit(solution)/shard_map/ppermute | solution.py:37
  100.1 0.3 broadcast_in_dim.49
  100.6 1.2 bitcast_dynamic-update-slice_fusion.1
  101.8 8.1 %collective-permute-done.8 = bf16[4,4,48,384]{3,2,1,0:T(8,128)(2,1)} collective-permute-done((bf16[4,4,48,384]{3,2,1,0:T(8,128)(2,1)S(1)}, bf16[4,4,48,384]{3,2,1,0:T(8,128)(2,1)}, u32[]{:S(2)}, u32[]{:S(2)}) %collective-permute-start.8) | collective-permute-done | bytes 589856 | tf_op jit(solution)/shard_map/ppermute | solution.py:37
  109.8 1.2 bitcast_dynamic-update-slice_fusion
  111.0 13.8 %collective-permute-done.9 = bf16[4,4,48,384]{3,2,1,0:T(8,128)(2,1)S(1)} collective-permute-done((bf16[4,4,48,384]{3,2,1,0:T(8,128)(2,1)S(1)}, bf16[4,4,48,384]{3,2,1,0:T(8,128)(2,1)S(1)}, u32[]{:S(2)}, u32[]{:S(2)}) %collective-permute-start.9) | collective-permute-done | bytes 589856 | tf_op jit(solution)/shard_map/ppermute | solution.py:37
  125.0 1.8 %reduce_sum.31 = bf16[3,192,384]{2,1,0:T(8,128)(2,1)S(1)} reduce(bf16[4,3,192,384]{3,2,1,0:T(8,128)(2,1)} %all-to-all-done.2, bf16[]{:T(256)} %constant.101.clone.1), dimensions={0}, to_apply=%region_1.2 | reduce | flops 663552 | bytes 2211842 | tf_op jit(solution)/shard_map/reduce_sum | solution.py:137
  126.9 0.4 fusion.26
  127.3 0.3 convolution_multiply_fusion
  127.5 1.0 fusion.4
  128.6 1.0 copy.59
  129.8 0.9 convolution_convert_fusion
  130.6 2.4 %collective-permute-start.10 = (bf16[96,3072]{1,0:T(8,128)(2,1)S(1)}, bf16[96,3072]{1,0:T(8,128)(2,1)S(1)}, u32[]{:S(2)}, u32[]{:S(2)}) collective-permute-start(bf16[96,3072]{1,0:T(8,128)(2,1)S(1)} %convolution_convert_fusion), channel_id=1, source_target_pairs={{0,1},{1,0},{2,3},{3,2},{4,5},{5,4},{6,7},{7,6},{8,9},{9,8},{10,11... | collective-permute-start | bytes 1769480 | tf_op jit(solution)/shard_map/ppermute | solution.py:54
  133.0 1.6 %collective-permute-done.10 = bf16[96,3072]{1,0:T(8,128)(2,1)S(1)} collective-permute-done((bf16[96,3072]{1,0:T(8,128)(2,1)S(1)}, bf16[96,3072]{1,0:T(8,128)(2,1)S(1)}, u32[]{:S(2)}, u32[]{:S(2)}) %collective-permute-start.10) | collective-permute-done | bytes 589856 | tf_op jit(solution)/shard_map/ppermute | solution.py:54
  134.6 1.9 %fusion.27 = (bf16[96,3072]{1,0:T(8,128)(2,1)S(1)}, f32[96,3072]{1,0:T(8,128)}) fusion(bf16[96,3072]{1,0:T(8,128)(2,1)S(1)} %collective-permute-done.10, bf16[96,384]{1,0:T(8,128)(2,1)S(1)} %bitcast.144, bf16[3072,384]{1,0:T(8,128)(2,1)S(1)} %bitcast.129), kind=kOutput, calls=%fused_computation.64 | convolution fusion | flops 227377152 | bytes 4792320 | tf_op jit(solution)/shard_map/dot_general | solution.py:149
  136.6 3.3 %collective-permute-start.13 = (bf16[24,3072]{1,0:T(8,128)(2,1)S(1)}, bf16[24,3072]{1,0:T(8,128)(2,1)S(1)}, u32[]{:S(2)}, u32[]{:S(2)}) collective-permute-start(bf16[24,3072]{1,0:T(8,128)(2,1)S(1)} %get-tuple-element.11), channel_id=1, source_target_pairs={{0,2},{1,3},{2,4},{3,5},{4,6},{5,7},{6,0},{7,1},{8,10},{9,11},{10,... | collective-permute-start | bytes 442376 | tf_op jit(solution)/shard_map/ppermute | solution.py:44
  139.9 4.3 %collective-permute-start.12 = (bf16[24,3072]{1,0:T(8,128)(2,1)S(1)}, bf16[24,3072]{1,0:T(8,128)(2,1)S(1)}, u32[]{:S(2)}, u32[]{:S(2)}) collective-permute-start(bf16[24,3072]{1,0:T(8,128)(2,1)S(1)} %get-tuple-element.12), channel_id=1, source_target_pairs={{0,4},{1,5},{2,6},{3,7},{4,0},{5,1},{6,2},{7,3},{8,12},{9,13},{10,... | collective-permute-start | bytes 442376 | tf_op jit(solution)/shard_map/ppermute | solution.py:44
  144.2 1.9 %collective-permute-start.11 = (bf16[24,3072]{1,0:T(8,128)(2,1)S(1)}, bf16[24,3072]{1,0:T(8,128)(2,1)S(1)}, u32[]{:S(2)}, u32[]{:S(2)}) collective-permute-start(bf16[24,3072]{1,0:T(8,128)(2,1)S(1)} %get-tuple-element.10), channel_id=1, source_target_pairs={{0,6},{1,7},{2,0},{3,1},{4,2},{5,3},{6,4},{7,5},{8,14},{9,15},{10,... | collective-permute-start | bytes 442376 | tf_op jit(solution)/shard_map/ppermute | solution.py:44
  146.3 6.9 %collective-permute-done.12 = bf16[24,3072]{1,0:T(8,128)(2,1)S(1)} collective-permute-done((bf16[24,3072]{1,0:T(8,128)(2,1)S(1)}, bf16[24,3072]{1,0:T(8,128)(2,1)S(1)}, u32[]{:S(2)}, u32[]{:S(2)}) %collective-permute-start.12) | collective-permute-done | bytes 147488 | tf_op jit(solution)/shard_map/ppermute | solution.py:44
  153.2 3.0 %collective-permute-done.11 = bf16[24,3072]{1,0:T(8,128)(2,1)S(1)} collective-permute-done((bf16[24,3072]{1,0:T(8,128)(2,1)S(1)}, bf16[24,3072]{1,0:T(8,128)(2,1)S(1)}, u32[]{:S(2)}, u32[]{:S(2)}) %collective-permute-start.11) | collective-permute-done | bytes 147488 | tf_op jit(solution)/shard_map/ppermute | solution.py:44
  156.2 1.8 %fusion.17 = (bf16[1,24,3072]{2,1,0:T(8,128)(2,1)}, bf16[24,3072]{1,0:T(8,128)(2,1)}) fusion(bf16[1,24,3072]{2,1,0:T(8,128)(2,1)S(1)} %copy-done.3, bf16[1,24,3072]{2,1,0:T(8,128)(2,1)S(1)} %copy-done.1, f32[]{:T(128)S(6)} %mul_shard_map.3, f32[]{:T(128)S(6)} %sub.50, bf16[24,3072]{1,0:T(8,128)(2,1)S(1)} %collective-permute-done.13, ...), kind=kLoop, calls=%fused_computation.41 | loop fusion | flops 1179648 | bytes 1339400 | tf_op jit(solution)/shard_map/broadcast_in_dim | solution.py:170
  (56 shorter events, 2.2 us)
Async XLA Ops:
  0.6 9.9 %copy-start = (bf16[3,64,384]{2,1,0:T(8,128)(2,1)S(1)}, bf16[3,64,384]{2,1,0:T(8,128)(2,1)}, u32[]{:S(2)}) copy-start(bf16[3,64,384]{2,1,0:T(8,128)(2,1)} %param.14) | copy-start | bytes 442372
  0.6 9.8 %copy-start.8 = (bf16[64,48]{0,1:T(8,128)(2,1)S(1)}, bf16[64,48]{0,1:T(8,128)(2,1)}, u32[]{:S(2)}) copy-start(bf16[64,48]{0,1:T(8,128)(2,1)} %param.17) | copy-start | bytes 18436
  0.7 9.8 %copy-start.5 = (bf16[384,64]{0,1:T(8,128)(2,1)S(1)}, bf16[384,64]{0,1:T(8,128)(2,1)}, u32[]{:S(2)}) copy-start(bf16[384,64]{0,1:T(8,128)(2,1)} %param.16) | copy-start | bytes 147460
  0.7 9.7 %copy-start.7 = (bf16[384,48]{0,1:T(8,128)(2,1)S(1)}, bf16[384,48]{0,1:T(8,128)(2,1)}, u32[]{:S(2)}) copy-start(bf16[384,48]{0,1:T(8,128)(2,1)} %param.15) | copy-start | bytes 110596
  0.7 9.9 %copy-start.6 = (bf16[3,48,64]{2,1,0:T(8,128)(2,1)S(1)}, bf16[3,48,64]{2,1,0:T(8,128)(2,1)}, u32[]{:S(2)}) copy-start(bf16[3,48,64]{2,1,0:T(8,128)(2,1)} %param.13) | copy-start | bytes 55300
  0.7 9.9 %copy-start.4 = (bf16[3,48,384]{2,1,0:T(8,128)(2,1)S(1)}, bf16[3,48,384]{2,1,0:T(8,128)(2,1)}, u32[]{:S(2)}) copy-start(bf16[3,48,384]{2,1,0:T(8,128)(2,1)} %param.12) | copy-start | bytes 331780
  6.1 42.8 %all-to-all-start = ((bf16[4,24,768]{2,1,0:T(8,128)(2,1)}), bf16[4,24,768]{2,1,0:T(8,128)(2,1)S(1)}, u32[]{:S(2)}, u32[]{:S(2)}) async-start(bf16[4,24,768]{2,1,0:T(8,128)(2,1)} %reshape.92), calls=%async_computation | async-start | bytes 294912 | tf_op jit(solution)/shard_map/all_to_all | solution.py:58
  39.8 38.4 %collective-permute-start.4 = (bf16[4,48,384]{2,1,0:T(8,128)(2,1)S(1)}, bf16[4,48,384]{2,1,0:T(8,128)(2,1)S(1)}, u32[]{:S(2)}, u32[]{:S(2)}) collective-permute-start(bf16[4,48,384]{2,1,0:T(8,128)(2,1)S(1)} %get-tuple-element.13), channel_id=1, source_target_pairs={{0,32},{8,40},{16,48},{24,56},{32,64},{40,72},{48,80},{56,88},{64,... | collective-permute-start | bytes 442376 | tf_op jit(solution)/shard_map/ppermute | solution.py:37
  43.1 35.2 %collective-permute-start.5 = (bf16[4,48,384]{2,1,0:T(8,128)(2,1)S(1)}, bf16[4,48,384]{2,1,0:T(8,128)(2,1)S(1)}, u32[]{:S(2)}, u32[]{:S(2)}) collective-permute-start(bf16[4,48,384]{2,1,0:T(8,128)(2,1)S(1)} %get-tuple-element.13), channel_id=1, source_target_pairs={{0,64},{8,72},{16,80},{24,88},{32,96},{40,104},{48,112},{56,120},{... | collective-permute-start | bytes 442376 | tf_op jit(solution)/shard_map/ppermute | solution.py:37
  50.3 32.4 %all-to-all-start.1 = ((bf16[4,4,3,48,384]{4,3,1,2,0:T(8,128)(2,1)}), bf16[4,4,3,48,384]{4,3,1,2,0:T(8,128)(2,1)S(1)}, u32[]{:S(2)}, u32[]{:S(2)}) async-start(bf16[4,4,3,48,384]{4,3,1,2,0:T(8,128)(2,1)} %broadcast_in_dim.48), calls=%async_computation.1 | async-start | bytes 3538944 | tf_op jit(solution)/shard_map/all_to_all | solution.py:58
  54.7 10.5 %collective-permute-start.2 = (bf16[4,24,768]{2,1,0:T(8,128)(2,1)S(1)}, bf16[4,24,768]{2,1,0:T(8,128)(2,1)S(1)}, u32[]{:S(2)}, u32[]{:S(2)}) collective-permute-start(bf16[4,24,768]{2,1,0:T(8,128)(2,1)S(1)} %broadcast_add_fusion), channel_id=1, source_target_pairs={{0,6},{1,7},{2,0},{3,1},{4,2},{5,3},{6,4},{7,5},{8,14},{9,15},{10,... | collective-permute-start | bytes 442376 | tf_op jit(solution)/shard_map/ppermute | solution.py:44
  58.1 11.1 %collective-permute-start.1 = (bf16[4,24,768]{2,1,0:T(8,128)(2,1)S(1)}, bf16[4,24,768]{2,1,0:T(8,128)(2,1)S(1)}, u32[]{:S(2)}, u32[]{:S(2)}) collective-permute-start(bf16[4,24,768]{2,1,0:T(8,128)(2,1)S(1)} %broadcast_add_fusion), channel_id=1, source_target_pairs={{0,4},{1,5},{2,6},{3,7},{4,0},{5,1},{6,2},{7,3},{8,12},{9,13},{10,... | collective-permute-start | bytes 442376 | tf_op jit(solution)/shard_map/ppermute | solution.py:44
  60.9 10.2 %collective-permute-start = (bf16[4,24,768]{2,1,0:T(8,128)(2,1)S(1)}, bf16[4,24,768]{2,1,0:T(8,128)(2,1)S(1)}, u32[]{:S(2)}, u32[]{:S(2)}) collective-permute-start(bf16[4,24,768]{2,1,0:T(8,128)(2,1)S(1)} %broadcast_add_fusion), channel_id=1, source_target_pairs={{0,2},{1,3},{2,4},{3,5},{4,6},{5,7},{6,0},{7,1},{8,10},{9,11},{10,... | collective-permute-start | bytes 442376 | tf_op jit(solution)/shard_map/ppermute | solution.py:44
  65.2 13.1 %collective-permute-start.6 = (bf16[4,48,384]{2,1,0:T(8,128)(2,1)S(1)}, bf16[4,48,384]{2,1,0:T(8,128)(2,1)S(1)}, u32[]{:S(2)}, u32[]{:S(2)}) collective-permute-start(bf16[4,48,384]{2,1,0:T(8,128)(2,1)S(1)} %get-tuple-element.13), channel_id=1, source_target_pairs={{0,96},{8,104},{16,112},{24,120},{32,0},{40,8},{48,16},{56,24},{64... | collective-permute-start | bytes 442376 | tf_op jit(solution)/shard_map/ppermute | solution.py:37
  71.2 10.3 %collective-permute-start.3 = (bf16[4,4,24,768]{3,2,0,1:T(8,128)(2,1)S(1)}, bf16[4,4,24,768]{3,2,0,1:T(8,128)(2,1)S(1)}, u32[]{:S(2)}, u32[]{:S(2)}) collective-permute-start(bf16[4,4,24,768]{3,2,0,1:T(8,128)(2,1)S(1)} %get-tuple-element.16), channel_id=1, source_target_pairs={{0,1},{1,0},{2,3},{3,2},{4,5},{5,4},{6,7},{7,6},{8,9},{9,8},{10,11... | collective-permute-start | bytes 1769480 | tf_op jit(solution)/shard_map/ppermute | solution.py:54
  78.4 22.2 %collective-permute-start.7 = (bf16[4,4,48,384]{3,2,1,0:T(8,128)(2,1)S(1)}, bf16[4,4,48,384]{3,2,1,0:T(8,128)(2,1)}, u32[]{:S(2)}, u32[]{:S(2)}) collective-permute-start(bf16[4,4,48,384]{3,2,1,0:T(8,128)(2,1)S(1)} %bitcast_dynamic-update-slice_fusion.4), channel_id=1, source_target_pairs={{0,8},{8,16},{16,24},{24,0},{32,40},{40,48},{48,56},{56,32},{64,72... | collective-permute-start | bytes 1769480 | tf_op jit(solution)/shard_map/ppermute | solution.py:37
  83.0 1.3 copy-start.2
  88.0 36.9 %all-to-all-start.2 = ((bf16[4,3,192,384]{3,2,1,0:T(8,128)(2,1)}), bf16[4,3,192,384]{3,2,1,0:T(8,128)(2,1)}, u32[]{:S(2)}, u32[]{:S(2)}) async-start(bf16[4,3,192,384]{3,2,1,0:T(8,128)(2,1)} %pad_maximum_fusion), calls=%async_computation.2 | async-start | bytes 3538944 | tf_op jit(solution)/shard_map/all_to_all | solution.py:58
  93.6 16.3 %collective-permute-start.8 = (bf16[4,4,48,384]{3,2,1,0:T(8,128)(2,1)S(1)}, bf16[4,4,48,384]{3,2,1,0:T(8,128)(2,1)}, u32[]{:S(2)}, u32[]{:S(2)}) collective-permute-start(bf16[4,4,48,384]{3,2,1,0:T(8,128)(2,1)S(1)} %bitcast_dynamic-update-slice_fusion.4), channel_id=1, source_target_pairs={{0,16},{8,24},{16,0},{24,8},{32,48},{40,56},{48,32},{56,40},{64,80... | collective-permute-start | bytes 1769480 | tf_op jit(solution)/shard_map/ppermute | solution.py:37
  96.2 28.7 %collective-permute-start.9 = (bf16[4,4,48,384]{3,2,1,0:T(8,128)(2,1)S(1)}, bf16[4,4,48,384]{3,2,1,0:T(8,128)(2,1)S(1)}, u32[]{:S(2)}, u32[]{:S(2)}) collective-permute-start(bf16[4,4,48,384]{3,2,1,0:T(8,128)(2,1)S(1)} %bitcast_dynamic-update-slice_fusion.4), channel_id=1, source_target_pairs={{0,24},{8,0},{16,8},{24,16},{32,56},{40,32},{48,40},{56,48},{64,88... | collective-permute-start | bytes 1769480 | tf_op jit(solution)/shard_map/ppermute | solution.py:37
  130.6 4.0 %collective-permute-start.10 = (bf16[96,3072]{1,0:T(8,128)(2,1)S(1)}, bf16[96,3072]{1,0:T(8,128)(2,1)S(1)}, u32[]{:S(2)}, u32[]{:S(2)}) collective-permute-start(bf16[96,3072]{1,0:T(8,128)(2,1)S(1)} %convolution_convert_fusion), channel_id=1, source_target_pairs={{0,1},{1,0},{2,3},{3,2},{4,5},{5,4},{6,7},{7,6},{8,9},{9,8},{10,11... | collective-permute-start | bytes 1769480 | tf_op jit(solution)/shard_map/ppermute | solution.py:54
  134.6 21.5 %copy-start.1 = (bf16[1,24,3072]{2,1,0:T(8,128)(2,1)S(1)}, bf16[1,24,3072]{2,1,0:T(8,128)(2,1)}, u32[]{:S(2)}) copy-start(bf16[1,24,3072]{2,1,0:T(8,128)(2,1)} %param.10) | copy-start | bytes 442372
  134.6 21.5 %copy-start.3 = (bf16[1,24,3072]{2,1,0:T(8,128)(2,1)S(1)}, bf16[1,24,3072]{2,1,0:T(8,128)(2,1)}, u32[]{:S(2)}) copy-start(bf16[1,24,3072]{2,1,0:T(8,128)(2,1)} %param.11) | copy-start | bytes 442372
  136.6 9.7 %collective-permute-start.13 = (bf16[24,3072]{1,0:T(8,128)(2,1)S(1)}, bf16[24,3072]{1,0:T(8,128)(2,1)S(1)}, u32[]{:S(2)}, u32[]{:S(2)}) collective-permute-start(bf16[24,3072]{1,0:T(8,128)(2,1)S(1)} %get-tuple-element.11), channel_id=1, source_target_pairs={{0,2},{1,3},{2,4},{3,5},{4,6},{5,7},{6,0},{7,1},{8,10},{9,11},{10,... | collective-permute-start | bytes 442376 | tf_op jit(solution)/shard_map/ppermute | solution.py:44
  139.9 13.3 %collective-permute-start.12 = (bf16[24,3072]{1,0:T(8,128)(2,1)S(1)}, bf16[24,3072]{1,0:T(8,128)(2,1)S(1)}, u32[]{:S(2)}, u32[]{:S(2)}) collective-permute-start(bf16[24,3072]{1,0:T(8,128)(2,1)S(1)} %get-tuple-element.12), channel_id=1, source_target_pairs={{0,4},{1,5},{2,6},{3,7},{4,0},{5,1},{6,2},{7,3},{8,12},{9,13},{10,... | collective-permute-start | bytes 442376 | tf_op jit(solution)/shard_map/ppermute | solution.py:44
  144.2 11.9 %collective-permute-start.11 = (bf16[24,3072]{1,0:T(8,128)(2,1)S(1)}, bf16[24,3072]{1,0:T(8,128)(2,1)S(1)}, u32[]{:S(2)}, u32[]{:S(2)}) collective-permute-start(bf16[24,3072]{1,0:T(8,128)(2,1)S(1)} %get-tuple-element.10), channel_id=1, source_target_pairs={{0,6},{1,7},{2,0},{3,1},{4,2},{5,3},{6,4},{7,5},{8,14},{9,15},{10,... | collective-permute-start | bytes 442376 | tf_op jit(solution)/shard_map/ppermute | solution.py:44

commit v3 on v2

v3 whole, which is shorter than its diff:
```python
import jax
import jax.numpy as jnp
from jax import lax
from jax.experimental import pallas as pl
from jax.experimental.pallas import tpu as pltpu
from jax.sharding import PartitionSpec as P

HEAD_DIM = 128
NSTEP = 16
QUAD = 4


EPSILON = 1e-06
SHIFT_FACTOR = 5.0
NOISE_LEVEL = 0.7


def plan_sigma(position):
    ramp = 1.0 - position / NSTEP
    return SHIFT_FACTOR * ramp / (1.0 + (SHIFT_FACTOR - 1.0) * ramp)


def fsdp_index(z, y, x):
    return ((z % QUAD) * QUAD + y % QUAD) * QUAD + x % QUAD


Y_GROUPS = [[fsdp_index(z, y, x) for y in range(QUAD)] for z in range(QUAD) for x in range(QUAD)]
Z_GROUPS = [[fsdp_index(z, y, x) for z in range(QUAD)] for y in range(QUAD) for x in range(QUAD)]
X_GROUPS = [[fsdp_index(z, y, x) for x in range(QUAD)] for z in range(QUAD) for y in range(QUAD)]


def shift_fsdp(value, dy=0, dx=0):
    pairs = [
        (fsdp_index(z, y, x), fsdp_index(z, y + dy, x + dx))
        for z in range(QUAD)
        for y in range(QUAD)
        for x in range(QUAD)
    ]
    return lax.ppermute(value, "fsdp", pairs)


def shift_run(value, dz):
    pairs = [
        (z * 2 + core, ((z + dz) % QUAD) * 2 + core) for z in range(QUAD) for core in range(2)
    ]
    return lax.ppermute(value, "sp", pairs)


def other_core(value):
    return lax.ppermute(value, "sp", [(i, i ^ 1) for i in range(2 * QUAD)])


def exchange(value, axis, groups):
    return lax.all_to_all(value, axis, 0, 0, axis_index_groups=groups, tiled=True)


def gather(value, axis, groups):
    return exchange(jnp.broadcast_to(value[None], (QUAD,) + value.shape), axis, groups)


def prepare_kernel(
    step_ref,
    latents_ref,
    modulation_ref,
    base_qkv_ref,
    down_qkv_ref,
    up_qkv_ref,
    base_out_ref,
    down_out_ref,
    up_out_ref,
    slices_ref,
    merged_ref,
):
    for p in range(3):
        lowrank = jnp.dot(down_qkv_ref[p], up_qkv_ref[p], preferred_element_type=jnp.float32)
        merged_ref[p] = (base_qkv_ref[p].astype(jnp.float32) + lowrank).astype(jnp.bfloat16)
    lowrank = jnp.dot(up_out_ref[...], down_out_ref[...], preferred_element_type=jnp.float32)
    merged_ref[3] = (base_out_ref[...].astype(jnp.float32) + lowrank).astype(jnp.bfloat16)

    step = step_ref[0]
    shift = modulation_ref[0, pl.ds(step, 1), :]
    scale = modulation_ref[1, pl.ds(step, 1), :]
    latent = latents_ref[...].astype(jnp.float32)
    mean_square = jnp.mean(latent * latent, axis=-1, keepdims=True)
    normed = latent * lax.rsqrt(mean_square + EPSILON) * (1.0 + scale) + shift
    slab = normed.shape[1] // QUAD
    piece = slab // QUAD
    x = lax.axis_index("fsdp") % QUAD
    for y in range(QUAD):
        blocks = [
            normed[:, z * slab + y * piece : z * slab + (y + 1) * piece] for z in range(QUAD)
        ]
        mine = jnp.concatenate(blocks, axis=1)
        for step in range(1, QUAD):
            cut = step * piece // QUAD
            turned = [part for block in blocks for part in (block[:, cut:], block[:, :cut])]
            mine = jnp.where(x == step, jnp.concatenate(turned, axis=1), mine)
        slices_ref[y] = mine.astype(jnp.bfloat16)


def attend_kernel(own_ref, first_ref, second_ref, third_ref, weights_ref, mine_ref, theirs_ref):
    projected = own_ref[...].astype(jnp.float32)
    for ref in (first_ref, second_ref, third_ref):
        projected = projected + ref[...].astype(jnp.float32)
    projected = projected.astype(jnp.bfloat16)
    columns = projected.shape[1] // 3
    heads = []
    for h in range(columns // HEAD_DIM):
        queries, keys, values = (
            projected[:, p * columns + h * HEAD_DIM : p * columns + (h + 1) * HEAD_DIM]
            for p in range(3)
        )
        scores = lax.dot_general(
            queries, keys, (((1,), (1,)), ((), ())), preferred_element_type=jnp.float32
        ) * (1.0 / HEAD_DIM**0.5)
        weights = jnp.exp(scores - jnp.max(scores, axis=-1, keepdims=True))
        weights = weights / jnp.sum(weights, axis=-1, keepdims=True)
        heads.append(
            jnp.dot(
                weights.astype(jnp.bfloat16), values, preferred_element_type=jnp.float32
            ).astype(jnp.bfloat16)
        )
    attended = jnp.concatenate(heads, axis=1)
    half, slab = mine_ref.shape[0], weights_ref.shape[1]
    for k in range(QUAD):
        out = lax.dot_general(
            attended, weights_ref[k], (((1,), (1,)), ((), ())), preferred_element_type=jnp.float32
        ).astype(jnp.bfloat16)
        mine_ref[:, k * slab : (k + 1) * slab] = out[:half]
        theirs_ref[:, k * slab : (k + 1) * slab] = out[half:]


def finish_kernel(
    step_ref,
    own_ref,
    first_ref,
    second_ref,
    third_ref,
    latents_ref,
    noise_ref,
    modulation_ref,
    velocity_ref,
    next_ref,
):
    step = step_ref[0]
    block_out = own_ref[...].astype(jnp.float32)
    for ref in (first_ref, second_ref, third_ref):
        block_out = block_out + ref[...].astype(jnp.float32)
    piece = block_out.shape[1] // QUAD**3
    starts = [
        ((x * QUAD + y) * QUAD + z) * piece
        for z in range(QUAD)
        for y in range(QUAD)
        for x in range(QUAD)
    ]
    ordered = jnp.concatenate([block_out[:, i : i + piece] for i in starts], axis=1)
    gate = modulation_ref[2, pl.ds(step, 1), :]
    velocity = ((1.0 + gate) * ordered).astype(jnp.bfloat16)
    velocity_ref[...] = velocity
    position = jnp.full((1, 1), step, jnp.int32).astype(jnp.float32)
    step_size = plan_sigma(position + 1.0) - plan_sigma(position)
    next_ref[...] = (
        latents_ref[...].astype(jnp.float32)
        + step_size * velocity.astype(jnp.float32)
        + NOISE_LEVEL * jnp.sqrt(-step_size) * noise_ref[...].astype(jnp.float32)
    ).astype(jnp.bfloat16)


def whole(shape):
    return pl.BlockSpec(shape, lambda i: (0,) * len(shape))


def call(kernel, out_shapes, *operands, scalars=0, mebibytes=40):
    smem = pl.BlockSpec(memory_space=pltpu.SMEM)
    return pl.pallas_call(
        kernel,
        grid=(1,),
        out_shape=out_shapes,
        in_specs=[smem] * scalars + [whole(x.shape) for x in operands[scalars:]],
        out_specs=jax.tree.map(lambda x: whole(x.shape), out_shapes),
        compiler_params=pltpu.CompilerParams(vmem_limit_bytes=mebibytes * 2**20),
    )(*operands)


def per_device(
    latents,
    step_noise,
    base_qkv,
    down_qkv,
    up_query_key_value,
    base_out,
    down_out,
    up_out,
    modulation,
    timestep,
):
    y = lax.axis_index("fsdp") // QUAD % QUAD
    rows, width = latents.shape[1:]
    part = base_qkv.shape[1]
    head_cols = base_qkv.shape[2]
    seq_len = rows * 2 * QUAD
    slab = width // QUAD

    slices, merged = call(
        prepare_kernel,
        (
            jax.ShapeDtypeStruct((QUAD, rows, slab), jnp.bfloat16),
            jax.ShapeDtypeStruct((4, part, head_cols), jnp.bfloat16),
        ),
        timestep,
        latents[0],
        modulation.transpose(1, 0, 2),
        base_qkv,
        down_qkv,
        up_query_key_value,
        base_out.T,
        down_out.T,
        up_out.T,
        scalars=1,
        mebibytes=60,
    )

    mine = exchange(slices, "fsdp", Y_GROUPS)
    mine = jnp.concatenate([mine, mine], axis=0)
    mine = lax.rev(lax.dynamic_slice_in_dim(mine, y + 1, QUAD, 0), (0,))

    held = lax.all_gather(merged, "fsdp", axis_index_groups=Z_GROUPS, axis=0)

    moving = held[:, :3]
    blocks = [moving] + [shift_fsdp(moving, dx=-k) for k in range(1, QUAD)]
    weights = jnp.stack(blocks, axis=1).transpose(0, 1, 3, 2, 4).reshape(slab, 3 * head_cols)

    out_rows = gather(held[:, 3].reshape(QUAD * part, head_cols), "fsdp", Y_GROUPS)
    out_rows = gather(out_rows.reshape(slab, head_cols), "fsdp", X_GROUPS)
    mine, held = lax.optimization_barrier((mine, held))

    run = jnp.stack([mine] + [shift_run(mine, k) for k in range(1, QUAD)], axis=1)
    tokens = jnp.stack([run, other_core(run)], axis=1).reshape(QUAD * seq_len, slab)

    partial = jnp.dot(tokens, weights, preferred_element_type=jnp.float32).astype(jnp.bfloat16)
    partial = partial.reshape(QUAD, seq_len, 3 * head_cols)
    parts = [partial[0]] + [shift_fsdp(partial[k], dy=-k) for k in (2, 1, 3)]

    half = seq_len // 2
    ours, theirs = call(
        attend_kernel,
        (jax.ShapeDtypeStruct((half, width), jnp.bfloat16),) * 2,
        *parts,
        out_rows,
    )
    pair = ours.astype(jnp.float32) + other_core(theirs).astype(jnp.float32)
    pair = pair.astype(jnp.bfloat16).reshape(QUAD, rows, width)
    returned = [pair[0]] + [shift_run(pair[k], -k) for k in (2, 1, 3)]
    velocity, next_rows = call(
        finish_kernel,
        (jax.ShapeDtypeStruct((rows, width), jnp.bfloat16),) * 2,
        timestep,
        *returned,
        latents[0],
        step_noise[0],
        modulation.transpose(1, 0, 2),
        scalars=1,
    )
    return (velocity[None], next_rows[None])


def solution(mesh):
    in_specs = (
        P("fsdp", "sp", None),
        P("fsdp", "sp", None),
        P(None, "fsdp", "sp"),
        P(None, "fsdp", None),
        P(None, None, "sp"),
        P("sp", "fsdp"),
        P("sp", None),
        P(None, "fsdp"),
        P(),
        P("fsdp"),
    )
    out_specs = (P("fsdp", "sp", None), P("fsdp", "sp", None))
    return jax.shard_map(
        per_device, mesh=mesh, in_specs=in_specs, out_specs=out_specs, check_vma=False
    )
```

time: 159 us -> 142 us (0.89)
  the two profiles are of different devices: /device:TPU:43 before, /device:TPU:11 now
where the time goes in v3:
time: 142 us; the launch traced here: 141 us
  starting transfers between devices  61.9 us (44%)
  blocking collectives  31.7 us (22%)
  waiting for transfers between devices  27 us (19%)
  local copies, waits for them, and re-layouts  8.63 us (6%)
  Pallas kernels  5.04 us (4%)
  other arithmetic  3.85 us (3%)
  matrix products  1.7 us (1%)
  between operations  1.56 us (1%)
    all_gather x1, blocking collectives, per_device(): held = lax.all_gather(merged, 'fsdp', axis_index_groups=Z_GROUPS, axis=0)  31.7 us
    ppermute x6, starting transfers between devices, shift_fsdp(): return lax.ppermute(value, 'fsdp', pairs)  18.3 us
    ppermute x6, starting transfers between devices, shift_run(): return lax.ppermute(value, 'sp', pairs)  18 us
    ppermute x6, waiting for transfers between devices, shift_fsdp(): return lax.ppermute(value, 'fsdp', pairs)  15.8 us
    ppermute x2, starting transfers between devices, other_core(): return lax.ppermute(value, 'sp', [(i, i ^ 1) for i in range(2 * QUAD)])  12.8 us
    all_to_all x3, starting transfers between devices, exchange(): lax.all_to_all(value, axis, 0, 0, axis_index_groups=groups, tiled=True)  12.7 us
    ppermute x6, waiting for transfers between devices, shift_run(): return lax.ppermute(value, 'sp', pairs)  9.63 us
    pallas_call x3, Pallas kernels, call(): pl.pallas_call(kernel, grid=(1,), out_shape=out_shapes, in_specs=[smem] *...  5.04 us
  transfers between devices with their start and end apart: 17, of which 6 were waited for; matrix products, arithmetic and copies ran while one was open for 7% of the time, Pallas kernels for 0%

profile of v3, /device:TPU:11, one launch (start us, length us, event | category | flops | bytes accessed | tf_op | source)
XLA Modules:
  0.0 141.4 jit_solution(2722463854329426394)
XLA Ops:
  1.3 2.3 %shard_map.113 = (bf16[4,24,768]{2,1,0:T(8,128)(2,1)}, bf16[4,48,384]{2,1,0:T(8,128)(2,1)}) custom-call(s32[1]{0:T(128)S(6)} %copy.20.step_ref, bf16[24,3072]{1,0:T(8,128)(2,1)} %bitcast.33, f32[3,16,3072]{2,1,0:T(8,128)} %bitcast.31, bf16[3,48,384]{2,1,0:T(8,128)(2,1)} %base_qkv_ref.1, bf16[3,48,64]{2,1,0:T(8,128)(2,1)} %down_qkv_ref.1, ...), custom_call_target="tpu_custom_call" | custom-call | tf_op jit(solution)/shard_map/pallas_call | solution.py:175
  3.6 4.4 %all-to-all-start = ((bf16[4,24,768]{2,1,0:T(8,128)(2,1)}), bf16[4,24,768]{2,1,0:T(8,128)(2,1)S(1)}, u32[]{:S(2)}, u32[]{:S(2)}) async-start(bf16[4,24,768]{2,1,0:T(8,128)(2,1)} %get-tuple-element.9), calls=%async_computation | async-start | bytes 294912 | tf_op jit(solution)/shard_map/all_to_all | solution.py:54
  7.9 31.7 %all-gather = bf16[16,48,384]{2,1,0:T(8,128)(2,1)S(1)} all-gather(bf16[4,48,384]{2,1,0:T(8,128)(2,1)} %get-tuple-element.10), channel_id=2, replica_groups={{0,128,256,384},{8,136,264,392},{16,144,272,400},{24,152,280,408},{32,1..., dimensions={0}, use_global_device_ids=true | all-gather | bytes 737280 | tf_op jit(solution)/shard_map/all_gather | solution.py:227
  39.6 0.0 all-to-all-done
  39.6 0.1 fusion
  39.7 4.8 %collective-permute-start.2 = (bf16[4,24,768]{2,1,0:T(8,128)(2,1)S(1)}, bf16[4,24,768]{2,1,0:T(8,128)(2,1)S(1)}, u32[]{:S(2)}, u32[]{:S(2)}) collective-permute-start(bf16[4,24,768]{2,1,0:T(8,128)(2,1)S(1)} %rev.3), channel_id=1, source_target_pairs={{0,6},{1,7},{2,0},{3,1},{4,2},{5,3},{6,4},{7,5},{8,14},{9,15},{10,... | collective-permute-start | bytes 442376 | tf_op jit(solution)/shard_map/ppermute | solution.py:46
  44.5 1.9 %collective-permute-start.1 = (bf16[4,24,768]{2,1,0:T(8,128)(2,1)S(1)}, bf16[4,24,768]{2,1,0:T(8,128)(2,1)S(1)}, u32[]{:S(2)}, u32[]{:S(2)}) collective-permute-start(bf16[4,24,768]{2,1,0:T(8,128)(2,1)S(1)} %rev.3), channel_id=1, source_target_pairs={{0,4},{1,5},{2,6},{3,7},{4,0},{5,1},{6,2},{7,3},{8,12},{9,13},{10,... | collective-permute-start | bytes 442376 | tf_op jit(solution)/shard_map/ppermute | solution.py:46
  46.4 2.2 %collective-permute-start = (bf16[4,24,768]{2,1,0:T(8,128)(2,1)S(1)}, bf16[4,24,768]{2,1,0:T(8,128)(2,1)S(1)}, u32[]{:S(2)}, u32[]{:S(2)}) collective-permute-start(bf16[4,24,768]{2,1,0:T(8,128)(2,1)S(1)} %rev.3), channel_id=1, source_target_pairs={{0,2},{1,3},{2,4},{3,5},{4,6},{5,7},{6,0},{7,1},{8,10},{9,11},{10,... | collective-permute-start | bytes 442376 | tf_op jit(solution)/shard_map/ppermute | solution.py:46
  48.6 0.8 slice_bitcast_fusion
  49.5 4.1 %collective-permute-start.5 = (bf16[4,3,48,384]{3,2,1,0:T(8,128)(2,1)}, bf16[4,3,48,384]{3,2,1,0:T(8,128)(2,1)}, u32[]{:S(2)}, u32[]{:S(2)}) collective-permute-start(bf16[4,3,48,384]{3,2,1,0:T(8,128)(2,1)} %get-tuple-element.25), channel_id=1, source_target_pairs={{0,16},{8,24},{16,0},{24,8},{32,48},{40,56},{48,32},{56,40},{64,80... | collective-permute-start | bytes 1327112 | tf_op jit(solution)/shard_map/ppermute | solution.py:39
  53.5 3.1 %collective-permute-start.4 = (bf16[4,3,48,384]{3,2,1,0:T(8,128)(2,1)}, bf16[4,3,48,384]{3,2,1,0:T(8,128)(2,1)}, u32[]{:S(2)}, u32[]{:S(2)}) collective-permute-start(bf16[4,3,48,384]{3,2,1,0:T(8,128)(2,1)} %get-tuple-element.25), channel_id=1, source_target_pairs={{0,24},{8,0},{16,8},{24,16},{32,56},{40,32},{48,40},{56,48},{64,88... | collective-permute-start | bytes 1327112 | tf_op jit(solution)/shard_map/ppermute | solution.py:39
  56.7 0.9 broadcast_in_dim.21
  57.5 4.2 %all-to-all-start.1 = ((bf16[4,192,384]{2,1,0:T(8,128)(2,1)}), bf16[4,192,384]{2,1,0:T(8,128)(2,1)S(1)}, u32[]{:S(2)}, u32[]{:S(2)}) async-start(bf16[4,192,384]{2,1,0:T(8,128)(2,1)} %broadcast_in_dim.21), calls=%async_computation.1 | async-start | bytes 1179648 | tf_op jit(solution)/shard_map/all_to_all | solution.py:54
  61.8 2.2 %collective-permute-start.6 = (bf16[4,3,48,384]{3,2,1,0:T(8,128)(2,1)}, bf16[4,3,48,384]{3,2,1,0:T(8,128)(2,1)}, u32[]{:S(2)}, u32[]{:S(2)}) collective-permute-start(bf16[4,3,48,384]{3,2,1,0:T(8,128)(2,1)} %get-tuple-element.25), channel_id=1, source_target_pairs={{0,8},{8,16},{16,24},{24,0},{32,40},{40,48},{48,56},{56,32},{64,72... | collective-permute-start | bytes 1327112 | tf_op jit(solution)/shard_map/ppermute | solution.py:39
  64.0 0.9 fusion.1
  64.9 8.6 %collective-permute-start.3 = (bf16[4,4,24,768]{3,2,0,1:T(8,128)(2,1)}, bf16[4,4,24,768]{3,2,0,1:T(8,128)(2,1)}, u32[]{:S(2)}, u32[]{:S(2)}) collective-permute-start(bf16[4,4,24,768]{3,2,0,1:T(8,128)(2,1)} %get-tuple-element.27), channel_id=1, source_target_pairs={{0,1},{1,0},{2,3},{3,2},{4,5},{5,4},{6,7},{7,6},{8,9},{9,8},{10,11... | collective-permute-start | bytes 1769480 | tf_op jit(solution)/shard_map/ppermute | solution.py:50
  73.5 1.6 %broadcast_in_dim.23 = bf16[4,768,384]{2,1,0:T(8,128)(2,1)} broadcast(bf16[768,384]{1,0:T(8,128)(2,1)S(1)} %bitcast.39), dimensions={1,2} | broadcast | bytes 2949120 | tf_op jit(solution)/shard_map/broadcast_in_dim | solution.py:58
  75.2 4.1 %all-to-all-start.2 = ((bf16[4,768,384]{2,1,0:T(8,128)(2,1)}), bf16[4,768,384]{2,1,0:T(8,128)(2,1)S(1)}, u32[]{:S(2)}, u32[]{:S(2)}) async-start(bf16[4,768,384]{2,1,0:T(8,128)(2,1)} %broadcast_in_dim.23), calls=%async_computation.2 | async-start | bytes 4718592 | tf_op jit(solution)/shard_map/all_to_all | solution.py:54
  79.2 1.6 %maximum_bitcast_fusion = bf16[4,4,48,3,384]{4,2,3,0,1:T(8,128)(2,1)S(1)} fusion(bf16[4,1,3,48,384]{4,3,2,0,1:T(8,128)(2,1)} %bitcast.16, bf16[4,1,3,48,384]{4,3,2,0,1:T(8,128)(2,1)} %bitcast.15, bf16[4,1,3,48,384]{4,3,2,0,1:T(8,128)(2,1)} %bitcast.14, bf16[4,1,3,48,384]{4,3,2,0,1:T(8,128)(2,1)S(1)} %get-tuple-element.24), kind=kLoop, calls=%fused_computation.1 | loop fusion | flops 2654208 | bytes 3538944 | tf_op jit(solution)/shard_map/transpose | solution.py:231
  80.8 1.1 copy.18
  81.9 0.3 copy.19
  82.2 1.2 pad_maximum_fusion
  83.4 0.1 copy.17
  83.5 1.7 %convolution_convert_fusion = bf16[768,1152]{1,0:T(8,128)(2,1)S(1)} fusion(bf16[768,768]{1,0:T(8,128)(2,1)S(1)} %bitcast.41, bf16[768,1152]{1,0:T(8,128)(2,1)S(1)} %bitcast.40), kind=kOutput, calls=%fused_computation | convolution fusion | flops 1359839232 | bytes 4718592 | tf_op jit(solution)/shard_map/dot_general | solution.py:240
  85.2 0.1 fusion.2
  85.4 3.1 %collective-permute-start.9 = (bf16[192,1152]{1,0:T(8,128)(2,1)S(1)}, bf16[192,1152]{1,0:T(8,128)(2,1)S(1)}, u32[]{:S(2)}, u32[]{:S(2)}) collective-permute-start(bf16[192,1152]{1,0:T(8,128)(2,1)S(1)} %get-tuple-element.16), channel_id=1, source_target_pairs={{0,32},{8,40},{16,48},{24,56},{32,64},{40,72},{48,80},{56,88},{64,... | collective-permute-start | bytes 1327112 | tf_op jit(solution)/shard_map/ppermute | solution.py:39
  88.5 2.2 %collective-permute-start.8 = (bf16[192,1152]{1,0:T(8,128)(2,1)S(1)}, bf16[192,1152]{1,0:T(8,128)(2,1)S(1)}, u32[]{:S(2)}, u32[]{:S(2)}) collective-permute-start(bf16[192,1152]{1,0:T(8,128)(2,1)S(1)} %get-tuple-element.17), channel_id=1, source_target_pairs={{0,96},{8,104},{16,112},{24,120},{32,0},{40,8},{48,16},{56,24},{64... | collective-permute-start | bytes 1327112 | tf_op jit(solution)/shard_map/ppermute | solution.py:39
  90.7 3.7 %collective-permute-start.7 = (bf16[192,1152]{1,0:T(8,128)(2,1)S(1)}, bf16[192,1152]{1,0:T(8,128)(2,1)S(1)}, u32[]{:S(2)}, u32[]{:S(2)}) collective-permute-start(bf16[192,1152]{1,0:T(8,128)(2,1)S(1)} %get-tuple-element.18), channel_id=1, source_target_pairs={{0,64},{8,72},{16,80},{24,88},{32,96},{40,104},{48,112},{56,120},{... | collective-permute-start | bytes 1327112 | tf_op jit(solution)/shard_map/ppermute | solution.py:39
  94.4 4.1 %collective-permute-done.9.third_ref = bf16[192,1152]{1,0:T(8,128)(2,1)S(1)} collective-permute-done((bf16[192,1152]{1,0:T(8,128)(2,1)S(1)}, bf16[192,1152]{1,0:T(8,128)(2,1)S(1)}, u32[]{:S(2)}, u32[]{:S(2)}) %collective-permute-start.9) | collective-permute-done | bytes 442400 | tf_op jit(solution)/shard_map/ppermute | solution.py:39
  98.5 3.1 %collective-permute-done.8.second_ref = bf16[192,1152]{1,0:T(8,128)(2,1)S(1)} collective-permute-done((bf16[192,1152]{1,0:T(8,128)(2,1)S(1)}, bf16[192,1152]{1,0:T(8,128)(2,1)S(1)}, u32[]{:S(2)}, u32[]{:S(2)}) %collective-permute-start.8) | collective-permute-done | bytes 442400 | tf_op jit(solution)/shard_map/ppermute | solution.py:39
  101.6 0.8 copy-done.2
  102.4 8.5 %collective-permute-done.7.first_ref = bf16[192,1152]{1,0:T(8,128)(2,1)S(1)} collective-permute-done((bf16[192,1152]{1,0:T(8,128)(2,1)S(1)}, bf16[192,1152]{1,0:T(8,128)(2,1)S(1)}, u32[]{:S(2)}, u32[]{:S(2)}) %collective-permute-start.7) | collective-permute-done | bytes 442400 | tf_op jit(solution)/shard_map/ppermute | solution.py:39
  110.9 0.8 copy-done.4
  111.7 1.0 copy-done.3
  112.7 1.0 copy-done.5
  113.7 1.8 %shard_map.114 = (bf16[96,3072]{1,0:T(8,128)(2,1)S(1)}, bf16[96,3072]{1,0:T(8,128)(2,1)S(1)}) custom-call(bf16[192,1152]{1,0:T(8,128)(2,1)S(1)} %get-tuple-element.19.own_ref, bf16[192,1152]{1,0:T(8,128)(2,1)S(1)} %copy-done.5, bf16[192,1152]{1,0:T(8,128)(2,1)S(1)} %copy-done.3, bf16[192,1152]{1,0:T(8,128)(2,1)S(1)} %collective-permute-done.9.third_ref, ...), custom_call_target="tpu_custom_call" | custom-call | tf_op jit(solution)/shard_map/pallas_call | solution.py:175
  115.5 0.0 copy-start
  115.5 0.0 copy-start.1
  115.5 0.0 copy-start.6
  115.5 4.2 %collective-permute-start.10 = (bf16[96,3072]{1,0:T(8,128)(2,1)S(1)}, bf16[96,3072]{1,0:T(8,128)(2,1)S(1)}, u32[]{:S(2)}, u32[]{:S(2)}) collective-permute-start(bf16[96,3072]{1,0:T(8,128)(2,1)S(1)} %get-tuple-element.13), channel_id=1, source_target_pairs={{0,1},{1,0},{2,3},{3,2},{4,5},{5,4},{6,7},{7,6},{8,9},{9,8},{10,11... | collective-permute-start | bytes 1769480 | tf_op jit(solution)/shard_map/ppermute | solution.py:50
  119.7 1.6 %collective-permute-done.10 = bf16[96,3072]{1,0:T(8,128)(2,1)S(1)} collective-permute-done((bf16[96,3072]{1,0:T(8,128)(2,1)S(1)}, bf16[96,3072]{1,0:T(8,128)(2,1)S(1)}, u32[]{:S(2)}, u32[]{:S(2)}) %collective-permute-start.10) | collective-permute-done | bytes 589856 | tf_op jit(solution)/shard_map/ppermute | solution.py:50
  121.3 0.1 add_convert_fusion
  121.5 4.2 %collective-permute-start.13 = (bf16[24,3072]{1,0:T(8,128)(2,1)S(1)}, bf16[24,3072]{1,0:T(8,128)(2,1)S(1)}, u32[]{:S(2)}, u32[]{:S(2)}) collective-permute-start(bf16[24,3072]{1,0:T(8,128)(2,1)S(1)} %get-tuple-element.20), channel_id=1, source_target_pairs={{0,2},{1,3},{2,4},{3,5},{4,6},{5,7},{6,0},{7,1},{8,10},{9,11},{10,... | collective-permute-start | bytes 442376 | tf_op jit(solution)/shard_map/ppermute | solution.py:46
  125.7 2.9 %collective-permute-start.12 = (bf16[24,3072]{1,0:T(8,128)(2,1)S(1)}, bf16[24,3072]{1,0:T(8,128)(2,1)S(1)}, u32[]{:S(2)}, u32[]{:S(2)}) collective-permute-start(bf16[24,3072]{1,0:T(8,128)(2,1)S(1)} %get-tuple-element.21), channel_id=1, source_target_pairs={{0,6},{1,7},{2,0},{3,1},{4,2},{5,3},{6,4},{7,5},{8,14},{9,15},{10,... | collective-permute-start | bytes 442376 | tf_op jit(solution)/shard_map/ppermute | solution.py:46
  128.6 2.1 %collective-permute-start.11 = (bf16[24,3072]{1,0:T(8,128)(2,1)S(1)}, bf16[24,3072]{1,0:T(8,128)(2,1)S(1)}, u32[]{:S(2)}, u32[]{:S(2)}) collective-permute-start(bf16[24,3072]{1,0:T(8,128)(2,1)S(1)} %get-tuple-element.22), channel_id=1, source_target_pairs={{0,4},{1,5},{2,6},{3,7},{4,0},{5,1},{6,2},{7,3},{8,12},{9,13},{10,... | collective-permute-start | bytes 442376 | tf_op jit(solution)/shard_map/ppermute | solution.py:46
  130.7 3.2 %collective-permute-done.12.second_ref = bf16[24,3072]{1,0:T(8,128)(2,1)S(1)} collective-permute-done((bf16[24,3072]{1,0:T(8,128)(2,1)S(1)}, bf16[24,3072]{1,0:T(8,128)(2,1)S(1)}, u32[]{:S(2)}, u32[]{:S(2)}) %collective-permute-start.12) | collective-permute-done | bytes 147488 | tf_op jit(solution)/shard_map/ppermute | solution.py:46
  134.0 6.4 %collective-permute-done.11.first_ref = bf16[24,3072]{1,0:T(8,128)(2,1)S(1)} collective-permute-done((bf16[24,3072]{1,0:T(8,128)(2,1)S(1)}, bf16[24,3072]{1,0:T(8,128)(2,1)S(1)}, u32[]{:S(2)}, u32[]{:S(2)}) %collective-permute-start.11) | collective-permute-done | bytes 147488 | tf_op jit(solution)/shard_map/ppermute | solution.py:46
  140.4 1.0 shard_map.115
  (20 shorter events, 0.1 us)
Async XLA Ops:
  3.6 36.0 %all-to-all-start = ((bf16[4,24,768]{2,1,0:T(8,128)(2,1)}), bf16[4,24,768]{2,1,0:T(8,128)(2,1)S(1)}, u32[]{:S(2)}, u32[]{:S(2)}) async-start(bf16[4,24,768]{2,1,0:T(8,128)(2,1)} %get-tuple-element.9), calls=%async_computation | async-start | bytes 294912 | tf_op jit(solution)/shard_map/all_to_all | solution.py:54
  39.7 22.1 %collective-permute-start.2 = (bf16[4,24,768]{2,1,0:T(8,128)(2,1)S(1)}, bf16[4,24,768]{2,1,0:T(8,128)(2,1)S(1)}, u32[]{:S(2)}, u32[]{:S(2)}) collective-permute-start(bf16[4,24,768]{2,1,0:T(8,128)(2,1)S(1)} %rev.3), channel_id=1, source_target_pairs={{0,6},{1,7},{2,0},{3,1},{4,2},{5,3},{6,4},{7,5},{8,14},{9,15},{10,... | collective-permute-start | bytes 442376 | tf_op jit(solution)/shard_map/ppermute | solution.py:46
  44.5 19.5 %collective-permute-start.1 = (bf16[4,24,768]{2,1,0:T(8,128)(2,1)S(1)}, bf16[4,24,768]{2,1,0:T(8,128)(2,1)S(1)}, u32[]{:S(2)}, u32[]{:S(2)}) collective-permute-start(bf16[4,24,768]{2,1,0:T(8,128)(2,1)S(1)} %rev.3), channel_id=1, source_target_pairs={{0,4},{1,5},{2,6},{3,7},{4,0},{5,1},{6,2},{7,3},{8,12},{9,13},{10,... | collective-permute-start | bytes 442376 | tf_op jit(solution)/shard_map/ppermute | solution.py:46
  46.4 17.5 %collective-permute-start = (bf16[4,24,768]{2,1,0:T(8,128)(2,1)S(1)}, bf16[4,24,768]{2,1,0:T(8,128)(2,1)S(1)}, u32[]{:S(2)}, u32[]{:S(2)}) collective-permute-start(bf16[4,24,768]{2,1,0:T(8,128)(2,1)S(1)} %rev.3), channel_id=1, source_target_pairs={{0,2},{1,3},{2,4},{3,5},{4,6},{5,7},{6,0},{7,1},{8,10},{9,11},{10,... | collective-permute-start | bytes 442376 | tf_op jit(solution)/shard_map/ppermute | solution.py:46
  49.5 29.8 %collective-permute-start.5 = (bf16[4,3,48,384]{3,2,1,0:T(8,128)(2,1)}, bf16[4,3,48,384]{3,2,1,0:T(8,128)(2,1)}, u32[]{:S(2)}, u32[]{:S(2)}) collective-permute-start(bf16[4,3,48,384]{3,2,1,0:T(8,128)(2,1)} %get-tuple-element.25), channel_id=1, source_target_pairs={{0,16},{8,24},{16,0},{24,8},{32,48},{40,56},{48,32},{56,40},{64,80... | collective-permute-start | bytes 1327112 | tf_op jit(solution)/shard_map/ppermute | solution.py:39
  53.5 25.7 %collective-permute-start.4 = (bf16[4,3,48,384]{3,2,1,0:T(8,128)(2,1)}, bf16[4,3,48,384]{3,2,1,0:T(8,128)(2,1)}, u32[]{:S(2)}, u32[]{:S(2)}) collective-permute-start(bf16[4,3,48,384]{3,2,1,0:T(8,128)(2,1)} %get-tuple-element.25), channel_id=1, source_target_pairs={{0,24},{8,0},{16,8},{24,16},{32,56},{40,32},{48,40},{56,48},{64,88... | collective-permute-start | bytes 1327112 | tf_op jit(solution)/shard_map/ppermute | solution.py:39
  57.5 16.0 %all-to-all-start.1 = ((bf16[4,192,384]{2,1,0:T(8,128)(2,1)}), bf16[4,192,384]{2,1,0:T(8,128)(2,1)S(1)}, u32[]{:S(2)}, u32[]{:S(2)}) async-start(bf16[4,192,384]{2,1,0:T(8,128)(2,1)} %broadcast_in_dim.21), calls=%async_computation.1 | async-start | bytes 1179648 | tf_op jit(solution)/shard_map/all_to_all | solution.py:54
  61.8 17.5 %collective-permute-start.6 = (bf16[4,3,48,384]{3,2,1,0:T(8,128)(2,1)}, bf16[4,3,48,384]{3,2,1,0:T(8,128)(2,1)}, u32[]{:S(2)}, u32[]{:S(2)}) collective-permute-start(bf16[4,3,48,384]{3,2,1,0:T(8,128)(2,1)} %get-tuple-element.25), channel_id=1, source_target_pairs={{0,8},{8,16},{16,24},{24,0},{32,40},{40,48},{48,56},{56,32},{64,72... | collective-permute-start | bytes 1327112 | tf_op jit(solution)/shard_map/ppermute | solution.py:39
  64.9 17.3 %collective-permute-start.3 = (bf16[4,4,24,768]{3,2,0,1:T(8,128)(2,1)}, bf16[4,4,24,768]{3,2,0,1:T(8,128)(2,1)}, u32[]{:S(2)}, u32[]{:S(2)}) collective-permute-start(bf16[4,4,24,768]{3,2,0,1:T(8,128)(2,1)} %get-tuple-element.27), channel_id=1, source_target_pairs={{0,1},{1,0},{2,3},{3,2},{4,5},{5,4},{6,7},{7,6},{8,9},{9,8},{10,11... | collective-permute-start | bytes 1769480 | tf_op jit(solution)/shard_map/ppermute | solution.py:50
  75.2 36.5 %all-to-all-start.2 = ((bf16[4,768,384]{2,1,0:T(8,128)(2,1)}), bf16[4,768,384]{2,1,0:T(8,128)(2,1)S(1)}, u32[]{:S(2)}, u32[]{:S(2)}) async-start(bf16[4,768,384]{2,1,0:T(8,128)(2,1)} %broadcast_in_dim.23), calls=%async_computation.2 | async-start | bytes 4718592 | tf_op jit(solution)/shard_map/all_to_all | solution.py:54
  85.4 13.1 %collective-permute-start.9 = (bf16[192,1152]{1,0:T(8,128)(2,1)S(1)}, bf16[192,1152]{1,0:T(8,128)(2,1)S(1)}, u32[]{:S(2)}, u32[]{:S(2)}) collective-permute-start(bf16[192,1152]{1,0:T(8,128)(2,1)S(1)} %get-tuple-element.16), channel_id=1, source_target_pairs={{0,32},{8,40},{16,48},{24,56},{32,64},{40,72},{48,80},{56,88},{64,... | collective-permute-start | bytes 1327112 | tf_op jit(solution)/shard_map/ppermute | solution.py:39
  88.5 13.1 %collective-permute-start.8 = (bf16[192,1152]{1,0:T(8,128)(2,1)S(1)}, bf16[192,1152]{1,0:T(8,128)(2,1)S(1)}, u32[]{:S(2)}, u32[]{:S(2)}) collective-permute-start(bf16[192,1152]{1,0:T(8,128)(2,1)S(1)} %get-tuple-element.17), channel_id=1, source_target_pairs={{0,96},{8,104},{16,112},{24,120},{32,0},{40,8},{48,16},{56,24},{64... | collective-permute-start | bytes 1327112 | tf_op jit(solution)/shard_map/ppermute | solution.py:39
  90.7 20.2 %collective-permute-start.7 = (bf16[192,1152]{1,0:T(8,128)(2,1)S(1)}, bf16[192,1152]{1,0:T(8,128)(2,1)S(1)}, u32[]{:S(2)}, u32[]{:S(2)}) collective-permute-start(bf16[192,1152]{1,0:T(8,128)(2,1)S(1)} %get-tuple-element.18), channel_id=1, source_target_pairs={{0,64},{8,72},{16,80},{24,88},{32,96},{40,104},{48,112},{56,120},{... | collective-permute-start | bytes 1327112 | tf_op jit(solution)/shard_map/ppermute | solution.py:39
  101.6 0.8 copy-start.2
  110.9 0.8 copy-start.4
  111.7 1.0 copy-start.3
  112.7 1.0 copy-start.5
  115.5 24.9 %copy-start = (f32[16,3,3072]{2,0,1:T(8,128)S(1)}, f32[16,3,3072]{2,0,1:T(8,128)}, u32[]{:S(2)}) copy-start(f32[16,3,3072]{2,0,1:T(8,128)} %param.18) | copy-start | bytes 1769476
  115.5 24.9 %copy-start.1 = (bf16[1,24,3072]{2,1,0:T(8,128)(2,1)S(1)}, bf16[1,24,3072]{2,1,0:T(8,128)(2,1)}, u32[]{:S(2)}) copy-start(bf16[1,24,3072]{2,1,0:T(8,128)(2,1)} %param.10) | copy-start | bytes 442372
  115.5 24.9 %copy-start.6 = (bf16[1,24,3072]{2,1,0:T(8,128)(2,1)S(1)}, bf16[1,24,3072]{2,1,0:T(8,128)(2,1)}, u32[]{:S(2)}) copy-start(bf16[1,24,3072]{2,1,0:T(8,128)(2,1)} %param.11) | copy-start | bytes 442372
  115.5 5.8 %collective-permute-start.10 = (bf16[96,3072]{1,0:T(8,128)(2,1)S(1)}, bf16[96,3072]{1,0:T(8,128)(2,1)S(1)}, u32[]{:S(2)}, u32[]{:S(2)}) collective-permute-start(bf16[96,3072]{1,0:T(8,128)(2,1)S(1)} %get-tuple-element.13), channel_id=1, source_target_pairs={{0,1},{1,0},{2,3},{3,2},{4,5},{5,4},{6,7},{7,6},{8,9},{9,8},{10,11... | collective-permute-start | bytes 1769480 | tf_op jit(solution)/shard_map/ppermute | solution.py:50
  121.5 9.2 %collective-permute-start.13 = (bf16[24,3072]{1,0:T(8,128)(2,1)S(1)}, bf16[24,3072]{1,0:T(8,128)(2,1)S(1)}, u32[]{:S(2)}, u32[]{:S(2)}) collective-permute-start(bf16[24,3072]{1,0:T(8,128)(2,1)S(1)} %get-tuple-element.20), channel_id=1, source_target_pairs={{0,2},{1,3},{2,4},{3,5},{4,6},{5,7},{6,0},{7,1},{8,10},{9,11},{10,... | collective-permute-start | bytes 442376 | tf_op jit(solution)/shard_map/ppermute | solution.py:46
  125.7 8.3 %collective-permute-start.12 = (bf16[24,3072]{1,0:T(8,128)(2,1)S(1)}, bf16[24,3072]{1,0:T(8,128)(2,1)S(1)}, u32[]{:S(2)}, u32[]{:S(2)}) collective-permute-start(bf16[24,3072]{1,0:T(8,128)(2,1)S(1)} %get-tuple-element.21), channel_id=1, source_target_pairs={{0,6},{1,7},{2,0},{3,1},{4,2},{5,3},{6,4},{7,5},{8,14},{9,15},{10,... | collective-permute-start | bytes 442376 | tf_op jit(solution)/shard_map/ppermute | solution.py:46
  128.6 11.7 %collective-permute-start.11 = (bf16[24,3072]{1,0:T(8,128)(2,1)S(1)}, bf16[24,3072]{1,0:T(8,128)(2,1)S(1)}, u32[]{:S(2)}, u32[]{:S(2)}) collective-permute-start(bf16[24,3072]{1,0:T(8,128)(2,1)S(1)} %get-tuple-element.22), channel_id=1, source_target_pairs={{0,4},{1,5},{2,6},{3,7},{4,0},{5,1},{6,2},{7,3},{8,12},{9,13},{10,... | collective-permute-start | bytes 442376 | tf_op jit(solution)/shard_map/ppermute | solution.py:46

commit v4 on v3

--- a/solution.py
+++ b/solution.py
@@ -70,6 +70,7 @@
     up_out_ref,
     slices_ref,
     merged_ref,
+    by_x,
 ):
     for p in range(3):
         lowrank = jnp.dot(down_qkv_ref[p], up_qkv_ref[p], preferred_element_type=jnp.float32)
@@ -85,24 +86,18 @@
     normed = latent * lax.rsqrt(mean_square + EPSILON) * (1.0 + scale) + shift
     slab = normed.shape[1] // QUAD
     piece = slab // QUAD
-    x = lax.axis_index("fsdp") % QUAD
+    x_here = lax.axis_index("fsdp") % QUAD
+    part = piece // QUAD
     for y in range(QUAD):
-        blocks = [
-            normed[:, z * slab + y * piece : z * slab + (y + 1) * piece] for z in range(QUAD)
-        ]
-        mine = jnp.concatenate(blocks, axis=1)
-        for step in range(1, QUAD):
-            cut = step * piece // QUAD
-            turned = [part for block in blocks for part in (block[:, cut:], block[:, :cut])]
-            mine = jnp.where(x == step, jnp.concatenate(turned, axis=1), mine)
-        slices_ref[y] = mine.astype(jnp.bfloat16)
-
-
-def attend_kernel(own_ref, first_ref, second_ref, third_ref, weights_ref, mine_ref, theirs_ref):
-    projected = own_ref[...].astype(jnp.float32)
-    for ref in (first_ref, second_ref, third_ref):
-        projected = projected + ref[...].astype(jnp.float32)
-    projected = projected.astype(jnp.bfloat16)
+        for x in range(QUAD):
+            starts = [z * slab + y * piece + x * part for z in range(QUAD)]
+            by_x[x] = jnp.concatenate([normed[:, i : i + part] for i in starts], axis=1)
+        turned = [by_x[lax.rem(x_here + k, QUAD)] for k in range(QUAD)]
+        slices_ref[y] = jnp.concatenate(turned, axis=1).astype(jnp.bfloat16)
+
+
+def attend_kernel(projected_ref, weights_ref, mine_ref, theirs_ref):
+    projected = projected_ref[...]
     columns = projected.shape[1] // 3
     heads = []
     for h in range(columns // HEAD_DIM):
@@ -166,11 +161,27 @@
     ).astype(jnp.bfloat16)
 
 
+def hold_kernel(*refs):
+    pass
+
+
+def hold(values, earlier):
+    held = pl.BlockSpec(memory_space=pl.ANY)
+    return pl.pallas_call(
+        hold_kernel,
+        out_shape=[jax.ShapeDtypeStruct(x.shape, x.dtype) for x in values],
+        in_specs=[held] * (len(values) + 1),
+        out_specs=[held] * len(values),
+        input_output_aliases={i: i for i in range(len(values))},
+        cost_estimate=pl.CostEstimate(flops=4 * 10**9, bytes_accessed=0, transcendentals=0),
+    )(*values, earlier)
+
+
 def whole(shape):
     return pl.BlockSpec(shape, lambda i: (0,) * len(shape))
 
 
-def call(kernel, out_shapes, *operands, scalars=0, mebibytes=40):
+def call(kernel, out_shapes, *operands, scalars=0, mebibytes=40, scratch=()):
     smem = pl.BlockSpec(memory_space=pltpu.SMEM)
     return pl.pallas_call(
         kernel,
@@ -178,6 +189,7 @@
         out_shape=out_shapes,
         in_specs=[smem] * scalars + [whole(x.shape) for x in operands[scalars:]],
         out_specs=jax.tree.map(lambda x: whole(x.shape), out_shapes),
+        scratch_shapes=scratch,
         compiler_params=pltpu.CompilerParams(vmem_limit_bytes=mebibytes * 2**20),
     )(*operands)
 
@@ -218,6 +230,7 @@
         up_out.T,
         scalars=1,
         mebibytes=60,
+        scratch=[pltpu.VMEM((QUAD, rows, slab // QUAD), jnp.float32)],
     )
 
     mine = exchange(slices, "fsdp", Y_GROUPS)
@@ -226,26 +239,33 @@
 
     held = lax.all_gather(merged, "fsdp", axis_index_groups=Z_GROUPS, axis=0)
 
-    moving = held[:, :3]
+    moving = held[:, :3].transpose(0, 2, 1, 3).reshape(QUAD * part, 3 * head_cols)
+    own_rows = held[:, 3].reshape(QUAD * part, head_cols)
+    mine, moving = lax.optimization_barrier((mine, moving))
     blocks = [moving] + [shift_fsdp(moving, dx=-k) for k in range(1, QUAD)]
-    weights = jnp.stack(blocks, axis=1).transpose(0, 1, 3, 2, 4).reshape(slab, 3 * head_cols)
-
-    out_rows = gather(held[:, 3].reshape(QUAD * part, head_cols), "fsdp", Y_GROUPS)
-    out_rows = gather(out_rows.reshape(slab, head_cols), "fsdp", X_GROUPS)
-    mine, held = lax.optimization_barrier((mine, held))
 
     run = jnp.stack([mine] + [shift_run(mine, k) for k in range(1, QUAD)], axis=1)
+
+    out_rows = gather(own_rows, "fsdp", Y_GROUPS).reshape(slab, head_cols)
+    copies = jnp.broadcast_to(out_rows[None], (QUAD, slab, head_cols))
+    blocks = blocks[:1] + list(hold(blocks[1:], out_rows))
+    out_rows = exchange(copies, "fsdp", X_GROUPS)
+    weights = jnp.concatenate(blocks, axis=0)
+
     tokens = jnp.stack([run, other_core(run)], axis=1).reshape(QUAD * seq_len, slab)
 
     partial = jnp.dot(tokens, weights, preferred_element_type=jnp.float32).astype(jnp.bfloat16)
     partial = partial.reshape(QUAD, seq_len, 3 * head_cols)
-    parts = [partial[0]] + [shift_fsdp(partial[k], dy=-k) for k in (2, 1, 3)]
+    projected = partial[0].astype(jnp.float32)
+    for k in (2, 1, 3):
+        projected = projected + shift_fsdp(partial[k], dy=-k).astype(jnp.float32)
+    projected = projected.astype(jnp.bfloat16)
 
     half = seq_len // 2
     ours, theirs = call(
         attend_kernel,
         (jax.ShapeDtypeStruct((half, width), jnp.bfloat16),) * 2,
-        *parts,
+        projected,
         out_rows,
     )
     pair = ours.astype(jnp.float32) + other_core(theirs).astype(jnp.float32)
@@ -260,6 +280,7 @@
         step_noise[0],
         modulation.transpose(1, 0, 2),
         scalars=1,
+        mebibytes=40,
     )
     return (velocity[None], next_rows[None])
 

time: 142 us -> 138 us (0.972)
  the two profiles are of different devices: /device:TPU:11 before, /device:TPU:27 now
where the time goes in v4:
time: 138 us; the launch traced here: 137 us
  starting transfers between devices  63 us (46%)
  blocking collectives  31.4 us (23%)
  waiting for transfers between devices  26.4 us (19%)
  Pallas kernels  5.2 us (4%)
  local copies, waits for them, and re-layouts  3.89 us (3%)
  matrix products  3.12 us (2%)
  other arithmetic  2.52 us (2%)
  between operations  1.56 us (1%)
    all_gather x1, blocking collectives, per_device(): held = lax.all_gather(merged, 'fsdp', axis_index_groups=Z_GROUPS, axis=0)  31.4 us
    ppermute x6, starting transfers between devices, shift_fsdp(): return lax.ppermute(value, 'fsdp', pairs)  18.6 us
    ppermute x6, starting transfers between devices, shift_run(): return lax.ppermute(value, 'sp', pairs)  18.5 us
    ppermute x6, waiting for transfers between devices, shift_fsdp(): return lax.ppermute(value, 'fsdp', pairs)  15.2 us
    ppermute x2, starting transfers between devices, other_core(): return lax.ppermute(value, 'sp', [(i, i ^ 1) for i in range(2 * QUAD)])  13.5 us
    all_to_all x3, starting transfers between devices, exchange(): lax.all_to_all(value, axis, 0, 0, axis_index_groups=groups, tiled=True)  12.4 us
    ppermute x6, waiting for transfers between devices, shift_run(): return lax.ppermute(value, 'sp', pairs)  9.63 us
    pallas_call x3, Pallas kernels, call(): pl.pallas_call(kernel, grid=(1,), out_shape=out_shapes, in_specs=[smem] *...  5.19 us
  transfers between devices with their start and end apart: 17, of which 7 were waited for; matrix products, arithmetic and copies ran while one was open for 7% of the time, Pallas kernels for 0%

profile of v4, /device:TPU:27, one launch (start us, length us, event | category | flops | bytes accessed | tf_op | source)
XLA Modules:
  0.0 137.1 jit_solution(1956569026079699560)
XLA Ops:
  1.3 2.5 %shard_map.113 = (bf16[4,24,768]{2,1,0:T(8,128)(2,1)}, bf16[4,48,384]{2,1,0:T(8,128)(2,1)}) custom-call(s32[1]{0:T(128)S(6)} %copy.25.step_ref, bf16[24,3072]{1,0:T(8,128)(2,1)} %bitcast.26, f32[3,16,3072]{2,1,0:T(8,128)} %bitcast.24, bf16[3,48,384]{2,1,0:T(8,128)(2,1)} %base_qkv_ref.1, bf16[3,48,64]{2,1,0:T(8,128)(2,1)} %down_qkv_ref.1, ...), custom_call_target="tpu_custom_call" | custom-call | tf_op jit(solution)/shard_map/pallas_call | solution.py:186
  3.7 4.1 %all-to-all-start = ((bf16[4,24,768]{2,1,0:T(8,128)(2,1)}), bf16[4,24,768]{2,1,0:T(8,128)(2,1)S(1)}, u32[]{:S(2)}, u32[]{:S(2)}) async-start(bf16[4,24,768]{2,1,0:T(8,128)(2,1)} %get-tuple-element.13), calls=%async_computation | async-start | bytes 294912 | tf_op jit(solution)/shard_map/all_to_all | solution.py:54
  7.9 31.4 %all-gather = bf16[16,48,384]{2,1,0:T(8,128)(2,1)S(1)} all-gather(bf16[4,48,384]{2,1,0:T(8,128)(2,1)} %get-tuple-element.14), channel_id=2, replica_groups={{0,128,256,384},{8,136,264,392},{16,144,272,400},{24,152,280,408},{32,1..., dimensions={0}, use_global_device_ids=true | all-gather | bytes 737280 | tf_op jit(solution)/shard_map/all_gather | solution.py:240
  39.3 0.2 copy.20
  39.5 0.8 copy.21
  40.3 0.0 all-to-all-done
  40.3 0.1 fusion.7
  40.4 5.1 %collective-permute-start.2 = (bf16[4,24,768]{2,1,0:T(8,128)(2,1)S(1)}, bf16[4,24,768]{2,1,0:T(8,128)(2,1)S(1)}, u32[]{:S(2)}, u32[]{:S(2)}) collective-permute-start(bf16[4,24,768]{2,1,0:T(8,128)(2,1)S(1)} %rev.3), channel_id=1, source_target_pairs={{0,6},{1,7},{2,0},{3,1},{4,2},{5,3},{6,4},{7,5},{8,14},{9,15},{10,... | collective-permute-start | bytes 442376 | tf_op jit(solution)/shard_map/ppermute | solution.py:46
  45.6 1.9 %collective-permute-start.1 = (bf16[4,24,768]{2,1,0:T(8,128)(2,1)S(1)}, bf16[4,24,768]{2,1,0:T(8,128)(2,1)S(1)}, u32[]{:S(2)}, u32[]{:S(2)}) collective-permute-start(bf16[4,24,768]{2,1,0:T(8,128)(2,1)S(1)} %rev.3), channel_id=1, source_target_pairs={{0,4},{1,5},{2,6},{3,7},{4,0},{5,1},{6,2},{7,3},{8,12},{9,13},{10,... | collective-permute-start | bytes 442376 | tf_op jit(solution)/shard_map/ppermute | solution.py:46
  47.5 2.2 %collective-permute-start = (bf16[4,24,768]{2,1,0:T(8,128)(2,1)S(1)}, bf16[4,24,768]{2,1,0:T(8,128)(2,1)S(1)}, u32[]{:S(2)}, u32[]{:S(2)}) collective-permute-start(bf16[4,24,768]{2,1,0:T(8,128)(2,1)S(1)} %rev.3), channel_id=1, source_target_pairs={{0,2},{1,3},{2,4},{3,5},{4,6},{5,7},{6,0},{7,1},{8,10},{9,11},{10,... | collective-permute-start | bytes 442376 | tf_op jit(solution)/shard_map/ppermute | solution.py:46
  49.7 0.9 broadcast_in_dim.19
  50.6 4.2 %all-to-all-start.1 = ((bf16[4,192,384]{2,1,0:T(8,128)(2,1)}), bf16[4,192,384]{2,1,0:T(8,128)(2,1)S(1)}, u32[]{:S(2)}, u32[]{:S(2)}) async-start(bf16[4,192,384]{2,1,0:T(8,128)(2,1)} %broadcast_in_dim.19), calls=%async_computation.1 | async-start | bytes 1179648 | tf_op jit(solution)/shard_map/all_to_all | solution.py:54
  54.8 3.1 %collective-permute-start.6 = (bf16[192,1152]{1,0:T(8,128)(2,1)}, bf16[192,1152]{1,0:T(8,128)(2,1)}, u32[]{:S(2)}, u32[]{:S(2)}) collective-permute-start(bf16[192,1152]{1,0:T(8,128)(2,1)} %bitcast.21), channel_id=1, source_target_pairs={{0,8},{8,16},{16,24},{24,0},{32,40},{40,48},{48,56},{56,32},{64,72... | collective-permute-start | bytes 1327112 | tf_op jit(solution)/shard_map/ppermute | solution.py:39
  58.0 3.0 %collective-permute-start.5 = (bf16[192,1152]{1,0:T(8,128)(2,1)}, bf16[192,1152]{1,0:T(8,128)(2,1)}, u32[]{:S(2)}, u32[]{:S(2)}) collective-permute-start(bf16[192,1152]{1,0:T(8,128)(2,1)} %bitcast.21), channel_id=1, source_target_pairs={{0,16},{8,24},{16,0},{24,8},{32,48},{40,56},{48,32},{56,40},{64,80... | collective-permute-start | bytes 1327112 | tf_op jit(solution)/shard_map/ppermute | solution.py:39
  61.0 3.8 %collective-permute-start.4 = (bf16[192,1152]{1,0:T(8,128)(2,1)}, bf16[192,1152]{1,0:T(8,128)(2,1)}, u32[]{:S(2)}, u32[]{:S(2)}) collective-permute-start(bf16[192,1152]{1,0:T(8,128)(2,1)} %bitcast.21), channel_id=1, source_target_pairs={{0,24},{8,0},{16,8},{24,16},{32,56},{40,32},{48,40},{56,48},{64,88... | collective-permute-start | bytes 1327112 | tf_op jit(solution)/shard_map/ppermute | solution.py:39
  64.8 0.0 collective-permute-done.1
  64.8 0.0 collective-permute-done
  64.8 0.9 fusion.9
  65.7 8.7 %collective-permute-start.3 = (bf16[4,4,24,768]{3,2,0,1:T(8,128)(2,1)}, bf16[4,4,24,768]{3,2,0,1:T(8,128)(2,1)}, u32[]{:S(2)}, u32[]{:S(2)}) collective-permute-start(bf16[4,4,24,768]{3,2,0,1:T(8,128)(2,1)} %get-tuple-element.32), channel_id=1, source_target_pairs={{0,1},{1,0},{2,3},{3,2},{4,5},{5,4},{6,7},{7,6},{8,9},{9,8},{10,11... | collective-permute-start | bytes 1769480 | tf_op jit(solution)/shard_map/ppermute | solution.py:50
  74.4 0.0 all-to-all-done.1
  74.4 1.6 %broadcast_in_dim.20 = bf16[4,768,384]{2,1,0:T(8,128)(2,1)} broadcast(bf16[768,384]{1,0:T(8,128)(2,1)S(1)} %bitcast.31), dimensions={1,2} | broadcast | bytes 2949120 | tf_op jit(solution)/shard_map/broadcast_in_dim | solution.py:250
  76.1 4.0 %all-to-all-start.2 = ((bf16[4,768,384]{2,1,0:T(8,128)(2,1)}), bf16[4,768,384]{2,1,0:T(8,128)(2,1)S(1)}, u32[]{:S(2)}, u32[]{:S(2)}) async-start(bf16[4,768,384]{2,1,0:T(8,128)(2,1)} %broadcast_in_dim.20), calls=%async_computation.2 | async-start | bytes 4718592 | tf_op jit(solution)/shard_map/all_to_all | solution.py:54
  80.1 0.0 collective-permute-done.6.refs_2_
  80.1 0.7 collective-permute-done.4.refs_0_
  80.7 1.2 pad_maximum_fusion
  81.9 0.1 copy.19
  82.0 3.1 %convolution_convert_fusion = bf16[768,1152]{1,0:T(8,128)(2,1)S(1)} fusion(bf16[768,768]{1,0:T(8,128)(2,1)S(1)} %bitcast.34, bf16[192,1152]{1,0:T(8,128)(2,1)} %get-tuple-element.19, bf16[192,1152]{1,0:T(8,128)(2,1)} %get-tuple-element.18, bf16[192,1152]{1,0:T(8,128)(2,1)} %get-tuple-element.17, bf16[192,1152]{1,0:T(8,128)(2,1)} %bitcast.21), kind=kOutput, calls=%fused_computation | convolution fusion | flops 1366917120 | bytes 4718592 | tf_op jit(solution)/shard_map/dot_general | solution.py:257
  85.1 0.1 fusion.10
  85.2 3.1 %collective-permute-start.7 = (bf16[192,1152]{1,0:T(8,128)(2,1)S(1)}, bf16[192,1152]{1,0:T(8,128)(2,1)S(1)}, u32[]{:S(2)}, u32[]{:S(2)}) collective-permute-start(bf16[192,1152]{1,0:T(8,128)(2,1)S(1)} %get-tuple-element.24), channel_id=1, source_target_pairs={{0,64},{8,72},{16,80},{24,88},{32,96},{40,104},{48,112},{56,120},{... | collective-permute-start | bytes 1327112 | tf_op jit(solution)/shard_map/ppermute | solution.py:39
  88.3 3.7 %collective-permute-start.9 = (bf16[192,1152]{1,0:T(8,128)(2,1)S(1)}, bf16[192,1152]{1,0:T(8,128)(2,1)S(1)}, u32[]{:S(2)}, u32[]{:S(2)}) collective-permute-start(bf16[192,1152]{1,0:T(8,128)(2,1)S(1)} %get-tuple-element.25), channel_id=1, source_target_pairs={{0,32},{8,40},{16,48},{24,56},{32,64},{40,72},{48,80},{56,88},{64,... | collective-permute-start | bytes 1327112 | tf_op jit(solution)/shard_map/ppermute | solution.py:39
  92.1 1.9 %collective-permute-start.8 = (bf16[192,1152]{1,0:T(8,128)(2,1)S(1)}, bf16[192,1152]{1,0:T(8,128)(2,1)S(1)}, u32[]{:S(2)}, u32[]{:S(2)}) collective-permute-start(bf16[192,1152]{1,0:T(8,128)(2,1)S(1)} %get-tuple-element.26), channel_id=1, source_target_pairs={{0,96},{8,104},{16,112},{24,120},{32,0},{40,8},{48,16},{56,24},{64... | collective-permute-start | bytes 1327112 | tf_op jit(solution)/shard_map/ppermute | solution.py:39
  94.0 2.8 %collective-permute-done.7 = bf16[192,1152]{1,0:T(8,128)(2,1)S(1)} collective-permute-done((bf16[192,1152]{1,0:T(8,128)(2,1)S(1)}, bf16[192,1152]{1,0:T(8,128)(2,1)S(1)}, u32[]{:S(2)}, u32[]{:S(2)}) %collective-permute-start.7) | collective-permute-done | bytes 442400 | tf_op jit(solution)/shard_map/ppermute | solution.py:39
  96.8 8.8 %collective-permute-done.9 = bf16[192,1152]{1,0:T(8,128)(2,1)S(1)} collective-permute-done((bf16[192,1152]{1,0:T(8,128)(2,1)S(1)}, bf16[192,1152]{1,0:T(8,128)(2,1)S(1)}, u32[]{:S(2)}, u32[]{:S(2)}) %collective-permute-start.9) | collective-permute-done | bytes 442400 | tf_op jit(solution)/shard_map/ppermute | solution.py:39
  105.6 3.0 %collective-permute-done.8 = bf16[192,1152]{1,0:T(8,128)(2,1)S(1)} collective-permute-done((bf16[192,1152]{1,0:T(8,128)(2,1)S(1)}, bf16[192,1152]{1,0:T(8,128)(2,1)S(1)}, u32[]{:S(2)}, u32[]{:S(2)}) %collective-permute-start.8) | collective-permute-done | bytes 442400 | tf_op jit(solution)/shard_map/ppermute | solution.py:39
  108.5 0.2 add_convert_fusion.1.projected_ref
  108.7 1.8 %shard_map.115 = (bf16[96,3072]{1,0:T(8,128)(2,1)S(1)}, bf16[96,3072]{1,0:T(8,128)(2,1)S(1)}) custom-call(bf16[192,1152]{1,0:T(8,128)(2,1)S(1)} %add_convert_fusion.1.projected_ref, bf16[4,768,384]{2,1,0:T(8,128)(2,1)S(1)} %all-to-all-done.2.weights_ref), custom_call_target="tpu_custom_call" | custom-call | tf_op jit(solution)/shard_map/pallas_call | solution.py:186
  110.5 0.0 copy-start
  110.5 0.0 copy-start.1
  110.5 0.0 copy-start.2
  110.5 4.8 %collective-permute-start.10 = (bf16[96,3072]{1,0:T(8,128)(2,1)S(1)}, bf16[96,3072]{1,0:T(8,128)(2,1)S(1)}, u32[]{:S(2)}, u32[]{:S(2)}) collective-permute-start(bf16[96,3072]{1,0:T(8,128)(2,1)S(1)} %get-tuple-element.21), channel_id=1, source_target_pairs={{0,1},{1,0},{2,3},{3,2},{4,5},{5,4},{6,7},{7,6},{8,9},{9,8},{10,11... | collective-permute-start | bytes 1769480 | tf_op jit(solution)/shard_map/ppermute | solution.py:50
  115.3 1.6 %collective-permute-done.10 = bf16[96,3072]{1,0:T(8,128)(2,1)S(1)} collective-permute-done((bf16[96,3072]{1,0:T(8,128)(2,1)S(1)}, bf16[96,3072]{1,0:T(8,128)(2,1)S(1)}, u32[]{:S(2)}, u32[]{:S(2)}) %collective-permute-start.10) | collective-permute-done | bytes 589856 | tf_op jit(solution)/shard_map/ppermute | solution.py:50
  116.9 0.1 add_convert_fusion
  117.1 4.0 %collective-permute-start.13 = (bf16[24,3072]{1,0:T(8,128)(2,1)S(1)}, bf16[24,3072]{1,0:T(8,128)(2,1)S(1)}, u32[]{:S(2)}, u32[]{:S(2)}) collective-permute-start(bf16[24,3072]{1,0:T(8,128)(2,1)S(1)} %get-tuple-element.27), channel_id=1, source_target_pairs={{0,2},{1,3},{2,4},{3,5},{4,6},{5,7},{6,0},{7,1},{8,10},{9,11},{10,... | collective-permute-start | bytes 442376 | tf_op jit(solution)/shard_map/ppermute | solution.py:46
  121.1 3.1 %collective-permute-start.12 = (bf16[24,3072]{1,0:T(8,128)(2,1)S(1)}, bf16[24,3072]{1,0:T(8,128)(2,1)S(1)}, u32[]{:S(2)}, u32[]{:S(2)}) collective-permute-start(bf16[24,3072]{1,0:T(8,128)(2,1)S(1)} %get-tuple-element.28), channel_id=1, source_target_pairs={{0,6},{1,7},{2,0},{3,1},{4,2},{5,3},{6,4},{7,5},{8,14},{9,15},{10,... | collective-permute-start | bytes 442376 | tf_op jit(solution)/shard_map/ppermute | solution.py:46
  124.2 2.2 %collective-permute-start.11 = (bf16[24,3072]{1,0:T(8,128)(2,1)S(1)}, bf16[24,3072]{1,0:T(8,128)(2,1)S(1)}, u32[]{:S(2)}, u32[]{:S(2)}) collective-permute-start(bf16[24,3072]{1,0:T(8,128)(2,1)S(1)} %get-tuple-element.29), channel_id=1, source_target_pairs={{0,4},{1,5},{2,6},{3,7},{4,0},{5,1},{6,2},{7,3},{8,12},{9,13},{10,... | collective-permute-start | bytes 442376 | tf_op jit(solution)/shard_map/ppermute | solution.py:46
  126.4 3.3 %collective-permute-done.12.second_ref = bf16[24,3072]{1,0:T(8,128)(2,1)S(1)} collective-permute-done((bf16[24,3072]{1,0:T(8,128)(2,1)S(1)}, bf16[24,3072]{1,0:T(8,128)(2,1)S(1)}, u32[]{:S(2)}, u32[]{:S(2)}) %collective-permute-start.12) | collective-permute-done | bytes 147488 | tf_op jit(solution)/shard_map/ppermute | solution.py:46
  129.7 6.4 %collective-permute-done.11.first_ref = bf16[24,3072]{1,0:T(8,128)(2,1)S(1)} collective-permute-done((bf16[24,3072]{1,0:T(8,128)(2,1)S(1)}, bf16[24,3072]{1,0:T(8,128)(2,1)S(1)}, u32[]{:S(2)}, u32[]{:S(2)}) %collective-permute-start.11) | collective-permute-done | bytes 147488 | tf_op jit(solution)/shard_map/ppermute | solution.py:46
  136.1 1.0 shard_map.116
  (15 shorter events, 0.1 us)
Async XLA Ops:
  3.7 36.6 %all-to-all-start = ((bf16[4,24,768]{2,1,0:T(8,128)(2,1)}), bf16[4,24,768]{2,1,0:T(8,128)(2,1)S(1)}, u32[]{:S(2)}, u32[]{:S(2)}) async-start(bf16[4,24,768]{2,1,0:T(8,128)(2,1)} %get-tuple-element.13), calls=%async_computation | async-start | bytes 294912 | tf_op jit(solution)/shard_map/all_to_all | solution.py:54
  40.4 20.6 %collective-permute-start.2 = (bf16[4,24,768]{2,1,0:T(8,128)(2,1)S(1)}, bf16[4,24,768]{2,1,0:T(8,128)(2,1)S(1)}, u32[]{:S(2)}, u32[]{:S(2)}) collective-permute-start(bf16[4,24,768]{2,1,0:T(8,128)(2,1)S(1)} %rev.3), channel_id=1, source_target_pairs={{0,6},{1,7},{2,0},{3,1},{4,2},{5,3},{6,4},{7,5},{8,14},{9,15},{10,... | collective-permute-start | bytes 442376 | tf_op jit(solution)/shard_map/ppermute | solution.py:46
  45.6 19.2 %collective-permute-start.1 = (bf16[4,24,768]{2,1,0:T(8,128)(2,1)S(1)}, bf16[4,24,768]{2,1,0:T(8,128)(2,1)S(1)}, u32[]{:S(2)}, u32[]{:S(2)}) collective-permute-start(bf16[4,24,768]{2,1,0:T(8,128)(2,1)S(1)} %rev.3), channel_id=1, source_target_pairs={{0,4},{1,5},{2,6},{3,7},{4,0},{5,1},{6,2},{7,3},{8,12},{9,13},{10,... | collective-permute-start | bytes 442376 | tf_op jit(solution)/shard_map/ppermute | solution.py:46
  47.5 17.3 %collective-permute-start = (bf16[4,24,768]{2,1,0:T(8,128)(2,1)S(1)}, bf16[4,24,768]{2,1,0:T(8,128)(2,1)S(1)}, u32[]{:S(2)}, u32[]{:S(2)}) collective-permute-start(bf16[4,24,768]{2,1,0:T(8,128)(2,1)S(1)} %rev.3), channel_id=1, source_target_pairs={{0,2},{1,3},{2,4},{3,5},{4,6},{5,7},{6,0},{7,1},{8,10},{9,11},{10,... | collective-permute-start | bytes 442376 | tf_op jit(solution)/shard_map/ppermute | solution.py:46
  50.6 23.8 %all-to-all-start.1 = ((bf16[4,192,384]{2,1,0:T(8,128)(2,1)}), bf16[4,192,384]{2,1,0:T(8,128)(2,1)S(1)}, u32[]{:S(2)}, u32[]{:S(2)}) async-start(bf16[4,192,384]{2,1,0:T(8,128)(2,1)} %broadcast_in_dim.19), calls=%async_computation.1 | async-start | bytes 1179648 | tf_op jit(solution)/shard_map/all_to_all | solution.py:54
  54.8 25.2 %collective-permute-start.6 = (bf16[192,1152]{1,0:T(8,128)(2,1)}, bf16[192,1152]{1,0:T(8,128)(2,1)}, u32[]{:S(2)}, u32[]{:S(2)}) collective-permute-start(bf16[192,1152]{1,0:T(8,128)(2,1)} %bitcast.21), channel_id=1, source_target_pairs={{0,8},{8,16},{16,24},{24,0},{32,40},{40,48},{48,56},{56,32},{64,72... | collective-permute-start | bytes 1327112 | tf_op jit(solution)/shard_map/ppermute | solution.py:39
  58.0 22.1 %collective-permute-start.5 = (bf16[192,1152]{1,0:T(8,128)(2,1)}, bf16[192,1152]{1,0:T(8,128)(2,1)}, u32[]{:S(2)}, u32[]{:S(2)}) collective-permute-start(bf16[192,1152]{1,0:T(8,128)(2,1)} %bitcast.21), channel_id=1, source_target_pairs={{0,16},{8,24},{16,0},{24,8},{32,48},{40,56},{48,32},{56,40},{64,80... | collective-permute-start | bytes 1327112 | tf_op jit(solution)/shard_map/ppermute | solution.py:39
  61.0 19.7 %collective-permute-start.4 = (bf16[192,1152]{1,0:T(8,128)(2,1)}, bf16[192,1152]{1,0:T(8,128)(2,1)}, u32[]{:S(2)}, u32[]{:S(2)}) collective-permute-start(bf16[192,1152]{1,0:T(8,128)(2,1)} %bitcast.21), channel_id=1, source_target_pairs={{0,24},{8,0},{16,8},{24,16},{32,56},{40,32},{48,40},{56,48},{64,88... | collective-permute-start | bytes 1327112 | tf_op jit(solution)/shard_map/ppermute | solution.py:39
  65.7 15.0 %collective-permute-start.3 = (bf16[4,4,24,768]{3,2,0,1:T(8,128)(2,1)}, bf16[4,4,24,768]{3,2,0,1:T(8,128)(2,1)}, u32[]{:S(2)}, u32[]{:S(2)}) collective-permute-start(bf16[4,4,24,768]{3,2,0,1:T(8,128)(2,1)} %get-tuple-element.32), channel_id=1, source_target_pairs={{0,1},{1,0},{2,3},{3,2},{4,5},{5,4},{6,7},{7,6},{8,9},{9,8},{10,11... | collective-permute-start | bytes 1769480 | tf_op jit(solution)/shard_map/ppermute | solution.py:50
  74.4 1.6 %copy-start.3 = (bf16[4,192,384]{2,1,0:T(8,128)(2,1)}, bf16[4,192,384]{2,1,0:T(8,128)(2,1)S(1)}, u32[]{:S(2)}) copy-start(bf16[4,192,384]{2,1,0:T(8,128)(2,1)S(1)} %all-to-all-done.1) | copy-start | bytes 1769476
  76.1 32.7 %all-to-all-start.2 = ((bf16[4,768,384]{2,1,0:T(8,128)(2,1)}), bf16[4,768,384]{2,1,0:T(8,128)(2,1)S(1)}, u32[]{:S(2)}, u32[]{:S(2)}) async-start(bf16[4,768,384]{2,1,0:T(8,128)(2,1)} %broadcast_in_dim.20), calls=%async_computation.2 | async-start | bytes 4718592 | tf_op jit(solution)/shard_map/all_to_all | solution.py:54
  85.2 11.5 %collective-permute-start.7 = (bf16[192,1152]{1,0:T(8,128)(2,1)S(1)}, bf16[192,1152]{1,0:T(8,128)(2,1)S(1)}, u32[]{:S(2)}, u32[]{:S(2)}) collective-permute-start(bf16[192,1152]{1,0:T(8,128)(2,1)S(1)} %get-tuple-element.24), channel_id=1, source_target_pairs={{0,64},{8,72},{16,80},{24,88},{32,96},{40,104},{48,112},{56,120},{... | collective-permute-start | bytes 1327112 | tf_op jit(solution)/shard_map/ppermute | solution.py:39
  88.3 17.2 %collective-permute-start.9 = (bf16[192,1152]{1,0:T(8,128)(2,1)S(1)}, bf16[192,1152]{1,0:T(8,128)(2,1)S(1)}, u32[]{:S(2)}, u32[]{:S(2)}) collective-permute-start(bf16[192,1152]{1,0:T(8,128)(2,1)S(1)} %get-tuple-element.25), channel_id=1, source_target_pairs={{0,32},{8,40},{16,48},{24,56},{32,64},{40,72},{48,80},{56,88},{64,... | collective-permute-start | bytes 1327112 | tf_op jit(solution)/shard_map/ppermute | solution.py:39
  92.1 16.5 %collective-permute-start.8 = (bf16[192,1152]{1,0:T(8,128)(2,1)S(1)}, bf16[192,1152]{1,0:T(8,128)(2,1)S(1)}, u32[]{:S(2)}, u32[]{:S(2)}) collective-permute-start(bf16[192,1152]{1,0:T(8,128)(2,1)S(1)} %get-tuple-element.26), channel_id=1, source_target_pairs={{0,96},{8,104},{16,112},{24,120},{32,0},{40,8},{48,16},{56,24},{64... | collective-permute-start | bytes 1327112 | tf_op jit(solution)/shard_map/ppermute | solution.py:39
  110.5 25.6 %copy-start = (f32[16,3,3072]{2,0,1:T(8,128)S(1)}, f32[16,3,3072]{2,0,1:T(8,128)}, u32[]{:S(2)}) copy-start(f32[16,3,3072]{2,0,1:T(8,128)} %param.18) | copy-start | bytes 1769476
  110.5 25.6 %copy-start.1 = (bf16[1,24,3072]{2,1,0:T(8,128)(2,1)S(1)}, bf16[1,24,3072]{2,1,0:T(8,128)(2,1)}, u32[]{:S(2)}) copy-start(bf16[1,24,3072]{2,1,0:T(8,128)(2,1)} %param.10) | copy-start | bytes 442372
  110.5 25.5 %copy-start.2 = (bf16[1,24,3072]{2,1,0:T(8,128)(2,1)S(1)}, bf16[1,24,3072]{2,1,0:T(8,128)(2,1)}, u32[]{:S(2)}) copy-start(bf16[1,24,3072]{2,1,0:T(8,128)(2,1)} %param.11) | copy-start | bytes 442372
  110.5 6.4 %collective-permute-start.10 = (bf16[96,3072]{1,0:T(8,128)(2,1)S(1)}, bf16[96,3072]{1,0:T(8,128)(2,1)S(1)}, u32[]{:S(2)}, u32[]{:S(2)}) collective-permute-start(bf16[96,3072]{1,0:T(8,128)(2,1)S(1)} %get-tuple-element.21), channel_id=1, source_target_pairs={{0,1},{1,0},{2,3},{3,2},{4,5},{5,4},{6,7},{7,6},{8,9},{9,8},{10,11... | collective-permute-start | bytes 1769480 | tf_op jit(solution)/shard_map/ppermute | solution.py:50
  117.1 9.3 %collective-permute-start.13 = (bf16[24,3072]{1,0:T(8,128)(2,1)S(1)}, bf16[24,3072]{1,0:T(8,128)(2,1)S(1)}, u32[]{:S(2)}, u32[]{:S(2)}) collective-permute-start(bf16[24,3072]{1,0:T(8,128)(2,1)S(1)} %get-tuple-element.27), channel_id=1, source_target_pairs={{0,2},{1,3},{2,4},{3,5},{4,6},{5,7},{6,0},{7,1},{8,10},{9,11},{10,... | collective-permute-start | bytes 442376 | tf_op jit(solution)/shard_map/ppermute | solution.py:46
  121.1 8.6 %collective-permute-start.12 = (bf16[24,3072]{1,0:T(8,128)(2,1)S(1)}, bf16[24,3072]{1,0:T(8,128)(2,1)S(1)}, u32[]{:S(2)}, u32[]{:S(2)}) collective-permute-start(bf16[24,3072]{1,0:T(8,128)(2,1)S(1)} %get-tuple-element.28), channel_id=1, source_target_pairs={{0,6},{1,7},{2,0},{3,1},{4,2},{5,3},{6,4},{7,5},{8,14},{9,15},{10,... | collective-permute-start | bytes 442376 | tf_op jit(solution)/shard_map/ppermute | solution.py:46
  124.2 11.8 %collective-permute-start.11 = (bf16[24,3072]{1,0:T(8,128)(2,1)S(1)}, bf16[24,3072]{1,0:T(8,128)(2,1)S(1)}, u32[]{:S(2)}, u32[]{:S(2)}) collective-permute-start(bf16[24,3072]{1,0:T(8,128)(2,1)S(1)} %get-tuple-element.29), channel_id=1, source_target_pairs={{0,4},{1,5},{2,6},{3,7},{4,0},{5,1},{6,2},{7,3},{8,12},{9,13},{10,... | collective-permute-start | bytes 442376 | tf_op jit(solution)/shard_map/ppermute | solution.py:46

commit v5 on v4

--- a/solution.py
+++ b/solution.py
@@ -78,9 +78,9 @@
     lowrank = jnp.dot(up_out_ref[...], down_out_ref[...], preferred_element_type=jnp.float32)
     merged_ref[3] = (base_out_ref[...].astype(jnp.float32) + lowrank).astype(jnp.bfloat16)
 
-    step = step_ref[0]
-    shift = modulation_ref[0, pl.ds(step, 1), :]
-    scale = modulation_ref[1, pl.ds(step, 1), :]
+    here = lax.broadcasted_iota(jnp.int32, (NSTEP, 1), 0) == step_ref[...]
+    shift = jnp.sum(jnp.where(here, modulation_ref[0], 0.0), axis=0, keepdims=True)
+    scale = jnp.sum(jnp.where(here, modulation_ref[1], 0.0), axis=0, keepdims=True)
     latent = latents_ref[...].astype(jnp.float32)
     mean_square = jnp.mean(latent * latent, axis=-1, keepdims=True)
     normed = latent * lax.rsqrt(mean_square + EPSILON) * (1.0 + scale) + shift
@@ -219,7 +219,7 @@
             jax.ShapeDtypeStruct((QUAD, rows, slab), jnp.bfloat16),
             jax.ShapeDtypeStruct((4, part, head_cols), jnp.bfloat16),
         ),
-        timestep,
+        timestep.reshape(1, 1),
         latents[0],
         modulation.transpose(1, 0, 2),
         base_qkv,
@@ -228,7 +228,6 @@
         base_out.T,
         down_out.T,
         up_out.T,
-        scalars=1,
         mebibytes=60,
         scratch=[pltpu.VMEM((QUAD, rows, slab // QUAD), jnp.float32)],
     )
@@ -241,7 +240,7 @@
 
     moving = held[:, :3].transpose(0, 2, 1, 3).reshape(QUAD * part, 3 * head_cols)
     own_rows = held[:, 3].reshape(QUAD * part, head_cols)
-    mine, moving = lax.optimization_barrier((mine, moving))
+    mine, held = lax.optimization_barrier((mine, held))
     blocks = [moving] + [shift_fsdp(moving, dx=-k) for k in range(1, QUAD)]
 
     run = jnp.stack([mine] + [shift_run(mine, k) for k in range(1, QUAD)], axis=1)

time: 138 us -> 138 us (level)
  no operation moved by 1% of the time
where the time goes in v5:
time: 138 us; the launch traced here: 137 us
  starting transfers between devices  63.2 us (46%)
  blocking collectives  31.4 us (23%)
  waiting for transfers between devices  26.6 us (19%)
  Pallas kernels  5.23 us (4%)
  local copies, waits for them, and re-layouts  3.89 us (3%)
  matrix products  3.12 us (2%)
  other arithmetic  2.52 us (2%)
  between operations  1.56 us (1%)
    all_gather x1, blocking collectives, per_device(): held = lax.all_gather(merged, 'fsdp', axis_index_groups=Z_GROUPS, axis=0)  31.4 us
    ppermute x6, starting transfers between devices, shift_run(): return lax.ppermute(value, 'sp', pairs)  19 us
    ppermute x6, starting transfers between devices, shift_fsdp(): return lax.ppermute(value, 'fsdp', pairs)  18 us
    ppermute x6, waiting for transfers between devices, shift_fsdp(): return lax.ppermute(value, 'fsdp', pairs)  15.7 us
    all_to_all x3, starting transfers between devices, exchange(): lax.all_to_all(value, axis, 0, 0, axis_index_groups=groups, tiled=True)  13.1 us
    ppermute x2, starting transfers between devices, other_core(): return lax.ppermute(value, 'sp', [(i, i ^ 1) for i in range(2 * QUAD)])  13.1 us
    ppermute x6, waiting for transfers between devices, shift_run(): return lax.ppermute(value, 'sp', pairs)  9.25 us
    pallas_call x3, Pallas kernels, call(): pl.pallas_call(kernel, grid=(1,), out_shape=out_shapes, in_specs=[smem] *...  5.23 us
  transfers between devices with their start and end apart: 17, of which 7 were waited for; matrix products, arithmetic and copies ran while one was open for 7% of the time, Pallas kernels for 0%

profile of v5, /device:TPU:27, one launch (start us, length us, event | category | flops | bytes accessed | tf_op | source)
XLA Modules:
  0.0 137.5 jit_solution(15328271291853456068)
XLA Ops:
  1.3 2.5 %shard_map.113 = (bf16[4,24,768]{2,1,0:T(8,128)(2,1)}, bf16[4,48,384]{2,1,0:T(8,128)(2,1)}) custom-call(s32[1,1]{1,0:T(1,128)} %bitcast.25.step_ref, bf16[24,3072]{1,0:T(8,128)(2,1)} %bitcast.28, f32[3,16,3072]{2,1,0:T(8,128)} %bitcast.26, bf16[3,48,384]{2,1,0:T(8,128)(2,1)} %base_qkv_ref.1, bf16[3,48,64]{2,1,0:T(8,128)(2,1)} %down_qkv_ref.1, ...), custom_call_target="tpu_custom_call" | custom-call | tf_op jit(solution)/shard_map/pallas_call | solution.py:186
  3.8 4.1 %all-to-all-start = ((bf16[4,24,768]{2,1,0:T(8,128)(2,1)}), bf16[4,24,768]{2,1,0:T(8,128)(2,1)S(1)}, u32[]{:S(2)}, u32[]{:S(2)}) async-start(bf16[4,24,768]{2,1,0:T(8,128)(2,1)} %get-tuple-element.12), calls=%async_computation | async-start | bytes 294912 | tf_op jit(solution)/shard_map/all_to_all | solution.py:54
  7.9 31.4 %all-gather = bf16[16,48,384]{2,1,0:T(8,128)(2,1)S(1)} all-gather(bf16[4,48,384]{2,1,0:T(8,128)(2,1)} %get-tuple-element.13), channel_id=2, replica_groups={{0,128,256,384},{8,136,264,392},{16,144,272,400},{24,152,280,408},{32,1..., dimensions={0}, use_global_device_ids=true | all-gather | bytes 737280 | tf_op jit(solution)/shard_map/all_gather | solution.py:239
  39.3 0.0 all-to-all-done
  39.3 0.1 fusion.7
  39.4 5.4 %collective-permute-start.2 = (bf16[4,24,768]{2,1,0:T(8,128)(2,1)S(1)}, bf16[4,24,768]{2,1,0:T(8,128)(2,1)S(1)}, u32[]{:S(2)}, u32[]{:S(2)}) collective-permute-start(bf16[4,24,768]{2,1,0:T(8,128)(2,1)S(1)} %rev.3), channel_id=1, source_target_pairs={{0,6},{1,7},{2,0},{3,1},{4,2},{5,3},{6,4},{7,5},{8,14},{9,15},{10,... | collective-permute-start | bytes 442376 | tf_op jit(solution)/shard_map/ppermute | solution.py:46
  44.8 1.9 %collective-permute-start.1 = (bf16[4,24,768]{2,1,0:T(8,128)(2,1)S(1)}, bf16[4,24,768]{2,1,0:T(8,128)(2,1)S(1)}, u32[]{:S(2)}, u32[]{:S(2)}) collective-permute-start(bf16[4,24,768]{2,1,0:T(8,128)(2,1)S(1)} %rev.3), channel_id=1, source_target_pairs={{0,4},{1,5},{2,6},{3,7},{4,0},{5,1},{6,2},{7,3},{8,12},{9,13},{10,... | collective-permute-start | bytes 442376 | tf_op jit(solution)/shard_map/ppermute | solution.py:46
  46.7 2.2 %collective-permute-start = (bf16[4,24,768]{2,1,0:T(8,128)(2,1)S(1)}, bf16[4,24,768]{2,1,0:T(8,128)(2,1)S(1)}, u32[]{:S(2)}, u32[]{:S(2)}) collective-permute-start(bf16[4,24,768]{2,1,0:T(8,128)(2,1)S(1)} %rev.3), channel_id=1, source_target_pairs={{0,2},{1,3},{2,4},{3,5},{4,6},{5,7},{6,0},{7,1},{8,10},{9,11},{10,... | collective-permute-start | bytes 442376 | tf_op jit(solution)/shard_map/ppermute | solution.py:46
  48.9 0.9 broadcast_in_dim.19
  49.8 4.2 %all-to-all-start.1 = ((bf16[4,192,384]{2,1,0:T(8,128)(2,1)}), bf16[4,192,384]{2,1,0:T(8,128)(2,1)S(1)}, u32[]{:S(2)}, u32[]{:S(2)}) async-start(bf16[4,192,384]{2,1,0:T(8,128)(2,1)} %broadcast_in_dim.19), calls=%async_computation.1 | async-start | bytes 1179648 | tf_op jit(solution)/shard_map/all_to_all | solution.py:54
  54.1 0.2 copy.20
  54.3 0.8 copy.21
  55.1 3.1 %collective-permute-start.6 = (bf16[192,1152]{1,0:T(8,128)(2,1)}, bf16[192,1152]{1,0:T(8,128)(2,1)}, u32[]{:S(2)}, u32[]{:S(2)}) collective-permute-start(bf16[192,1152]{1,0:T(8,128)(2,1)} %bitcast.22), channel_id=1, source_target_pairs={{0,8},{8,16},{16,24},{24,0},{32,40},{40,48},{48,56},{56,32},{64,72... | collective-permute-start | bytes 1327112 | tf_op jit(solution)/shard_map/ppermute | solution.py:39
  58.3 2.7 %collective-permute-start.5 = (bf16[192,1152]{1,0:T(8,128)(2,1)}, bf16[192,1152]{1,0:T(8,128)(2,1)}, u32[]{:S(2)}, u32[]{:S(2)}) collective-permute-start(bf16[192,1152]{1,0:T(8,128)(2,1)} %bitcast.22), channel_id=1, source_target_pairs={{0,16},{8,24},{16,0},{24,8},{32,48},{40,56},{48,32},{56,40},{64,80... | collective-permute-start | bytes 1327112 | tf_op jit(solution)/shard_map/ppermute | solution.py:39
  61.0 3.4 %collective-permute-start.4 = (bf16[192,1152]{1,0:T(8,128)(2,1)}, bf16[192,1152]{1,0:T(8,128)(2,1)}, u32[]{:S(2)}, u32[]{:S(2)}) collective-permute-start(bf16[192,1152]{1,0:T(8,128)(2,1)} %bitcast.22), channel_id=1, source_target_pairs={{0,24},{8,0},{16,8},{24,16},{32,56},{40,32},{48,40},{56,48},{64,88... | collective-permute-start | bytes 1327112 | tf_op jit(solution)/shard_map/ppermute | solution.py:39
  64.5 0.0 collective-permute-done.1
  64.5 0.9 fusion.9
  65.4 8.3 %collective-permute-start.3 = (bf16[4,4,24,768]{3,2,0,1:T(8,128)(2,1)}, bf16[4,4,24,768]{3,2,0,1:T(8,128)(2,1)}, u32[]{:S(2)}, u32[]{:S(2)}) collective-permute-start(bf16[4,4,24,768]{3,2,0,1:T(8,128)(2,1)} %get-tuple-element.30), channel_id=1, source_target_pairs={{0,1},{1,0},{2,3},{3,2},{4,5},{5,4},{6,7},{7,6},{8,9},{9,8},{10,11... | collective-permute-start | bytes 1769480 | tf_op jit(solution)/shard_map/ppermute | solution.py:50
  73.7 1.6 %broadcast_in_dim.20 = bf16[4,768,384]{2,1,0:T(8,128)(2,1)} broadcast(bf16[768,384]{1,0:T(8,128)(2,1)S(1)} %bitcast.33), dimensions={1,2} | broadcast | bytes 2949120 | tf_op jit(solution)/shard_map/broadcast_in_dim | solution.py:249
  75.4 4.7 %all-to-all-start.2 = ((bf16[4,768,384]{2,1,0:T(8,128)(2,1)}), bf16[4,768,384]{2,1,0:T(8,128)(2,1)S(1)}, u32[]{:S(2)}, u32[]{:S(2)}) async-start(bf16[4,768,384]{2,1,0:T(8,128)(2,1)} %broadcast_in_dim.20), calls=%async_computation.2 | async-start | bytes 4718592 | tf_op jit(solution)/shard_map/all_to_all | solution.py:54
  80.1 0.0 collective-permute-done.6.refs_2_
  80.1 0.0 collective-permute-done.5.refs_1_
  80.1 1.2 collective-permute-done.4.refs_0_
  81.3 0.0 collective-permute-done.3
  81.3 1.2 pad_maximum_fusion
  82.5 0.1 copy.18
  82.6 3.1 %convolution_convert_fusion = bf16[768,1152]{1,0:T(8,128)(2,1)S(1)} fusion(bf16[768,768]{1,0:T(8,128)(2,1)S(1)} %bitcast.36, bf16[192,1152]{1,0:T(8,128)(2,1)} %get-tuple-element.17, bf16[192,1152]{1,0:T(8,128)(2,1)} %get-tuple-element.16, bf16[192,1152]{1,0:T(8,128)(2,1)} %get-tuple-element.15, bf16[192,1152]{1,0:T(8,128)(2,1)} %bitcast.22), kind=kOutput, calls=%fused_computation | convolution fusion | flops 1366917120 | bytes 4718592 | tf_op jit(solution)/shard_map/dot_general | solution.py:256
  85.7 0.1 fusion.10
  85.8 3.1 %collective-permute-start.7 = (bf16[192,1152]{1,0:T(8,128)(2,1)S(1)}, bf16[192,1152]{1,0:T(8,128)(2,1)S(1)}, u32[]{:S(2)}, u32[]{:S(2)}) collective-permute-start(bf16[192,1152]{1,0:T(8,128)(2,1)S(1)} %get-tuple-element.22), channel_id=1, source_target_pairs={{0,64},{8,72},{16,80},{24,88},{32,96},{40,104},{48,112},{56,120},{... | collective-permute-start | bytes 1327112 | tf_op jit(solution)/shard_map/ppermute | solution.py:39
  88.9 3.7 %collective-permute-start.9 = (bf16[192,1152]{1,0:T(8,128)(2,1)S(1)}, bf16[192,1152]{1,0:T(8,128)(2,1)S(1)}, u32[]{:S(2)}, u32[]{:S(2)}) collective-permute-start(bf16[192,1152]{1,0:T(8,128)(2,1)S(1)} %get-tuple-element.23), channel_id=1, source_target_pairs={{0,32},{8,40},{16,48},{24,56},{32,64},{40,72},{48,80},{56,88},{64,... | collective-permute-start | bytes 1327112 | tf_op jit(solution)/shard_map/ppermute | solution.py:39
  92.6 1.9 %collective-permute-start.8 = (bf16[192,1152]{1,0:T(8,128)(2,1)S(1)}, bf16[192,1152]{1,0:T(8,128)(2,1)S(1)}, u32[]{:S(2)}, u32[]{:S(2)}) collective-permute-start(bf16[192,1152]{1,0:T(8,128)(2,1)S(1)} %get-tuple-element.24), channel_id=1, source_target_pairs={{0,96},{8,104},{16,112},{24,120},{32,0},{40,8},{48,16},{56,24},{64... | collective-permute-start | bytes 1327112 | tf_op jit(solution)/shard_map/ppermute | solution.py:39
  94.5 2.8 %collective-permute-done.7 = bf16[192,1152]{1,0:T(8,128)(2,1)S(1)} collective-permute-done((bf16[192,1152]{1,0:T(8,128)(2,1)S(1)}, bf16[192,1152]{1,0:T(8,128)(2,1)S(1)}, u32[]{:S(2)}, u32[]{:S(2)}) %collective-permute-start.7) | collective-permute-done | bytes 442400 | tf_op jit(solution)/shard_map/ppermute | solution.py:39
  97.3 8.8 %collective-permute-done.9 = bf16[192,1152]{1,0:T(8,128)(2,1)S(1)} collective-permute-done((bf16[192,1152]{1,0:T(8,128)(2,1)S(1)}, bf16[192,1152]{1,0:T(8,128)(2,1)S(1)}, u32[]{:S(2)}, u32[]{:S(2)}) %collective-permute-start.9) | collective-permute-done | bytes 442400 | tf_op jit(solution)/shard_map/ppermute | solution.py:39
  106.1 3.0 %collective-permute-done.8 = bf16[192,1152]{1,0:T(8,128)(2,1)S(1)} collective-permute-done((bf16[192,1152]{1,0:T(8,128)(2,1)S(1)}, bf16[192,1152]{1,0:T(8,128)(2,1)S(1)}, u32[]{:S(2)}, u32[]{:S(2)}) %collective-permute-start.8) | collective-permute-done | bytes 442400 | tf_op jit(solution)/shard_map/ppermute | solution.py:39
  109.1 0.2 add_convert_fusion.1.projected_ref
  109.3 1.8 %shard_map.115 = (bf16[96,3072]{1,0:T(8,128)(2,1)S(1)}, bf16[96,3072]{1,0:T(8,128)(2,1)S(1)}) custom-call(bf16[192,1152]{1,0:T(8,128)(2,1)S(1)} %add_convert_fusion.1.projected_ref, bf16[4,768,384]{2,1,0:T(8,128)(2,1)S(1)} %all-to-all-done.2.weights_ref), custom_call_target="tpu_custom_call" | custom-call | tf_op jit(solution)/shard_map/pallas_call | solution.py:186
  111.1 0.0 copy-start
  111.1 0.0 copy-start.1
  111.1 0.0 copy-start.2
  111.1 4.8 %collective-permute-start.10 = (bf16[96,3072]{1,0:T(8,128)(2,1)S(1)}, bf16[96,3072]{1,0:T(8,128)(2,1)S(1)}, u32[]{:S(2)}, u32[]{:S(2)}) collective-permute-start(bf16[96,3072]{1,0:T(8,128)(2,1)S(1)} %get-tuple-element.19), channel_id=1, source_target_pairs={{0,1},{1,0},{2,3},{3,2},{4,5},{5,4},{6,7},{7,6},{8,9},{9,8},{10,11... | collective-permute-start | bytes 1769480 | tf_op jit(solution)/shard_map/ppermute | solution.py:50
  115.9 1.6 %collective-permute-done.10 = bf16[96,3072]{1,0:T(8,128)(2,1)S(1)} collective-permute-done((bf16[96,3072]{1,0:T(8,128)(2,1)S(1)}, bf16[96,3072]{1,0:T(8,128)(2,1)S(1)}, u32[]{:S(2)}, u32[]{:S(2)}) %collective-permute-start.10) | collective-permute-done | bytes 589856 | tf_op jit(solution)/shard_map/ppermute | solution.py:50
  117.5 0.1 add_convert_fusion
  117.7 4.2 %collective-permute-start.13 = (bf16[24,3072]{1,0:T(8,128)(2,1)S(1)}, bf16[24,3072]{1,0:T(8,128)(2,1)S(1)}, u32[]{:S(2)}, u32[]{:S(2)}) collective-permute-start(bf16[24,3072]{1,0:T(8,128)(2,1)S(1)} %get-tuple-element.25), channel_id=1, source_target_pairs={{0,2},{1,3},{2,4},{3,5},{4,6},{5,7},{6,0},{7,1},{8,10},{9,11},{10,... | collective-permute-start | bytes 442376 | tf_op jit(solution)/shard_map/ppermute | solution.py:46
  121.9 2.9 %collective-permute-start.12 = (bf16[24,3072]{1,0:T(8,128)(2,1)S(1)}, bf16[24,3072]{1,0:T(8,128)(2,1)S(1)}, u32[]{:S(2)}, u32[]{:S(2)}) collective-permute-start(bf16[24,3072]{1,0:T(8,128)(2,1)S(1)} %get-tuple-element.26), channel_id=1, source_target_pairs={{0,6},{1,7},{2,0},{3,1},{4,2},{5,3},{6,4},{7,5},{8,14},{9,15},{10,... | collective-permute-start | bytes 442376 | tf_op jit(solution)/shard_map/ppermute | solution.py:46
  124.8 2.4 %collective-permute-start.11 = (bf16[24,3072]{1,0:T(8,128)(2,1)S(1)}, bf16[24,3072]{1,0:T(8,128)(2,1)S(1)}, u32[]{:S(2)}, u32[]{:S(2)}) collective-permute-start(bf16[24,3072]{1,0:T(8,128)(2,1)S(1)} %get-tuple-element.27), channel_id=1, source_target_pairs={{0,4},{1,5},{2,6},{3,7},{4,0},{5,1},{6,2},{7,3},{8,12},{9,13},{10,... | collective-permute-start | bytes 442376 | tf_op jit(solution)/shard_map/ppermute | solution.py:46
  127.3 2.8 %collective-permute-done.12.second_ref = bf16[24,3072]{1,0:T(8,128)(2,1)S(1)} collective-permute-done((bf16[24,3072]{1,0:T(8,128)(2,1)S(1)}, bf16[24,3072]{1,0:T(8,128)(2,1)S(1)}, u32[]{:S(2)}, u32[]{:S(2)}) %collective-permute-start.12) | collective-permute-done | bytes 147488 | tf_op jit(solution)/shard_map/ppermute | solution.py:46
  130.1 6.4 %collective-permute-done.11.first_ref = bf16[24,3072]{1,0:T(8,128)(2,1)S(1)} collective-permute-done((bf16[24,3072]{1,0:T(8,128)(2,1)S(1)}, bf16[24,3072]{1,0:T(8,128)(2,1)S(1)}, u32[]{:S(2)}, u32[]{:S(2)}) %collective-permute-start.11) | collective-permute-done | bytes 147488 | tf_op jit(solution)/shard_map/ppermute | solution.py:46
  136.5 1.0 shard_map.116
  (15 shorter events, 0.1 us)
Async XLA Ops:
  3.8 35.5 %all-to-all-start = ((bf16[4,24,768]{2,1,0:T(8,128)(2,1)}), bf16[4,24,768]{2,1,0:T(8,128)(2,1)S(1)}, u32[]{:S(2)}, u32[]{:S(2)}) async-start(bf16[4,24,768]{2,1,0:T(8,128)(2,1)} %get-tuple-element.12), calls=%async_computation | async-start | bytes 294912 | tf_op jit(solution)/shard_map/all_to_all | solution.py:54
  39.4 21.6 %collective-permute-start.2 = (bf16[4,24,768]{2,1,0:T(8,128)(2,1)S(1)}, bf16[4,24,768]{2,1,0:T(8,128)(2,1)S(1)}, u32[]{:S(2)}, u32[]{:S(2)}) collective-permute-start(bf16[4,24,768]{2,1,0:T(8,128)(2,1)S(1)} %rev.3), channel_id=1, source_target_pairs={{0,6},{1,7},{2,0},{3,1},{4,2},{5,3},{6,4},{7,5},{8,14},{9,15},{10,... | collective-permute-start | bytes 442376 | tf_op jit(solution)/shard_map/ppermute | solution.py:46
  44.8 19.7 %collective-permute-start.1 = (bf16[4,24,768]{2,1,0:T(8,128)(2,1)S(1)}, bf16[4,24,768]{2,1,0:T(8,128)(2,1)S(1)}, u32[]{:S(2)}, u32[]{:S(2)}) collective-permute-start(bf16[4,24,768]{2,1,0:T(8,128)(2,1)S(1)} %rev.3), channel_id=1, source_target_pairs={{0,4},{1,5},{2,6},{3,7},{4,0},{5,1},{6,2},{7,3},{8,12},{9,13},{10,... | collective-permute-start | bytes 442376 | tf_op jit(solution)/shard_map/ppermute | solution.py:46
  46.7 17.8 %collective-permute-start = (bf16[4,24,768]{2,1,0:T(8,128)(2,1)S(1)}, bf16[4,24,768]{2,1,0:T(8,128)(2,1)S(1)}, u32[]{:S(2)}, u32[]{:S(2)}) collective-permute-start(bf16[4,24,768]{2,1,0:T(8,128)(2,1)S(1)} %rev.3), channel_id=1, source_target_pairs={{0,2},{1,3},{2,4},{3,5},{4,6},{5,7},{6,0},{7,1},{8,10},{9,11},{10,... | collective-permute-start | bytes 442376 | tf_op jit(solution)/shard_map/ppermute | solution.py:46
  49.8 23.9 %all-to-all-start.1 = ((bf16[4,192,384]{2,1,0:T(8,128)(2,1)}), bf16[4,192,384]{2,1,0:T(8,128)(2,1)S(1)}, u32[]{:S(2)}, u32[]{:S(2)}) async-start(bf16[4,192,384]{2,1,0:T(8,128)(2,1)} %broadcast_in_dim.19), calls=%async_computation.1 | async-start | bytes 1179648 | tf_op jit(solution)/shard_map/all_to_all | solution.py:54
  55.1 24.9 %collective-permute-start.6 = (bf16[192,1152]{1,0:T(8,128)(2,1)}, bf16[192,1152]{1,0:T(8,128)(2,1)}, u32[]{:S(2)}, u32[]{:S(2)}) collective-permute-start(bf16[192,1152]{1,0:T(8,128)(2,1)} %bitcast.22), channel_id=1, source_target_pairs={{0,8},{8,16},{16,24},{24,0},{32,40},{40,48},{48,56},{56,32},{64,72... | collective-permute-start | bytes 1327112 | tf_op jit(solution)/shard_map/ppermute | solution.py:39
  58.3 21.8 %collective-permute-start.5 = (bf16[192,1152]{1,0:T(8,128)(2,1)}, bf16[192,1152]{1,0:T(8,128)(2,1)}, u32[]{:S(2)}, u32[]{:S(2)}) collective-permute-start(bf16[192,1152]{1,0:T(8,128)(2,1)} %bitcast.22), channel_id=1, source_target_pairs={{0,16},{8,24},{16,0},{24,8},{32,48},{40,56},{48,32},{56,40},{64,80... | collective-permute-start | bytes 1327112 | tf_op jit(solution)/shard_map/ppermute | solution.py:39
  61.0 20.3 %collective-permute-start.4 = (bf16[192,1152]{1,0:T(8,128)(2,1)}, bf16[192,1152]{1,0:T(8,128)(2,1)}, u32[]{:S(2)}, u32[]{:S(2)}) collective-permute-start(bf16[192,1152]{1,0:T(8,128)(2,1)} %bitcast.22), channel_id=1, source_target_pairs={{0,24},{8,0},{16,8},{24,16},{32,56},{40,32},{48,40},{56,48},{64,88... | collective-permute-start | bytes 1327112 | tf_op jit(solution)/shard_map/ppermute | solution.py:39
  65.4 15.9 %collective-permute-start.3 = (bf16[4,4,24,768]{3,2,0,1:T(8,128)(2,1)}, bf16[4,4,24,768]{3,2,0,1:T(8,128)(2,1)}, u32[]{:S(2)}, u32[]{:S(2)}) collective-permute-start(bf16[4,4,24,768]{3,2,0,1:T(8,128)(2,1)} %get-tuple-element.30), channel_id=1, source_target_pairs={{0,1},{1,0},{2,3},{3,2},{4,5},{5,4},{6,7},{7,6},{8,9},{9,8},{10,11... | collective-permute-start | bytes 1769480 | tf_op jit(solution)/shard_map/ppermute | solution.py:50
  73.7 1.6 %copy-start.3 = (bf16[4,192,384]{2,1,0:T(8,128)(2,1)}, bf16[4,192,384]{2,1,0:T(8,128)(2,1)S(1)}, u32[]{:S(2)}) copy-start(bf16[4,192,384]{2,1,0:T(8,128)(2,1)S(1)} %all-to-all-done.1) | copy-start | bytes 1769476
  75.4 34.0 %all-to-all-start.2 = ((bf16[4,768,384]{2,1,0:T(8,128)(2,1)}), bf16[4,768,384]{2,1,0:T(8,128)(2,1)S(1)}, u32[]{:S(2)}, u32[]{:S(2)}) async-start(bf16[4,768,384]{2,1,0:T(8,128)(2,1)} %broadcast_in_dim.20), calls=%async_computation.2 | async-start | bytes 4718592 | tf_op jit(solution)/shard_map/all_to_all | solution.py:54
  85.8 11.5 %collective-permute-start.7 = (bf16[192,1152]{1,0:T(8,128)(2,1)S(1)}, bf16[192,1152]{1,0:T(8,128)(2,1)S(1)}, u32[]{:S(2)}, u32[]{:S(2)}) collective-permute-start(bf16[192,1152]{1,0:T(8,128)(2,1)S(1)} %get-tuple-element.22), channel_id=1, source_target_pairs={{0,64},{8,72},{16,80},{24,88},{32,96},{40,104},{48,112},{56,120},{... | collective-permute-start | bytes 1327112 | tf_op jit(solution)/shard_map/ppermute | solution.py:39
  88.9 17.2 %collective-permute-start.9 = (bf16[192,1152]{1,0:T(8,128)(2,1)S(1)}, bf16[192,1152]{1,0:T(8,128)(2,1)S(1)}, u32[]{:S(2)}, u32[]{:S(2)}) collective-permute-start(bf16[192,1152]{1,0:T(8,128)(2,1)S(1)} %get-tuple-element.23), channel_id=1, source_target_pairs={{0,32},{8,40},{16,48},{24,56},{32,64},{40,72},{48,80},{56,88},{64,... | collective-permute-start | bytes 1327112 | tf_op jit(solution)/shard_map/ppermute | solution.py:39
  92.6 16.5 %collective-permute-start.8 = (bf16[192,1152]{1,0:T(8,128)(2,1)S(1)}, bf16[192,1152]{1,0:T(8,128)(2,1)S(1)}, u32[]{:S(2)}, u32[]{:S(2)}) collective-permute-start(bf16[192,1152]{1,0:T(8,128)(2,1)S(1)} %get-tuple-element.24), channel_id=1, source_target_pairs={{0,96},{8,104},{16,112},{24,120},{32,0},{40,8},{48,16},{56,24},{64... | collective-permute-start | bytes 1327112 | tf_op jit(solution)/shard_map/ppermute | solution.py:39
  111.1 25.4 %copy-start = (f32[16,3,3072]{2,0,1:T(8,128)S(1)}, f32[16,3,3072]{2,0,1:T(8,128)}, u32[]{:S(2)}) copy-start(f32[16,3,3072]{2,0,1:T(8,128)} %param.18) | copy-start | bytes 1769476
  111.1 25.4 %copy-start.1 = (bf16[1,24,3072]{2,1,0:T(8,128)(2,1)S(1)}, bf16[1,24,3072]{2,1,0:T(8,128)(2,1)}, u32[]{:S(2)}) copy-start(bf16[1,24,3072]{2,1,0:T(8,128)(2,1)} %param.10) | copy-start | bytes 442372
  111.1 25.4 %copy-start.2 = (bf16[1,24,3072]{2,1,0:T(8,128)(2,1)S(1)}, bf16[1,24,3072]{2,1,0:T(8,128)(2,1)}, u32[]{:S(2)}) copy-start(bf16[1,24,3072]{2,1,0:T(8,128)(2,1)} %param.11) | copy-start | bytes 442372
  111.1 6.4 %collective-permute-start.10 = (bf16[96,3072]{1,0:T(8,128)(2,1)S(1)}, bf16[96,3072]{1,0:T(8,128)(2,1)S(1)}, u32[]{:S(2)}, u32[]{:S(2)}) collective-permute-start(bf16[96,3072]{1,0:T(8,128)(2,1)S(1)} %get-tuple-element.19), channel_id=1, source_target_pairs={{0,1},{1,0},{2,3},{3,2},{4,5},{5,4},{6,7},{7,6},{8,9},{9,8},{10,11... | collective-permute-start | bytes 1769480 | tf_op jit(solution)/shard_map/ppermute | solution.py:50
  117.7 9.5 %collective-permute-start.13 = (bf16[24,3072]{1,0:T(8,128)(2,1)S(1)}, bf16[24,3072]{1,0:T(8,128)(2,1)S(1)}, u32[]{:S(2)}, u32[]{:S(2)}) collective-permute-start(bf16[24,3072]{1,0:T(8,128)(2,1)S(1)} %get-tuple-element.25), channel_id=1, source_target_pairs={{0,2},{1,3},{2,4},{3,5},{4,6},{5,7},{6,0},{7,1},{8,10},{9,11},{10,... | collective-permute-start | bytes 442376 | tf_op jit(solution)/shard_map/ppermute | solution.py:46
  121.9 8.1 %collective-permute-start.12 = (bf16[24,3072]{1,0:T(8,128)(2,1)S(1)}, bf16[24,3072]{1,0:T(8,128)(2,1)S(1)}, u32[]{:S(2)}, u32[]{:S(2)}) collective-permute-start(bf16[24,3072]{1,0:T(8,128)(2,1)S(1)} %get-tuple-element.26), channel_id=1, source_target_pairs={{0,6},{1,7},{2,0},{3,1},{4,2},{5,3},{6,4},{7,5},{8,14},{9,15},{10,... | collective-permute-start | bytes 442376 | tf_op jit(solution)/shard_map/ppermute | solution.py:46
  124.8 11.7 %collective-permute-start.11 = (bf16[24,3072]{1,0:T(8,128)(2,1)S(1)}, bf16[24,3072]{1,0:T(8,128)(2,1)S(1)}, u32[]{:S(2)}, u32[]{:S(2)}) collective-permute-start(bf16[24,3072]{1,0:T(8,128)(2,1)S(1)} %get-tuple-element.27), channel_id=1, source_target_pairs={{0,4},{1,5},{2,6},{3,7},{4,0},{5,1},{6,2},{7,3},{8,12},{9,13},{10,... | collective-permute-start | bytes 442376 | tf_op jit(solution)/shard_map/ppermute | solution.py:46

commit v6 on v4

--- a/solution.py
+++ b/solution.py
@@ -181,7 +181,7 @@
     return pl.BlockSpec(shape, lambda i: (0,) * len(shape))
 
 
-def call(kernel, out_shapes, *operands, scalars=0, mebibytes=40, scratch=()):
+def call(kernel, out_shapes, *operands, scalars=0, mebibytes=20, scratch=()):
     smem = pl.BlockSpec(memory_space=pltpu.SMEM)
     return pl.pallas_call(
         kernel,
@@ -280,7 +280,7 @@
         step_noise[0],
         modulation.transpose(1, 0, 2),
         scalars=1,
-        mebibytes=40,
+        mebibytes=20,
     )
     return (velocity[None], next_rows[None])
 

time: 138 us -> 138 us (level)
  no operation moved by 1% of the time
where the time goes in v6:
time: 138 us; the launch traced here: 137 us
  starting transfers between devices  63 us (46%)
  blocking collectives  31.4 us (23%)
  waiting for transfers between devices  26.4 us (19%)
  Pallas kernels  5.2 us (4%)
  local copies, waits for them, and re-layouts  3.89 us (3%)
  matrix products  3.12 us (2%)
  other arithmetic  2.52 us (2%)
  between operations  1.56 us (1%)
    all_gather x1, blocking collectives, per_device(): held = lax.all_gather(merged, 'fsdp', axis_index_groups=Z_GROUPS, axis=0)  31.4 us
    ppermute x6, starting transfers between devices, shift_fsdp(): return lax.ppermute(value, 'fsdp', pairs)  18.6 us
    ppermute x6, starting transfers between devices, shift_run(): return lax.ppermute(value, 'sp', pairs)  18.5 us
    ppermute x6, waiting for transfers between devices, shift_fsdp(): return lax.ppermute(value, 'fsdp', pairs)  15.2 us
    ppermute x2, starting transfers between devices, other_core(): return lax.ppermute(value, 'sp', [(i, i ^ 1) for i in range(2 * QUAD)])  13.5 us
    all_to_all x3, starting transfers between devices, exchange(): lax.all_to_all(value, axis, 0, 0, axis_index_groups=groups, tiled=True)  12.4 us
    ppermute x6, waiting for transfers between devices, shift_run(): return lax.ppermute(value, 'sp', pairs)  9.63 us
    pallas_call x3, Pallas kernels, call(): pl.pallas_call(kernel, grid=(1,), out_shape=out_shapes, in_specs=[smem] *...  5.19 us
  transfers between devices with their start and end apart: 17, of which 7 were waited for; matrix products, arithmetic and copies ran while one was open for 7% of the time, Pallas kernels for 0%

profile of v6, /device:TPU:27, one launch (start us, length us, event | category | flops | bytes accessed | tf_op | source)
XLA Modules:
  0.0 137.1 jit_solution(14612669856150392520)
XLA Ops:
  1.3 2.5 %shard_map.113 = (bf16[4,24,768]{2,1,0:T(8,128)(2,1)}, bf16[4,48,384]{2,1,0:T(8,128)(2,1)}) custom-call(s32[1]{0:T(128)S(6)} %copy.25.step_ref, bf16[24,3072]{1,0:T(8,128)(2,1)} %bitcast.26, f32[3,16,3072]{2,1,0:T(8,128)} %bitcast.24, bf16[3,48,384]{2,1,0:T(8,128)(2,1)} %base_qkv_ref.1, bf16[3,48,64]{2,1,0:T(8,128)(2,1)} %down_qkv_ref.1, ...), custom_call_target="tpu_custom_call" | custom-call | tf_op jit(solution)/shard_map/pallas_call | solution.py:186
  3.7 4.1 %all-to-all-start = ((bf16[4,24,768]{2,1,0:T(8,128)(2,1)}), bf16[4,24,768]{2,1,0:T(8,128)(2,1)S(1)}, u32[]{:S(2)}, u32[]{:S(2)}) async-start(bf16[4,24,768]{2,1,0:T(8,128)(2,1)} %get-tuple-element.13), calls=%async_computation | async-start | bytes 294912 | tf_op jit(solution)/shard_map/all_to_all | solution.py:54
  7.9 31.4 %all-gather = bf16[16,48,384]{2,1,0:T(8,128)(2,1)S(1)} all-gather(bf16[4,48,384]{2,1,0:T(8,128)(2,1)} %get-tuple-element.14), channel_id=2, replica_groups={{0,128,256,384},{8,136,264,392},{16,144,272,400},{24,152,280,408},{32,1..., dimensions={0}, use_global_device_ids=true | all-gather | bytes 737280 | tf_op jit(solution)/shard_map/all_gather | solution.py:240
  39.3 0.2 copy.20
  39.5 0.8 copy.21
  40.3 0.0 all-to-all-done
  40.3 0.1 fusion.7
  40.4 5.1 %collective-permute-start.2 = (bf16[4,24,768]{2,1,0:T(8,128)(2,1)S(1)}, bf16[4,24,768]{2,1,0:T(8,128)(2,1)S(1)}, u32[]{:S(2)}, u32[]{:S(2)}) collective-permute-start(bf16[4,24,768]{2,1,0:T(8,128)(2,1)S(1)} %rev.3), channel_id=1, source_target_pairs={{0,6},{1,7},{2,0},{3,1},{4,2},{5,3},{6,4},{7,5},{8,14},{9,15},{10,... | collective-permute-start | bytes 442376 | tf_op jit(solution)/shard_map/ppermute | solution.py:46
  45.6 1.9 %collective-permute-start.1 = (bf16[4,24,768]{2,1,0:T(8,128)(2,1)S(1)}, bf16[4,24,768]{2,1,0:T(8,128)(2,1)S(1)}, u32[]{:S(2)}, u32[]{:S(2)}) collective-permute-start(bf16[4,24,768]{2,1,0:T(8,128)(2,1)S(1)} %rev.3), channel_id=1, source_target_pairs={{0,4},{1,5},{2,6},{3,7},{4,0},{5,1},{6,2},{7,3},{8,12},{9,13},{10,... | collective-permute-start | bytes 442376 | tf_op jit(solution)/shard_map/ppermute | solution.py:46
  47.5 2.2 %collective-permute-start = (bf16[4,24,768]{2,1,0:T(8,128)(2,1)S(1)}, bf16[4,24,768]{2,1,0:T(8,128)(2,1)S(1)}, u32[]{:S(2)}, u32[]{:S(2)}) collective-permute-start(bf16[4,24,768]{2,1,0:T(8,128)(2,1)S(1)} %rev.3), channel_id=1, source_target_pairs={{0,2},{1,3},{2,4},{3,5},{4,6},{5,7},{6,0},{7,1},{8,10},{9,11},{10,... | collective-permute-start | bytes 442376 | tf_op jit(solution)/shard_map/ppermute | solution.py:46
  49.7 0.9 broadcast_in_dim.19
  50.6 4.2 %all-to-all-start.1 = ((bf16[4,192,384]{2,1,0:T(8,128)(2,1)}), bf16[4,192,384]{2,1,0:T(8,128)(2,1)S(1)}, u32[]{:S(2)}, u32[]{:S(2)}) async-start(bf16[4,192,384]{2,1,0:T(8,128)(2,1)} %broadcast_in_dim.19), calls=%async_computation.1 | async-start | bytes 1179648 | tf_op jit(solution)/shard_map/all_to_all | solution.py:54
  54.8 3.1 %collective-permute-start.6 = (bf16[192,1152]{1,0:T(8,128)(2,1)}, bf16[192,1152]{1,0:T(8,128)(2,1)}, u32[]{:S(2)}, u32[]{:S(2)}) collective-permute-start(bf16[192,1152]{1,0:T(8,128)(2,1)} %bitcast.21), channel_id=1, source_target_pairs={{0,8},{8,16},{16,24},{24,0},{32,40},{40,48},{48,56},{56,32},{64,72... | collective-permute-start | bytes 1327112 | tf_op jit(solution)/shard_map/ppermute | solution.py:39
  58.0 3.0 %collective-permute-start.5 = (bf16[192,1152]{1,0:T(8,128)(2,1)}, bf16[192,1152]{1,0:T(8,128)(2,1)}, u32[]{:S(2)}, u32[]{:S(2)}) collective-permute-start(bf16[192,1152]{1,0:T(8,128)(2,1)} %bitcast.21), channel_id=1, source_target_pairs={{0,16},{8,24},{16,0},{24,8},{32,48},{40,56},{48,32},{56,40},{64,80... | collective-permute-start | bytes 1327112 | tf_op jit(solution)/shard_map/ppermute | solution.py:39
  61.0 3.8 %collective-permute-start.4 = (bf16[192,1152]{1,0:T(8,128)(2,1)}, bf16[192,1152]{1,0:T(8,128)(2,1)}, u32[]{:S(2)}, u32[]{:S(2)}) collective-permute-start(bf16[192,1152]{1,0:T(8,128)(2,1)} %bitcast.21), channel_id=1, source_target_pairs={{0,24},{8,0},{16,8},{24,16},{32,56},{40,32},{48,40},{56,48},{64,88... | collective-permute-start | bytes 1327112 | tf_op jit(solution)/shard_map/ppermute | solution.py:39
  64.8 0.0 collective-permute-done.1
  64.8 0.0 collective-permute-done
  64.8 0.9 fusion.9
  65.7 8.7 %collective-permute-start.3 = (bf16[4,4,24,768]{3,2,0,1:T(8,128)(2,1)}, bf16[4,4,24,768]{3,2,0,1:T(8,128)(2,1)}, u32[]{:S(2)}, u32[]{:S(2)}) collective-permute-start(bf16[4,4,24,768]{3,2,0,1:T(8,128)(2,1)} %get-tuple-element.32), channel_id=1, source_target_pairs={{0,1},{1,0},{2,3},{3,2},{4,5},{5,4},{6,7},{7,6},{8,9},{9,8},{10,11... | collective-permute-start | bytes 1769480 | tf_op jit(solution)/shard_map/ppermute | solution.py:50
  74.4 0.0 all-to-all-done.1
  74.4 1.6 %broadcast_in_dim.20 = bf16[4,768,384]{2,1,0:T(8,128)(2,1)} broadcast(bf16[768,384]{1,0:T(8,128)(2,1)S(1)} %bitcast.31), dimensions={1,2} | broadcast | bytes 2949120 | tf_op jit(solution)/shard_map/broadcast_in_dim | solution.py:250
  76.1 4.0 %all-to-all-start.2 = ((bf16[4,768,384]{2,1,0:T(8,128)(2,1)}), bf16[4,768,384]{2,1,0:T(8,128)(2,1)S(1)}, u32[]{:S(2)}, u32[]{:S(2)}) async-start(bf16[4,768,384]{2,1,0:T(8,128)(2,1)} %broadcast_in_dim.20), calls=%async_computation.2 | async-start | bytes 4718592 | tf_op jit(solution)/shard_map/all_to_all | solution.py:54
  80.1 0.0 collective-permute-done.6.refs_2_
  80.1 0.7 collective-permute-done.4.refs_0_
  80.7 1.2 pad_maximum_fusion
  81.9 0.1 copy.19
  82.0 3.1 %convolution_convert_fusion = bf16[768,1152]{1,0:T(8,128)(2,1)S(1)} fusion(bf16[768,768]{1,0:T(8,128)(2,1)S(1)} %bitcast.34, bf16[192,1152]{1,0:T(8,128)(2,1)} %get-tuple-element.19, bf16[192,1152]{1,0:T(8,128)(2,1)} %get-tuple-element.18, bf16[192,1152]{1,0:T(8,128)(2,1)} %get-tuple-element.17, bf16[192,1152]{1,0:T(8,128)(2,1)} %bitcast.21), kind=kOutput, calls=%fused_computation | convolution fusion | flops 1366917120 | bytes 4718592 | tf_op jit(solution)/shard_map/dot_general | solution.py:257
  85.1 0.1 fusion.10
  85.2 3.1 %collective-permute-start.7 = (bf16[192,1152]{1,0:T(8,128)(2,1)S(1)}, bf16[192,1152]{1,0:T(8,128)(2,1)S(1)}, u32[]{:S(2)}, u32[]{:S(2)}) collective-permute-start(bf16[192,1152]{1,0:T(8,128)(2,1)S(1)} %get-tuple-element.24), channel_id=1, source_target_pairs={{0,64},{8,72},{16,80},{24,88},{32,96},{40,104},{48,112},{56,120},{... | collective-permute-start | bytes 1327112 | tf_op jit(solution)/shard_map/ppermute | solution.py:39
  88.3 3.7 %collective-permute-start.9 = (bf16[192,1152]{1,0:T(8,128)(2,1)S(1)}, bf16[192,1152]{1,0:T(8,128)(2,1)S(1)}, u32[]{:S(2)}, u32[]{:S(2)}) collective-permute-start(bf16[192,1152]{1,0:T(8,128)(2,1)S(1)} %get-tuple-element.25), channel_id=1, source_target_pairs={{0,32},{8,40},{16,48},{24,56},{32,64},{40,72},{48,80},{56,88},{64,... | collective-permute-start | bytes 1327112 | tf_op jit(solution)/shard_map/ppermute | solution.py:39
  92.1 1.9 %collective-permute-start.8 = (bf16[192,1152]{1,0:T(8,128)(2,1)S(1)}, bf16[192,1152]{1,0:T(8,128)(2,1)S(1)}, u32[]{:S(2)}, u32[]{:S(2)}) collective-permute-start(bf16[192,1152]{1,0:T(8,128)(2,1)S(1)} %get-tuple-element.26), channel_id=1, source_target_pairs={{0,96},{8,104},{16,112},{24,120},{32,0},{40,8},{48,16},{56,24},{64... | collective-permute-start | bytes 1327112 | tf_op jit(solution)/shard_map/ppermute | solution.py:39
  94.0 2.8 %collective-permute-done.7 = bf16[192,1152]{1,0:T(8,128)(2,1)S(1)} collective-permute-done((bf16[192,1152]{1,0:T(8,128)(2,1)S(1)}, bf16[192,1152]{1,0:T(8,128)(2,1)S(1)}, u32[]{:S(2)}, u32[]{:S(2)}) %collective-permute-start.7) | collective-permute-done | bytes 442400 | tf_op jit(solution)/shard_map/ppermute | solution.py:39
  96.8 8.8 %collective-permute-done.9 = bf16[192,1152]{1,0:T(8,128)(2,1)S(1)} collective-permute-done((bf16[192,1152]{1,0:T(8,128)(2,1)S(1)}, bf16[192,1152]{1,0:T(8,128)(2,1)S(1)}, u32[]{:S(2)}, u32[]{:S(2)}) %collective-permute-start.9) | collective-permute-done | bytes 442400 | tf_op jit(solution)/shard_map/ppermute | solution.py:39
  105.6 3.0 %collective-permute-done.8 = bf16[192,1152]{1,0:T(8,128)(2,1)S(1)} collective-permute-done((bf16[192,1152]{1,0:T(8,128)(2,1)S(1)}, bf16[192,1152]{1,0:T(8,128)(2,1)S(1)}, u32[]{:S(2)}, u32[]{:S(2)}) %collective-permute-start.8) | collective-permute-done | bytes 442400 | tf_op jit(solution)/shard_map/ppermute | solution.py:39
  108.5 0.2 add_convert_fusion.1.projected_ref
  108.7 1.8 %shard_map.115 = (bf16[96,3072]{1,0:T(8,128)(2,1)S(1)}, bf16[96,3072]{1,0:T(8,128)(2,1)S(1)}) custom-call(bf16[192,1152]{1,0:T(8,128)(2,1)S(1)} %add_convert_fusion.1.projected_ref, bf16[4,768,384]{2,1,0:T(8,128)(2,1)S(1)} %all-to-all-done.2.weights_ref), custom_call_target="tpu_custom_call" | custom-call | tf_op jit(solution)/shard_map/pallas_call | solution.py:186
  110.5 0.0 copy-start
  110.5 0.0 copy-start.1
  110.5 0.0 copy-start.2
  110.5 4.8 %collective-permute-start.10 = (bf16[96,3072]{1,0:T(8,128)(2,1)S(1)}, bf16[96,3072]{1,0:T(8,128)(2,1)S(1)}, u32[]{:S(2)}, u32[]{:S(2)}) collective-permute-start(bf16[96,3072]{1,0:T(8,128)(2,1)S(1)} %get-tuple-element.21), channel_id=1, source_target_pairs={{0,1},{1,0},{2,3},{3,2},{4,5},{5,4},{6,7},{7,6},{8,9},{9,8},{10,11... | collective-permute-start | bytes 1769480 | tf_op jit(solution)/shard_map/ppermute | solution.py:50
  115.3 1.6 %collective-permute-done.10 = bf16[96,3072]{1,0:T(8,128)(2,1)S(1)} collective-permute-done((bf16[96,3072]{1,0:T(8,128)(2,1)S(1)}, bf16[96,3072]{1,0:T(8,128)(2,1)S(1)}, u32[]{:S(2)}, u32[]{:S(2)}) %collective-permute-start.10) | collective-permute-done | bytes 589856 | tf_op jit(solution)/shard_map/ppermute | solution.py:50
  116.9 0.1 add_convert_fusion
  117.1 4.0 %collective-permute-start.13 = (bf16[24,3072]{1,0:T(8,128)(2,1)S(1)}, bf16[24,3072]{1,0:T(8,128)(2,1)S(1)}, u32[]{:S(2)}, u32[]{:S(2)}) collective-permute-start(bf16[24,3072]{1,0:T(8,128)(2,1)S(1)} %get-tuple-element.27), channel_id=1, source_target_pairs={{0,2},{1,3},{2,4},{3,5},{4,6},{5,7},{6,0},{7,1},{8,10},{9,11},{10,... | collective-permute-start | bytes 442376 | tf_op jit(solution)/shard_map/ppermute | solution.py:46
  121.1 3.1 %collective-permute-start.12 = (bf16[24,3072]{1,0:T(8,128)(2,1)S(1)}, bf16[24,3072]{1,0:T(8,128)(2,1)S(1)}, u32[]{:S(2)}, u32[]{:S(2)}) collective-permute-start(bf16[24,3072]{1,0:T(8,128)(2,1)S(1)} %get-tuple-element.28), channel_id=1, source_target_pairs={{0,6},{1,7},{2,0},{3,1},{4,2},{5,3},{6,4},{7,5},{8,14},{9,15},{10,... | collective-permute-start | bytes 442376 | tf_op jit(solution)/shard_map/ppermute | solution.py:46
  124.2 2.2 %collective-permute-start.11 = (bf16[24,3072]{1,0:T(8,128)(2,1)S(1)}, bf16[24,3072]{1,0:T(8,128)(2,1)S(1)}, u32[]{:S(2)}, u32[]{:S(2)}) collective-permute-start(bf16[24,3072]{1,0:T(8,128)(2,1)S(1)} %get-tuple-element.29), channel_id=1, source_target_pairs={{0,4},{1,5},{2,6},{3,7},{4,0},{5,1},{6,2},{7,3},{8,12},{9,13},{10,... | collective-permute-start | bytes 442376 | tf_op jit(solution)/shard_map/ppermute | solution.py:46
  126.4 3.3 %collective-permute-done.12.second_ref = bf16[24,3072]{1,0:T(8,128)(2,1)S(1)} collective-permute-done((bf16[24,3072]{1,0:T(8,128)(2,1)S(1)}, bf16[24,3072]{1,0:T(8,128)(2,1)S(1)}, u32[]{:S(2)}, u32[]{:S(2)}) %collective-permute-start.12) | collective-permute-done | bytes 147488 | tf_op jit(solution)/shard_map/ppermute | solution.py:46
  129.7 6.4 %collective-permute-done.11.first_ref = bf16[24,3072]{1,0:T(8,128)(2,1)S(1)} collective-permute-done((bf16[24,3072]{1,0:T(8,128)(2,1)S(1)}, bf16[24,3072]{1,0:T(8,128)(2,1)S(1)}, u32[]{:S(2)}, u32[]{:S(2)}) %collective-permute-start.11) | collective-permute-done | bytes 147488 | tf_op jit(solution)/shard_map/ppermute | solution.py:46
  136.1 1.0 shard_map.116
  (15 shorter events, 0.1 us)
Async XLA Ops:
  3.7 36.6 %all-to-all-start = ((bf16[4,24,768]{2,1,0:T(8,128)(2,1)}), bf16[4,24,768]{2,1,0:T(8,128)(2,1)S(1)}, u32[]{:S(2)}, u32[]{:S(2)}) async-start(bf16[4,24,768]{2,1,0:T(8,128)(2,1)} %get-tuple-element.13), calls=%async_computation | async-start | bytes 294912 | tf_op jit(solution)/shard_map/all_to_all | solution.py:54
  40.4 20.6 %collective-permute-start.2 = (bf16[4,24,768]{2,1,0:T(8,128)(2,1)S(1)}, bf16[4,24,768]{2,1,0:T(8,128)(2,1)S(1)}, u32[]{:S(2)}, u32[]{:S(2)}) collective-permute-start(bf16[4,24,768]{2,1,0:T(8,128)(2,1)S(1)} %rev.3), channel_id=1, source_target_pairs={{0,6},{1,7},{2,0},{3,1},{4,2},{5,3},{6,4},{7,5},{8,14},{9,15},{10,... | collective-permute-start | bytes 442376 | tf_op jit(solution)/shard_map/ppermute | solution.py:46
  45.6 19.2 %collective-permute-start.1 = (bf16[4,24,768]{2,1,0:T(8,128)(2,1)S(1)}, bf16[4,24,768]{2,1,0:T(8,128)(2,1)S(1)}, u32[]{:S(2)}, u32[]{:S(2)}) collective-permute-start(bf16[4,24,768]{2,1,0:T(8,128)(2,1)S(1)} %rev.3), channel_id=1, source_target_pairs={{0,4},{1,5},{2,6},{3,7},{4,0},{5,1},{6,2},{7,3},{8,12},{9,13},{10,... | collective-permute-start | bytes 442376 | tf_op jit(solution)/shard_map/ppermute | solution.py:46
  47.5 17.3 %collective-permute-start = (bf16[4,24,768]{2,1,0:T(8,128)(2,1)S(1)}, bf16[4,24,768]{2,1,0:T(8,128)(2,1)S(1)}, u32[]{:S(2)}, u32[]{:S(2)}) collective-permute-start(bf16[4,24,768]{2,1,0:T(8,128)(2,1)S(1)} %rev.3), channel_id=1, source_target_pairs={{0,2},{1,3},{2,4},{3,5},{4,6},{5,7},{6,0},{7,1},{8,10},{9,11},{10,... | collective-permute-start | bytes 442376 | tf_op jit(solution)/shard_map/ppermute | solution.py:46
  50.6 23.8 %all-to-all-start.1 = ((bf16[4,192,384]{2,1,0:T(8,128)(2,1)}), bf16[4,192,384]{2,1,0:T(8,128)(2,1)S(1)}, u32[]{:S(2)}, u32[]{:S(2)}) async-start(bf16[4,192,384]{2,1,0:T(8,128)(2,1)} %broadcast_in_dim.19), calls=%async_computation.1 | async-start | bytes 1179648 | tf_op jit(solution)/shard_map/all_to_all | solution.py:54
  54.8 25.2 %collective-permute-start.6 = (bf16[192,1152]{1,0:T(8,128)(2,1)}, bf16[192,1152]{1,0:T(8,128)(2,1)}, u32[]{:S(2)}, u32[]{:S(2)}) collective-permute-start(bf16[192,1152]{1,0:T(8,128)(2,1)} %bitcast.21), channel_id=1, source_target_pairs={{0,8},{8,16},{16,24},{24,0},{32,40},{40,48},{48,56},{56,32},{64,72... | collective-permute-start | bytes 1327112 | tf_op jit(solution)/shard_map/ppermute | solution.py:39
  58.0 22.1 %collective-permute-start.5 = (bf16[192,1152]{1,0:T(8,128)(2,1)}, bf16[192,1152]{1,0:T(8,128)(2,1)}, u32[]{:S(2)}, u32[]{:S(2)}) collective-permute-start(bf16[192,1152]{1,0:T(8,128)(2,1)} %bitcast.21), channel_id=1, source_target_pairs={{0,16},{8,24},{16,0},{24,8},{32,48},{40,56},{48,32},{56,40},{64,80... | collective-permute-start | bytes 1327112 | tf_op jit(solution)/shard_map/ppermute | solution.py:39
  61.0 19.7 %collective-permute-start.4 = (bf16[192,1152]{1,0:T(8,128)(2,1)}, bf16[192,1152]{1,0:T(8,128)(2,1)}, u32[]{:S(2)}, u32[]{:S(2)}) collective-permute-start(bf16[192,1152]{1,0:T(8,128)(2,1)} %bitcast.21), channel_id=1, source_target_pairs={{0,24},{8,0},{16,8},{24,16},{32,56},{40,32},{48,40},{56,48},{64,88... | collective-permute-start | bytes 1327112 | tf_op jit(solution)/shard_map/ppermute | solution.py:39
  65.7 15.0 %collective-permute-start.3 = (bf16[4,4,24,768]{3,2,0,1:T(8,128)(2,1)}, bf16[4,4,24,768]{3,2,0,1:T(8,128)(2,1)}, u32[]{:S(2)}, u32[]{:S(2)}) collective-permute-start(bf16[4,4,24,768]{3,2,0,1:T(8,128)(2,1)} %get-tuple-element.32), channel_id=1, source_target_pairs={{0,1},{1,0},{2,3},{3,2},{4,5},{5,4},{6,7},{7,6},{8,9},{9,8},{10,11... | collective-permute-start | bytes 1769480 | tf_op jit(solution)/shard_map/ppermute | solution.py:50
  74.4 1.6 %copy-start.3 = (bf16[4,192,384]{2,1,0:T(8,128)(2,1)}, bf16[4,192,384]{2,1,0:T(8,128)(2,1)S(1)}, u32[]{:S(2)}) copy-start(bf16[4,192,384]{2,1,0:T(8,128)(2,1)S(1)} %all-to-all-done.1) | copy-start | bytes 1769476
  76.1 32.7 %all-to-all-start.2 = ((bf16[4,768,384]{2,1,0:T(8,128)(2,1)}), bf16[4,768,384]{2,1,0:T(8,128)(2,1)S(1)}, u32[]{:S(2)}, u32[]{:S(2)}) async-start(bf16[4,768,384]{2,1,0:T(8,128)(2,1)} %broadcast_in_dim.20), calls=%async_computation.2 | async-start | bytes 4718592 | tf_op jit(solution)/shard_map/all_to_all | solution.py:54
  85.2 11.5 %collective-permute-start.7 = (bf16[192,1152]{1,0:T(8,128)(2,1)S(1)}, bf16[192,1152]{1,0:T(8,128)(2,1)S(1)}, u32[]{:S(2)}, u32[]{:S(2)}) collective-permute-start(bf16[192,1152]{1,0:T(8,128)(2,1)S(1)} %get-tuple-element.24), channel_id=1, source_target_pairs={{0,64},{8,72},{16,80},{24,88},{32,96},{40,104},{48,112},{56,120},{... | collective-permute-start | bytes 1327112 | tf_op jit(solution)/shard_map/ppermute | solution.py:39
  88.3 17.2 %collective-permute-start.9 = (bf16[192,1152]{1,0:T(8,128)(2,1)S(1)}, bf16[192,1152]{1,0:T(8,128)(2,1)S(1)}, u32[]{:S(2)}, u32[]{:S(2)}) collective-permute-start(bf16[192,1152]{1,0:T(8,128)(2,1)S(1)} %get-tuple-element.25), channel_id=1, source_target_pairs={{0,32},{8,40},{16,48},{24,56},{32,64},{40,72},{48,80},{56,88},{64,... | collective-permute-start | bytes 1327112 | tf_op jit(solution)/shard_map/ppermute | solution.py:39
  92.1 16.5 %collective-permute-start.8 = (bf16[192,1152]{1,0:T(8,128)(2,1)S(1)}, bf16[192,1152]{1,0:T(8,128)(2,1)S(1)}, u32[]{:S(2)}, u32[]{:S(2)}) collective-permute-start(bf16[192,1152]{1,0:T(8,128)(2,1)S(1)} %get-tuple-element.26), channel_id=1, source_target_pairs={{0,96},{8,104},{16,112},{24,120},{32,0},{40,8},{48,16},{56,24},{64... | collective-permute-start | bytes 1327112 | tf_op jit(solution)/shard_map/ppermute | solution.py:39
  110.5 25.6 %copy-start = (f32[16,3,3072]{2,0,1:T(8,128)S(1)}, f32[16,3,3072]{2,0,1:T(8,128)}, u32[]{:S(2)}) copy-start(f32[16,3,3072]{2,0,1:T(8,128)} %param.18) | copy-start | bytes 1769476
  110.5 25.6 %copy-start.1 = (bf16[1,24,3072]{2,1,0:T(8,128)(2,1)S(1)}, bf16[1,24,3072]{2,1,0:T(8,128)(2,1)}, u32[]{:S(2)}) copy-start(bf16[1,24,3072]{2,1,0:T(8,128)(2,1)} %param.10) | copy-start | bytes 442372
  110.5 25.5 %copy-start.2 = (bf16[1,24,3072]{2,1,0:T(8,128)(2,1)S(1)}, bf16[1,24,3072]{2,1,0:T(8,128)(2,1)}, u32[]{:S(2)}) copy-start(bf16[1,24,3072]{2,1,0:T(8,128)(2,1)} %param.11) | copy-start | bytes 442372
  110.5 6.4 %collective-permute-start.10 = (bf16[96,3072]{1,0:T(8,128)(2,1)S(1)}, bf16[96,3072]{1,0:T(8,128)(2,1)S(1)}, u32[]{:S(2)}, u32[]{:S(2)}) collective-permute-start(bf16[96,3072]{1,0:T(8,128)(2,1)S(1)} %get-tuple-element.21), channel_id=1, source_target_pairs={{0,1},{1,0},{2,3},{3,2},{4,5},{5,4},{6,7},{7,6},{8,9},{9,8},{10,11... | collective-permute-start | bytes 1769480 | tf_op jit(solution)/shard_map/ppermute | solution.py:50
  117.1 9.3 %collective-permute-start.13 = (bf16[24,3072]{1,0:T(8,128)(2,1)S(1)}, bf16[24,3072]{1,0:T(8,128)(2,1)S(1)}, u32[]{:S(2)}, u32[]{:S(2)}) collective-permute-start(bf16[24,3072]{1,0:T(8,128)(2,1)S(1)} %get-tuple-element.27), channel_id=1, source_target_pairs={{0,2},{1,3},{2,4},{3,5},{4,6},{5,7},{6,0},{7,1},{8,10},{9,11},{10,... | collective-permute-start | bytes 442376 | tf_op jit(solution)/shard_map/ppermute | solution.py:46
  121.1 8.6 %collective-permute-start.12 = (bf16[24,3072]{1,0:T(8,128)(2,1)S(1)}, bf16[24,3072]{1,0:T(8,128)(2,1)S(1)}, u32[]{:S(2)}, u32[]{:S(2)}) collective-permute-start(bf16[24,3072]{1,0:T(8,128)(2,1)S(1)} %get-tuple-element.28), channel_id=1, source_target_pairs={{0,6},{1,7},{2,0},{3,1},{4,2},{5,3},{6,4},{7,5},{8,14},{9,15},{10,... | collective-permute-start | bytes 442376 | tf_op jit(solution)/shard_map/ppermute | solution.py:46
  124.2 11.8 %collective-permute-start.11 = (bf16[24,3072]{1,0:T(8,128)(2,1)S(1)}, bf16[24,3072]{1,0:T(8,128)(2,1)S(1)}, u32[]{:S(2)}, u32[]{:S(2)}) collective-permute-start(bf16[24,3072]{1,0:T(8,128)(2,1)S(1)} %get-tuple-element.29), channel_id=1, source_target_pairs={{0,4},{1,5},{2,6},{3,7},{4,0},{5,1},{6,2},{7,3},{8,12},{9,13},{10,... | collective-permute-start | bytes 442376 | tf_op jit(solution)/shard_map/ppermute | solution.py:46
